TPU v7x, 32 devices: a whole 2x2x4 slice. The times are simulated.
32 devices in a mesh: seq: 8 (over z, x), head: 4 (over y, core).
Axes of the slice: x: 2, y: 2, z: 4, core: 2. Of those that a mesh axis runs over, the one named last changes fastest.
Arguments:
- tokens: bfloat16 [2, 4096, 1536], P(None, 'seq'), may hold values from -6 to 6
- norm_gain: float32 [1536], replicated, may hold values from 0.5 to 1.5
- gate_input_weight: bfloat16 [1536, 2, 3072], P(None, None, 'head'), may hold values from -0.15625 to 0.15625
- coefficient_weight: bfloat16 [1536, 2, 128], P(None, None, 'head'), may hold values from -0.15625 to 0.15625
- step_weight: bfloat16 [1536, 48], P(None, 'head'), may hold values from -0.15625 to 0.15625
- conv_x: float32 [4, 3072], P(None, 'head'), may hold values from -0.6 to 0.6
- conv_bc: float32 [4, 2, 128], P(None, None, 'head'), may hold values from -0.6 to 0.6
- conv_bias_x: float32 [3072], P('head'), may hold values from -0.5 to 0.5
- conv_bias_bc: float32 [2, 128], P(None, 'head'), may hold values from -0.5 to 0.5
- dt_bias: float32 [48], P('head'), may hold values from -3 to -1
- a_log: float32 [48], P('head'), as said below
- d_skip: float32 [48], P('head'), may hold values from 0.5 to 1.5
- gate_gain: float32 [3072], P('head'), may hold values from 0.5 to 1.5
- output_weight: bfloat16 [3072, 1536], P('head'), may hold values from -0.109375 to 0.109375
- cotangent: bfloat16 [2, 4096, 1536], P(None, 'seq'), may hold values from -6 to 6
Outputs:
- block_out: bfloat16 [2, 4096, 1536], P(None, 'seq', 'head')
- grad_input: float32 [2, 4096, 1536], P(None, 'seq', 'head')
- grad_norm_gain: float32 [1536], P('head')
- grad_gate_input_weight: float32 [1536, 2, 3072], P(None, None, 'head')
- grad_coefficient_weight: float32 [1536, 2, 128], P(None, None, 'head')
- grad_step_weight: float32 [1536, 48], P(None, 'head')
- grad_conv_x: float32 [4, 3072], P(None, 'head')
- grad_conv_bc: float32 [4, 2, 128], P(None, None, 'head')
- grad_conv_bias_x: float32 [3072], P('head')
- grad_conv_bias_bc: float32 [2, 128], P(None, 'head')
- grad_dt_bias: float32 [48], P('head')
- grad_a_log: float32 [48], P('head')
- grad_d_skip: float32 [48], P('head')
- grad_gate_gain: float32 [3072], P('head')
- grad_w_out: float32 [3072, 1536], P('head')
Inputs may be any that keep to these rules, and one draw needn't show every extreme that they name: Each head's a_log lies between log(0.3 / 4096) and log(2).
All inputs are finite; a program needn't handle non-finite values.
Results may differ from a plain program's by a relative error of at most 0.0095.
The roundings to bfloat16 on the way count: a program that leaves them out, or rounds other values in their place, can miss the bound.
Values may be sent and summed in bfloat16 or wider, within the bound.
A program may use at most 192 MiB of HBM per device.

v0:
```python
import jax
import jax.numpy as jnp
from jax import lax
from jax.sharding import PartitionSpec as P

KER = 4
GROUP = 256


EPSILON = 1e-05
EXACT_PRECISION = lax.Precision.HIGHEST


def from_behind(x, axis, by):
    length = lax.axis_size(axis)
    pairs = [(i, i + by) for i in range(length) if 0 <= i + by < length]
    return lax.ppermute(x, axis, pairs)


def prefix(part, axis, combine, identity, reverse):
    count = lax.axis_size(axis)
    place = lax.axis_index(axis)
    ahead = count - 1 - place if reverse else place
    gathered = jax.tree.map(lambda a: lax.all_gather(a, axis), part)
    state = jax.tree.map(lambda a, e: jnp.zeros_like(a) + jnp.asarray(e, a.dtype), part, identity)

    def one(step, state):
        source = count - 1 - step if reverse else step
        return combine(
            state, jax.tree.map(lambda a: lax.dynamic_index_in_dim(a, source, 0, False), gathered)
        )

    return lax.fori_loop(0, ahead, one, state)


def silu_value(array_in):
    return array_in * jax.nn.sigmoid(array_in)


def silu_slope(array_in):
    sigma_value = jax.nn.sigmoid(array_in)
    return sigma_value * (1.0 + array_in * (1.0 - sigma_value))


def group_step(carry_state, pieces):
    x_heads, b_rows, c_rows, log_decay, step_size = pieces
    cum_decay = jnp.cumsum(log_decay, axis=1)
    position = jnp.arange(log_decay.shape[1])
    lower_mask = (position[:, None] >= position[None, :])[None, :, :, None]
    gap_decay = cum_decay[:, :, None, :] - cum_decay[:, None, :, :]
    decay_mask = jnp.where(lower_mask, jnp.exp(jnp.where(lower_mask, gap_decay, 0.0)), 0.0)
    scores = jnp.einsum("sqn,skn->sqk", c_rows, b_rows, precision=EXACT_PRECISION)
    mixing = scores[:, :, :, None] * decay_mask * step_size[:, None, :, :]
    within = jnp.einsum("sqkh,skhp->sqhp", mixing, x_heads, precision=EXACT_PRECISION)
    carried = (
        jnp.einsum("sqn,shpn->sqhp", c_rows, carry_state, precision=EXACT_PRECISION)
        * jnp.exp(cum_decay)[:, :, :, None]
    )
    tail_weight = jnp.exp(cum_decay[:, -1:, :] - cum_decay) * step_size
    weighted = x_heads * tail_weight[:, :, :, None]
    fresh_state = jnp.einsum("skhp,skn->shpn", weighted, b_rows, precision=EXACT_PRECISION)
    new_state = jnp.exp(cum_decay[:, -1, :])[:, :, None, None] * carry_state + fresh_state
    return (new_state, within + carried)


def ssd_scan(x_heads, b_rows, c_rows, log_decay, step_size, carry_state):
    seq_count, block_len = (log_decay.shape[0], log_decay.shape[1])
    group_count = block_len // GROUP

    def grouped(array_in):
        return jnp.moveaxis(
            array_in.reshape((seq_count, group_count, GROUP) + array_in.shape[2:]), 1, 0
        )

    final_state, outputs = lax.scan(
        jax.checkpoint(group_step),
        carry_state,
        (
            grouped(x_heads),
            grouped(b_rows),
            grouped(c_rows),
            grouped(log_decay),
            grouped(step_size),
        ),
    )
    return (jnp.moveaxis(outputs, 0, 1).reshape(x_heads.shape), final_state)


def linked(earlier, later):
    return (earlier[0] * later[0], later[1] + later[0][:, :, None, None] * earlier[1])


def body(
    tokens,
    norm_gain,
    gate_input_weight,
    coefficient_weight,
    step_weight,
    conv_x,
    conv_bc,
    conv_bias_x,
    conv_bias_bc,
    dt_bias,
    a_log,
    d_skip,
    gate_gain,
    output_weight,
    cotangent,
):
    seq_count, block_len, width = tokens.shape
    inner_len = gate_input_weight.shape[2]
    state_part = coefficient_weight.shape[2]
    head_count = step_weight.shape[1]
    head_dim = inner_len // head_count
    head_parts = lax.axis_size("head")
    my_head = lax.axis_index("head")
    col_count = width // head_parts
    state_full = state_part * head_parts
    edge_len = KER - 1
    input_batch = tokens.astype(jnp.float32)
    row_scale = lax.rsqrt(jnp.mean(input_batch * input_batch, axis=-1, keepdims=True) + EPSILON)
    unit_rows = input_batch * row_scale
    normalized_input = (unit_rows * norm_gain).astype(jnp.bfloat16)
    gate_input_projected = jnp.einsum(
        "rhp,pkw->rhkw", normalized_input, gate_input_weight, preferred_element_type=jnp.float32
    )
    coefficient_projected = jnp.einsum(
        "jxp,pyh->jxyh", normalized_input, coefficient_weight, preferred_element_type=jnp.float32
    )
    step_unactivated = jnp.einsum(
        "ajn,ng->ajg", normalized_input, step_weight, preferred_element_type=jnp.float32
    )
    gate_pre = gate_input_projected[:, :, 0]
    conv_input = jnp.concatenate(
        [
            gate_input_projected[:, :, 1],
            coefficient_projected.reshape(seq_count, block_len, 2 * state_part),
        ],
        axis=-1,
    )
    conv_taps = jnp.concatenate([conv_x, conv_bc.reshape(KER, 2 * state_part)], axis=-1)
    biases = jnp.concatenate([conv_bias_x, conv_bias_bc.reshape(2 * state_part)])
    edge_rows = from_behind(conv_input[:, block_len - edge_len :], "seq", 1)
    extended = jnp.concatenate([edge_rows, conv_input], axis=1)
    conv_out = biases
    for tap_index in range(KER):
        conv_out = conv_out + conv_taps[tap_index] * extended[:, tap_index : tap_index + block_len]
    activated = silu_value(conv_out).astype(jnp.bfloat16)
    bc_local = activated[:, :, inner_len:].reshape(seq_count, block_len, 2, state_part)
    bc_whole = lax.all_gather(bc_local, "head", axis=3, tiled=True).astype(jnp.float32)
    b_rows = bc_whole[:, :, 0]
    c_rows = bc_whole[:, :, 1]
    x_heads = (
        activated[:, :, :inner_len]
        .astype(jnp.float32)
        .reshape(seq_count, block_len, head_count, head_dim)
    )
    dt_input = step_unactivated + dt_bias
    step_size = jax.nn.softplus(dt_input)
    decay_speed = jnp.exp(a_log)
    log_decay = -decay_speed * step_size
    zero_state = jnp.zeros((seq_count, head_count, head_dim, state_full), jnp.float32)
    local_out, local_state = ssd_scan(x_heads, b_rows, c_rows, log_decay, step_size, zero_state)
    block_cum = jnp.cumsum(log_decay, axis=1)
    block_logs = block_cum[:, -1]
    block_decay = jnp.exp(block_logs)
    no_decay = jnp.ones_like(block_decay)
    incoming = prefix((block_decay, local_state), "seq", linked, (no_decay, zero_state), False)[1]
    decay_rows = jnp.exp(block_cum)[:, :, :, None]
    ssd_out = (
        local_out
        + jnp.einsum("sln,shpn->slhp", c_rows, incoming, precision=EXACT_PRECISION) * decay_rows
        + d_skip[:, None] * x_heads
    )
    ssd_flat = ssd_out.reshape(seq_count, block_len, inner_len)
    gate_act = silu_value(gate_pre)
    gated = ssd_flat * gate_act
    square_sum = lax.psum(jnp.sum(gated * gated, axis=-1), "head")
    gate_scale = lax.rsqrt(square_sum / (inner_len * head_parts) + EPSILON)[:, :, None]
    scaled_gate = gated * gate_scale
    normalized_gate_result = (scaled_gate * gate_gain).astype(jnp.bfloat16)
    mixer_result = jnp.einsum(
        "qwy,yk->qwk", normalized_gate_result, output_weight, preferred_element_type=jnp.float32
    )
    mixed = lax.psum_scatter(
        mixer_result.astype(jnp.bfloat16), "head", scatter_dimension=2, tiled=True
    ).astype(jnp.float32)
    own_inputs = lax.dynamic_slice_in_dim(input_batch, my_head * col_count, col_count, 2)
    block_out = (own_inputs + mixed).astype(jnp.bfloat16)
    grad_normalized_gate = jnp.einsum(
        "erz,qz->erq", cotangent, output_weight, preferred_element_type=jnp.float32
    )
    grad_w_out = jnp.einsum(
        "ejm,eja->ma", normalized_gate_result, cotangent, preferred_element_type=jnp.float32
    )
    grad_gate_gain = jnp.sum(grad_normalized_gate * scaled_gate, axis=(0, 1))
    d_scaled = grad_normalized_gate * gate_gain
    cross_sum = lax.psum(jnp.sum(d_scaled * gated, axis=-1), "head")
    d_gated = (
        gate_scale * d_scaled
        - gated * gate_scale**3 * (cross_sum / (inner_len * head_parts))[:, :, None]
    )
    d_flat = d_gated * gate_act
    d_gate = (d_gated * ssd_flat * silu_slope(gate_pre)).astype(jnp.bfloat16)
    d_ssd = d_flat.reshape(seq_count, block_len, head_count, head_dim)
    grad_d_skip = jnp.sum(d_ssd * x_heads, axis=(0, 1, 3))
    d_entering = jnp.einsum("slhp,sln->shpn", d_ssd * decay_rows, c_rows, precision=EXACT_PRECISION)
    leaving = prefix((block_decay, d_entering), "seq", linked, (no_decay, zero_state), True)[1]
    _, pull_back = jax.vjp(ssd_scan, x_heads, b_rows, c_rows, log_decay, step_size, incoming)
    d_x_heads, d_b_rows, d_c_rows, d_log_decay, d_step, _ = pull_back((d_ssd, leaving))
    grad_a_log = jnp.sum(d_log_decay * log_decay, axis=(0, 1))
    d_step_all = d_step - decay_speed * d_log_decay
    d_dt_input = d_step_all * jax.nn.sigmoid(dt_input)
    grad_dt_bias = jnp.sum(d_dt_input, axis=(0, 1))
    grad_step_unactivated = d_dt_input.astype(jnp.bfloat16)
    d_bc_whole = jnp.stack([d_b_rows, d_c_rows], axis=2)
    d_bc_local = lax.psum_scatter(d_bc_whole, "head", scatter_dimension=3, tiled=True)
    d_x_total = (d_x_heads + d_skip[:, None] * d_ssd).reshape(seq_count, block_len, inner_len)
    d_activated = jnp.concatenate(
        [d_x_total, d_bc_local.reshape(seq_count, block_len, 2 * state_part)], axis=-1
    )
    d_conv = d_activated * silu_slope(conv_out)
    grad_taps = jnp.stack(
        [
            jnp.sum(d_conv * extended[:, tap_index : tap_index + block_len], axis=(0, 1))
            for tap_index in range(KER)
        ]
    )
    grad_biases = jnp.sum(d_conv, axis=(0, 1))
    d_extended = jnp.pad(conv_taps[0] * d_conv, ((0, 0), (0, edge_len), (0, 0)))
    for tap_index in range(1, KER):
        d_extended = d_extended + jnp.pad(
            conv_taps[tap_index] * d_conv, ((0, 0), (tap_index, edge_len - tap_index), (0, 0))
        )
    spill_rows = from_behind(d_extended[:, :edge_len], "seq", -1)
    d_input = (
        d_extended[:, edge_len:] + jnp.pad(spill_rows, ((0, 0), (block_len - edge_len, 0), (0, 0)))
    ).astype(jnp.bfloat16)
    grad_gate_input_projected = jnp.stack([d_gate, d_input[:, :, :inner_len]], axis=2)
    grad_coefficient_projected = d_input[:, :, inner_len:].reshape(
        seq_count, block_len, 2, state_part
    )
    grad_gate_input_weight = jnp.einsum(
        "zgu,zgno->uno",
        normalized_input,
        grad_gate_input_projected,
        preferred_element_type=jnp.float32,
    )
    grad_coefficient_weight = jnp.einsum(
        "fju,fjgq->ugq",
        normalized_input,
        grad_coefficient_projected,
        preferred_element_type=jnp.float32,
    )
    grad_step_weight = jnp.einsum(
        "vwc,vwp->cp", normalized_input, grad_step_unactivated, preferred_element_type=jnp.float32
    )
    grad_normalized = jnp.einsum(
        "ygtz,jtz->ygj",
        grad_gate_input_projected,
        gate_input_weight,
        preferred_element_type=jnp.float32,
    )
    grad_normalized = grad_normalized + jnp.einsum(
        "yrze,tze->yrt",
        grad_coefficient_projected,
        coefficient_weight,
        preferred_element_type=jnp.float32,
    )
    grad_normalized = grad_normalized + jnp.einsum(
        "yjw,zw->yjz", grad_step_unactivated, step_weight, preferred_element_type=jnp.float32
    )
    own_cotangent = lax.dynamic_slice_in_dim(cotangent, my_head * col_count, col_count, 2).astype(
        jnp.float32
    )
    own_units = lax.dynamic_slice_in_dim(unit_rows, my_head * col_count, col_count, 2)
    d_own = lax.psum_scatter(
        grad_normalized.astype(jnp.bfloat16), "head", scatter_dimension=2, tiled=True
    ).astype(jnp.float32)
    own_gain = lax.dynamic_slice_in_dim(norm_gain, my_head * col_count, col_count, 0)
    grad_norm_gain = jnp.sum(d_own * own_units, axis=(0, 1))
    d_units = d_own * own_gain
    row_sum = lax.psum(jnp.sum(d_units * own_inputs, axis=-1), "head")
    grad_input = (
        row_scale * d_units
        - own_inputs * row_scale**3 * (row_sum / width)[:, :, None]
        + own_cotangent
    )
    totals = lax.psum(
        (
            grad_gate_input_weight,
            grad_coefficient_weight,
            grad_step_weight,
            grad_taps,
            grad_biases,
            grad_dt_bias,
            grad_a_log,
            grad_d_skip,
            grad_gate_gain,
            grad_w_out,
            grad_norm_gain,
        ),
        "seq",
    )
    return (
        block_out,
        grad_input,
        totals[10],
        totals[0],
        totals[1],
        totals[2],
        totals[3][:, :inner_len],
        totals[3][:, inner_len:].reshape(KER, 2, state_part),
        totals[4][:inner_len],
        totals[4][inner_len:].reshape(2, state_part),
        totals[5],
        totals[6],
        totals[7],
        totals[8],
        totals[9],
    )


def solution(mesh):
    placed = (
        P(None, "seq", None),
        P(),
        P(None, None, "head"),
        P(None, None, "head"),
        P(None, "head"),
        P(None, "head"),
        P(None, None, "head"),
        P("head"),
        P(None, "head"),
        P("head"),
        P("head"),
        P("head"),
        P("head"),
        P("head", None),
        P(None, "seq", None),
    )
    return jax.shard_map(
        body,
        mesh=mesh,
        in_specs=placed,
        out_specs=(
            P(None, "seq", "head"),
            P(None, "seq", "head"),
            P("head"),
            P(None, None, "head"),
            P(None, None, "head"),
            P(None, "head"),
            P(None, "head"),
            P(None, None, "head"),
            P("head"),
            P(None, "head"),
            P("head"),
            P("head"),
            P("head"),
            P("head"),
            P("head", None),
        ),
        check_vma=False,
    )
```

profile of v0, /device:TPU:0, one launch (start us, length us, event | category | flops | bytes accessed | tf_op | source)
XLA Modules:
  0.0 1189.2 jit_solution(7475870058990578946)
XLA Ops:
  10.6 7.4 fusion.98
  24.8 4.8 collective-permute-start
  46.5 7.4 all_gather.21
  67.2 5.2 reshape_reshape.7
  82.9 38.3 %while.79 = (s32[]{:T(128)}, f32[2,12,64,128]{3,2,1,0:T(8,128)S(1)}, f32[2,2,256,12,64]{2,4,3,1,0:T(8,128)}, f32[2,2,256,12]{2,1,3,0:T(2,128)S(1)}, f32[2,2,256,...) while((s32[]{:T(128)}, ...), condition=%wide.region_4.5_spmd.clone, body=%wide.region_1.4_spmd.clone.sunk | while | flops 2627940352 | bytes 27958208 | solution.py:75
  86.5 9.5 fusion.254
  96.0 4.3 bitcast_dynamic-update-slice_fusion.14
  105.7 9.5 fusion.254
  115.2 4.2 bitcast_dynamic-update-slice_fusion.14
  130.0 19.0 %all-gather.1 = f32[16,1,12]{2,1,0:T(1,128)S(1)} all-gather(f32[2,1,12]{2,1,0:T(1,128)S(1)} %bitcast.571), channel_id=3, replica_groups=mesh['seq'=8,'head'=4] {'seq'}, dimensions={0}, use_global_device_ids=true | all-gather | bytes 864 | tf_op jit(solution)/shard_map/all_gather | solution.py:24
  154.6 66.4 %all-gather.6.cloned.1.call-done = f32[16,12,64,128]{3,2,1,0:T(8,128)} async-done(((f32[2,12,64,128]{3,2,1,0:T(8,128)}), f32[16,12,64,128]{3,2,1,0:T(8,128)}) %all-gather.6.cloned.1.call-update) | async-done | bytes 6291472 | tf_op jit(solution)/shard_map/all_gather | solution.py:24
  222.0 7.8 multiply_reduce_fusion.12
  233.5 6.0 psum.98
  239.5 10.2 multiply_reduce_fusion.9
  249.7 6.2 psum.99
  255.9 8.2 multiply_reduce_fusion.10
  267.7 4.4 fusion.115
  272.1 5.2 reshape_reshape.8
  277.3 12.3 %while.77 = (s32[]{:T(128)}, f32[2,12,64,128]{3,2,1,0:T(8,128)S(1)}, f32[2,2,12,64,128]{4,3,2,1,0:T(8,128)}, f32[2,2,256,12]{2,1,3,0:T(2,128)S(1)}, f32[2,2,256,...) while((s32[]{:T(128)}, ...), condition=%wide.region_19.20_spmd, body=%wide.region_16.19_spmd.sunk | while | flops 605564992 | bytes 5476301 | solution.py:75
  289.6 88.4 %all-gather.8.cloned.1.call-done = f32[16,12,64,128]{3,2,1,0:T(8,128)} async-done(((f32[2,12,64,128]{3,2,1,0:T(8,128)}), f32[16,12,64,128]{3,2,1,0:T(8,128)}) %all-gather.8.cloned.1.call-update) | async-done | bytes 6291472 | tf_op jit(solution)/shard_map/all_gather | solution.py:24
  378.1 9.6 while.76
  393.0 173.1 %while.78 = (s32[]{:T(128)}, f32[2,12,64,128]{3,2,1,0:T(8,128)S(1)}, f32[2,2,256,12,64]{2,4,3,1,0:T(8,128)}, f32[2,2,256,128]{3,2,0,1:T(8,128)}, f32[2,2,256,128...) while((s32[]{:T(128)}, ...), condition=%wide.region_33.34_spmd, body=%wide.region_20.33_spmd.sunk | while | flops 6077286400 | bytes 95466648 | solution.py:75
  424.2 12.6 %fusion.237 = (f32[2,256,12]{1,2,0:T(8,128)S(1)}, f32[2,256,12]{1,2,0:T(8,128)}, f32[2,256,12]{1,2,0:T(8,128)}, f32[2,256,256]{2,1,0:T(8,128)}) fusion(f32[2,256,12]{1,2,0:T(8,128)S(1)} %copy.588, f32[2,256,12]{1,2,0:T(8,128)S(1)} %copy.591, f32[2,256,256]{2,1,0:T(8,128)} %fusion.236, pred[256,256]{1,0:T(8,128)(4,1)S(1)} %iota_compare_fusion.4, ...), kind=kOutput, calls=%fused_computation.28.clone.1 | convolution fusion | flops 1231403008 | bytes 4382720 | tf_op jit(solution)/shard_map/transpose(jvp())/while/body/eval_jaxpr/checkpoint/sqkh,skhp->sqhp/dot_general | solution.py:54
  457.4 5.0 reduce-window.90
  464.4 4.3 fusion.243
  479.3 6.7 bitcast_dynamic-update-slice_fusion.11
  502.2 12.6 %fusion.237 = (f32[2,256,12]{1,2,0:T(8,128)S(1)}, f32[2,256,12]{1,2,0:T(8,128)}, f32[2,256,12]{1,2,0:T(8,128)}, f32[2,256,256]{2,1,0:T(8,128)}) fusion(f32[2,256,12]{1,2,0:T(8,128)S(1)} %copy.588, f32[2,256,12]{1,2,0:T(8,128)S(1)} %copy.591, f32[2,256,256]{2,1,0:T(8,128)} %fusion.236, pred[256,256]{1,0:T(8,128)(4,1)S(1)} %iota_compare_fusion.4, ...), kind=kOutput, calls=%fused_computation.28.clone.1 | convolution fusion | flops 1231403008 | bytes 4382720 | tf_op jit(solution)/shard_map/transpose(jvp())/while/body/eval_jaxpr/checkpoint/sqkh,skhp->sqhp/dot_general | solution.py:54
  535.5 5.0 reduce-window.90
  542.4 4.3 fusion.243
  557.4 6.7 bitcast_dynamic-update-slice_fusion.11
  568.9 6.1 convolution_convert_fusion
  574.9 8.7 copy.503
  583.6 4.4 copy.541
  590.1 6.1 copy.449
  596.2 5.5 reshape.358
  605.9 5.0 multiply_add_fusion.1
  613.9 10.3 fusion.151
  640.3 7.0 fusion.96
  650.0 8.6 copy.505
  658.6 4.4 copy.542
  663.1 7.9 convolution_bitcast_fusion.1
  674.5 8.4 convolution_bitcast_fusion
  682.9 5.5 convert_element_type.55
  688.4 5.0 broadcast_multiply_fusion
  707.3 39.7 %all-reduce.8 = (f32[384]{0:T(512)}, f32[4,832]{1,0:T(4,128)S(1)}, f32[832]{0:T(1024)S(1)}, f32[12]{0:T(128)}, f32[12]{0:T(128)}, /*index=5*/f32[12]{0:T(128)}, f32[768]{0:T(1024)}) all-reduce(f32[384]{0:T(512)S(1)} %get-tuple-element.811, f32[4,832]{1,0:T(4,128)S(1)} %pad_maximum_fusion.5, ...), channel_id=1, replica_groups=mesh['seq'=8,'head'=4] {'seq'}, use_global_device_ids=true, to_apply=%region_39.40 | all-reduce | flops 5348 | bytes 42784 | tf_op jit(solution)/shard_map/psum | solution.py:289
  748.9 6.0 psum.100
  758.9 402.4 %all-reduce.15.cloned.1.call-done = (f32[1536,2,768]{2,0,1:T(8,128)}, f32[1536,2,32]{0,2,1:T(8,128)}, f32[1536,12]{0,1:T(8,128)}, f32[768,1536]{1,0:T(8,128)}) async-done(((f32[1536,2,768]{2,0,1:T(8,128)}, f32[1536,2,32]{0,2,1:T(8,128)}, f32[1536,12]{0,1:T(8,128)}, f32[768,1536]{1,0:T(8,128)}), (f32[1536,2,768]{2,0,1:T(8,128)}, f32[1536,2,32]{0,2,1:T(8,128)}, f32[1536,12]{0,1:T(8,128)}, ...) | async-done | bytes 14622736 | tf_op jit(solution)/shard_map/psum | solution.py:289
  1161.4 17.2 %copy.466 = f32[1536,2,768]{2,1,0:T(2,128)} copy(f32[1536,2,768]{2,0,1:T(8,128)} %get-tuple-element.902) | data formatting | bytes 18874368
  (536 shorter events, 265.5 us)
Async XLA Ops:
  7.2 232.3 %copy-start = (bf16[768,1536]{1,0:T(8,128)(2,1)S(1)}, bf16[768,1536]{1,0:T(8,128)(2,1)}, u32[]{:S(2)}) copy-start(bf16[768,1536]{1,0:T(8,128)(2,1)} %param.38) | copy-start | bytes 7077892
  7.2 213.8 %all-gather.6.cloned.1.call-start = ((), (), s32[]{:S(2)}) async-start(), calls=%async_computation.2 | async-start | bytes 7077888 | tf_op jit(solution)/shard_map/all_gather | solution.py:24
  10.6 20.0 %copy-start.58 = (f32[2,512]{1,0:T(2,128)}, f32[2,512]{1,0:T(2,128)S(1)}, u32[]{:S(2)}) copy-start(f32[2,512]{1,0:T(2,128)S(1)} %get-tuple-element.943) | copy-start | bytes 12292
  24.0 9.5 copy-start.19
  24.8 9.3 copy-start.73
  24.8 10.0 collective-permute-start
  29.9 7.5 copy-start.60
  29.9 7.5 copy-start.62
  29.9 7.5 copy-start.64
  29.9 7.5 copy-start.66
  82.9 39.3 %copy-start.44 = (f32[2,512,12]{1,2,0:T(8,128)S(1)}, f32[2,512,12]{1,2,0:T(8,128)}, u32[]{:S(2)}) copy-start(f32[2,512,12]{1,2,0:T(8,128)} %copy-done.43) | copy-start | bytes 147460
  122.1 256.0 %all-gather.8.cloned.1.call-start = ((), (), s32[]{:S(2)}) async-start(), calls=%async_computation.3 | async-start | bytes 7077888 | tf_op jit(solution)/shard_map/all_gather | solution.py:24
  126.3 22.7 %copy-start.26 = (bf16[2,512,2,128]{1,2,0,3:T(2,128)(2,1)S(1)}, bf16[2,512,2,128]{1,2,0,3:T(2,128)(2,1)}, u32[]{:S(2)}) copy-start(bf16[2,512,2,128]{1,2,0,3:T(2,128)(2,1)} %copy-done.25) | copy-start | bytes 1572868
  229.9 9.7 copy-start.50
  239.5 16.4 %copy-start.47 = (f32[2,512]{1,0:T(2,128)}, f32[2,512]{1,0:T(2,128)S(1)}, u32[]{:S(2)}) copy-start(f32[2,512]{1,0:T(2,128)S(1)} %get-tuple-element.945) | copy-start | bytes 12292
  272.1 338.7 %all-reduce.13.cloned.1.call-start = ((), (), s32[]{:S(2)}) async-start(), calls=%async_computation.6 | async-start | bytes 2097152
  423.1 13.7 %copy-start.36 = (f32[2,256,12]{1,2,0:T(8,128)}, f32[2,256,12]{1,2,0:T(8,128)S(1)}, u32[]{:S(2)}) copy-start(f32[2,256,12]{1,2,0:T(8,128)S(1)} %copy.591) | copy-start | bytes 73732 | tf_op jit(solution)/shard_map/transpose(jvp())/while
  424.2 12.6 %copy-start.38 = (f32[2,256,12]{1,2,0:T(8,128)}, f32[2,256,12]{1,2,0:T(8,128)S(1)}, u32[]{:S(2)}) copy-start(f32[2,256,12]{1,2,0:T(8,128)S(1)} %copy.588) | copy-start | bytes 73732 | tf_op jit(solution)/shard_map/transpose(jvp())/while
  424.2 12.6 %copy-start.28 = (pred[256,256]{1,0:T(8,128)(4,1)}, pred[256,256]{1,0:T(8,128)(4,1)S(1)}, u32[]{:S(2)}) copy-start(pred[256,256]{1,0:T(8,128)(4,1)S(1)} %iota_compare_fusion.4) | copy-start | bytes 196612 | tf_op jit(solution)/shard_map/transpose(jvp())/while
  442.5 8.7 copy-start.40
  468.7 10.6 copy-start.37
  472.2 7.1 copy-start.22
  472.2 7.1 copy-start.29
  472.2 7.1 copy-start.39
  501.1 13.7 %copy-start.36 = (f32[2,256,12]{1,2,0:T(8,128)}, f32[2,256,12]{1,2,0:T(8,128)S(1)}, u32[]{:S(2)}) copy-start(f32[2,256,12]{1,2,0:T(8,128)S(1)} %copy.591) | copy-start | bytes 73732 | tf_op jit(solution)/shard_map/transpose(jvp())/while
  502.2 12.6 %copy-start.38 = (f32[2,256,12]{1,2,0:T(8,128)}, f32[2,256,12]{1,2,0:T(8,128)S(1)}, u32[]{:S(2)}) copy-start(f32[2,256,12]{1,2,0:T(8,128)S(1)} %copy.588) | copy-start | bytes 73732 | tf_op jit(solution)/shard_map/transpose(jvp())/while
  502.2 12.6 %copy-start.28 = (pred[256,256]{1,0:T(8,128)(4,1)}, pred[256,256]{1,0:T(8,128)(4,1)S(1)}, u32[]{:S(2)}) copy-start(pred[256,256]{1,0:T(8,128)(4,1)S(1)} %iota_compare_fusion.4) | copy-start | bytes 196612 | tf_op jit(solution)/shard_map/transpose(jvp())/while
  520.5 8.7 copy-start.40
  546.7 10.6 copy-start.37
  550.2 7.1 copy-start.22
  568.8 124.8 %reduce-scatter.7.cloned.1.call-start = ((), (), s32[]{:S(2)}) async-start(), calls=%async_computation.4 | async-start | bytes 3932160
  588.1 111.2 %reduce-scatter.9.cloned.1.call-start = ((), (), s32[]{:S(2)}) async-start(), calls=%async_computation.5 | async-start | bytes 3932160
  605.8 8.0 copy-start.21
  613.8 10.3 copy-start.61
  613.8 10.3 copy-start.63
  613.9 10.3 copy-start.65
  613.9 10.3 copy-start.67
  627.2 5.8 collective-permute-start.1
  663.0 8.0 copy-start.59
  663.1 8.0 copy-start.78
  663.1 498.3 %all-reduce.15.cloned.1.call-start = ((), (), s32[]{:S(2)}) async-start(), calls=%async_computation.7 | async-start | bytes 29294592 | tf_op jit(solution)/shard_map/psum | solution.py:289
  663.1 7.9 copy-start.16
  702.6 52.4 %copy-start.69 = (f32[2,512]{1,0:T(2,128)S(1)}, f32[2,512]{1,0:T(2,128)}, u32[]{:S(2)}) copy-start(f32[2,512]{1,0:T(2,128)} %get-tuple-element.942) | copy-start | bytes 12292
  747.0 11.9 %copy-start.79 = (f32[832]{0:T(1024)}, f32[832]{0:T(1024)S(1)}, u32[]{:S(2)}) copy-start(f32[832]{0:T(1024)S(1)} %get-tuple-element.897) | copy-start | bytes 9988
  1161.4 18.6 %slice-start = ((s8[4718592]{0:T(1024)(128)(4,1)}), s8[4194304]{0:T(1024)(128)(4,1)S(1)}, s32[]{:S(2)}) async-start(s8[4718592]{0:T(1024)(128)(4,1)} %bitcast.542), calls=%async_computation.8 | async-start | bytes 8388608
  1161.4 17.2 %copy-start.46 = (f32[1536,2,32]{0,2,1:T(8,128)S(1)}, f32[1536,2,32]{0,2,1:T(8,128)}, u32[]{:S(2)}) copy-start(f32[1536,2,32]{0,2,1:T(8,128)} %get-tuple-element.1416) | copy-start | bytes 1179652
  1161.4 18.0 %copy-start.55 = (f32[1536,12]{0,1:T(8,128)S(1)}, f32[1536,12]{0,1:T(8,128)}, u32[]{:S(2)}) copy-start(f32[1536,12]{0,1:T(8,128)} %get-tuple-element.1417) | copy-start | bytes 221188
  1161.4 18.6 %slice-start.1 = ((s8[4718592]{0:T(1024)(128)(4,1)}), s8[524288]{0:T(1024)(128)(4,1)S(1)}, s32[]{:S(2)}) async-start(s8[4718592]{0:T(1024)(128)(4,1)} %bitcast.542), calls=%async_computation.9 | async-start | bytes 1048576
  (67 other events, 252.2 us)
Sparse Core Ops, SparseCore 0:
  122.2 98.7 all-gather.5
  272.2 105.7 all-gather.7
  568.9 33.3 all-reduce.12
  604.9 38.2 reduce-scatter.6
  663.2 36.1 reduce-scatter.8
  705.8 455.5 all-reduce.14
where the time goes:
time: 1200 us; the launch traced here: 1190 us
  waiting for transfers between devices  560 us (47%)
  matrix products  198 us (16%)
  local copies, waits for them, and re-layouts  196 us (16%)
  other arithmetic  110 us (9%)
  blocking collectives  84.4 us (7%)
  loops' own time  18.6 us (2%)
  between operations  15.9 us (1%)
    psum x1, waiting for transfers between devices, body(): lax.psum((grad_gate_input_weight, grad_coefficient_weight, grad_step_weig...  402 us
    all_gather x2, waiting for transfers between devices, prefix(): gathered = jax.tree.map(lambda a: lax.all_gather(a, axis), part)  155 us
    unnamed x149, local copies, waits for them, and re-layouts  73 us
    dot_general x6, matrix products, group_step(): jnp.einsum('sqkh,skhp->sqhp', mixing, x_heads, precision=EXACT_PRECISION)  57.6 us
    psum x1, blocking collectives, body(): lax.psum((grad_gate_input_weight, grad_coefficient_weight, grad_step_weig...  39.7 us
    dot_general x8, matrix products, group_step(): jnp.einsum('skhp,skn->shpn', weighted, b_rows, precision=EXACT_PRECISION)  26.3 us
    dot_general x8, matrix products, group_step(): jnp.einsum('sqn,shpn->sqhp', c_rows, carry_state, precision=EXACT_PRECISION)  25.2 us
  transfers between devices with their start and end apart: 8, of which 5 were waited for; matrix products, arithmetic and copies ran while one was open for 14% of the time, Pallas kernels for 0%

commit v1 on v0

--- a/solution.py
+++ b/solution.py
@@ -1,6 +1,10 @@
+import functools
+
 import jax
 import jax.numpy as jnp
 from jax import lax
+from jax.experimental import pallas as pl
+from jax.experimental.pallas import tpu as pltpu
 from jax.sharding import PartitionSpec as P
 
 KER = 4
@@ -88,6 +92,178 @@
 
 def linked(earlier, later):
     return (earlier[0] * later[0], later[1] + later[0][:, :, None, None] * earlier[1])
+
+MESH = pl.DeviceIdType.MESH
+
+
+def ring_place(count):
+    place = lax.axis_index("seq")
+    row, col = place // 2, place % 2
+    return jnp.where(col == 0, row, count - 1 - row)
+
+
+def ring_device(rank, count):
+    return jnp.where(rank < count // 2, 2 * rank, 2 * (count - 1 - rank) + 1)
+
+
+def ring_kernel(count, plan, *refs):
+    n_lhs = 1 + max(p[0] for p in plan)
+    n_rhs = 1 + max(p[1] for p in plan)
+    streams = len(plan)
+    lhs, refs = refs[:n_lhs], refs[n_lhs:]
+    rhs, refs = refs[:n_rhs], refs[n_rhs:]
+    small_ref, refs = refs[0], refs[1:]
+    outs, refs = refs[:streams], refs[streams:]
+    small_out, refs = refs[0], refs[1:]
+    bufs, refs = refs[:streams], refs[streams:]
+    small_buf, rs_send, rs_recv, ag_send, ag_recv, sm_send, sm_recv = refs
+    head = lax.axis_index("head")
+    place = lax.axis_index("seq")
+    rank = ring_place(count)
+    peers = {
+        1: (ring_device(lax.rem(rank + 1, count), count), head),
+        -1: (ring_device(lax.rem(rank + count - 1, count), count), head),
+    }
+    barrier = pltpu.get_barrier_semaphore()
+
+    def greet(i, _):
+        other = lax.rem(place + i, count)
+        pl.semaphore_signal(barrier, inc=1, device_id=(other, head), device_id_type=MESH)
+        return 0
+
+    lax.fori_loop(1, count, greet, 0)
+    pl.semaphore_wait(barrier, count - 1)
+
+    small_buf[place] = small_ref[...]
+
+    def small_copy(i):
+        other = lax.rem(place + i, count)
+        return pltpu.make_async_remote_copy(
+            src_ref=small_ref,
+            dst_ref=small_buf.at[place],
+            send_sem=sm_send.at[i],
+            recv_sem=sm_recv.at[i],
+            device_id=(other, head),
+            device_id_type=MESH,
+        )
+
+    def small_start(i, _):
+        small_copy(i).start()
+        return 0
+
+    lax.fori_loop(1, count, small_start, 0)
+
+    def chunk_of(direction, step):
+        return lax.rem(rank - direction * step + 2 * count, count)
+
+    def partial(i, chunk):
+        l, r, first, cols, _ = plan[i]
+        rows = lhs[l].shape[0] // count
+        left = lhs[l][pl.ds(pl.multiple_of(chunk * rows, rows), rows), :]
+        return jnp.dot(left, rhs[r][:, first : first + cols], preferred_element_type=jnp.float32)
+
+    def rs_copy(i, step):
+        return pltpu.make_async_remote_copy(
+            src_ref=bufs[i].at[step],
+            dst_ref=bufs[i].at[step + 1],
+            send_sem=rs_send.at[i, step],
+            recv_sem=rs_recv.at[i, step],
+            device_id=peers[plan[i][4]],
+            device_id_type=MESH,
+        )
+
+    def ag_copy(i, step):
+        rows = bufs[i].shape[1]
+        chunk = chunk_of(plan[i][4], step - 1)
+        block = outs[i].at[pl.ds(pl.multiple_of(chunk * rows, rows), rows)]
+        return pltpu.make_async_remote_copy(
+            src_ref=block,
+            dst_ref=block,
+            send_sem=ag_send.at[i, step],
+            recv_sem=ag_recv.at[i, step],
+            device_id=peers[plan[i][4]],
+            device_id_type=MESH,
+        )
+
+    for i in range(streams):
+        bufs[i][0] = partial(i, chunk_of(plan[i][4], 0)).astype(jnp.bfloat16)
+        rs_copy(i, 0).start()
+
+    def rs_step(step, _):
+        for i in range(streams):
+            own = partial(i, chunk_of(plan[i][4], step))
+            rs_copy(i, step - 1).wait_recv()
+            bufs[i][step] = (own + bufs[i][step].astype(jnp.float32)).astype(jnp.bfloat16)
+            rs_copy(i, step).start()
+        return 0
+
+    lax.fori_loop(1, count - 1, rs_step, 0)
+    for i in range(streams):
+        chunk = chunk_of(plan[i][4], count - 1)
+        rows = bufs[i].shape[1]
+        own = partial(i, chunk)
+        rs_copy(i, count - 2).wait_recv()
+        done = (own + bufs[i][count - 1].astype(jnp.float32)).astype(jnp.bfloat16)
+        outs[i][pl.ds(pl.multiple_of(chunk * rows, rows), rows), :] = done
+        ag_copy(i, 0).start()
+
+    def ag_step(step, _):
+        for i in range(streams):
+            ag_copy(i, step - 1).wait_recv()
+            ag_copy(i, step).start()
+        return 0
+
+    lax.fori_loop(1, count - 1, ag_step, 0)
+    for i in range(streams):
+        ag_copy(i, count - 2).wait_recv()
+
+    def small_wait(i, _):
+        small_copy(i).wait()
+        return 0
+
+    lax.fori_loop(1, count, small_wait, 0)
+    total = small_buf[0]
+    for i in range(1, count):
+        total = total + small_buf[i]
+    small_out[...] = total
+
+    def drain(step, _):
+        for i in range(streams):
+            rs_copy(i, step).wait_send()
+            ag_copy(i, step).wait_send()
+        return 0
+
+    lax.fori_loop(0, count - 1, drain, 0)
+
+
+def ring_sum(count, plan, lhs, rhs, small):
+    rows = [lhs[p[0]].shape[0] for p in plan]
+    vmem = pl.BlockSpec(memory_space=pltpu.VMEM)
+    streams = len(plan)
+    sems = pltpu.SemaphoreType.DMA((streams, count))
+    return pl.pallas_call(
+        functools.partial(ring_kernel, count, plan),
+        out_shape=[jax.ShapeDtypeStruct((r, p[3]), jnp.bfloat16) for r, p in zip(rows, plan)]
+        + [jax.ShapeDtypeStruct(small.shape, jnp.float32)],
+        in_specs=[vmem] * (len(lhs) + len(rhs) + 1),
+        out_specs=[vmem] * (streams + 1),
+        scratch_shapes=[
+            pltpu.VMEM((count, r // count, p[3]), jnp.bfloat16) for r, p in zip(rows, plan)
+        ]
+        + [
+            pltpu.VMEM((count,) + small.shape, jnp.float32),
+            sems,
+            sems,
+            sems,
+            sems,
+            pltpu.SemaphoreType.DMA((count,)),
+            pltpu.SemaphoreType.DMA((count,)),
+        ],
+        compiler_params=pltpu.CompilerParams(
+            collective_id=1, has_side_effects=True, vmem_limit_bytes=56 * 2**20
+        ),
+        name="weight_ring",
+    )(*lhs, *rhs, small)
 
 
 def body(
@@ -190,9 +366,6 @@
     grad_normalized_gate = jnp.einsum(
         "erz,qz->erq", cotangent, output_weight, preferred_element_type=jnp.float32
     )
-    grad_w_out = jnp.einsum(
-        "ejm,eja->ma", normalized_gate_result, cotangent, preferred_element_type=jnp.float32
-    )
     grad_gate_gain = jnp.sum(grad_normalized_gate * scaled_gate, axis=(0, 1))
     d_scaled = grad_normalized_gate * gate_gain
     cross_sum = lax.psum(jnp.sum(d_scaled * gated, axis=-1), "head")
@@ -240,21 +413,6 @@
     grad_coefficient_projected = d_input[:, :, inner_len:].reshape(
         seq_count, block_len, 2, state_part
     )
-    grad_gate_input_weight = jnp.einsum(
-        "zgu,zgno->uno",
-        normalized_input,
-        grad_gate_input_projected,
-        preferred_element_type=jnp.float32,
-    )
-    grad_coefficient_weight = jnp.einsum(
-        "fju,fjgq->ugq",
-        normalized_input,
-        grad_coefficient_projected,
-        preferred_element_type=jnp.float32,
-    )
-    grad_step_weight = jnp.einsum(
-        "vwc,vwp->cp", normalized_input, grad_step_unactivated, preferred_element_type=jnp.float32
-    )
     grad_normalized = jnp.einsum(
         "ygtz,jtz->ygj",
         grad_gate_input_projected,
@@ -286,38 +444,81 @@
         - own_inputs * row_scale**3 * (row_sum / width)[:, :, None]
         + own_cotangent
     )
-    totals = lax.psum(
-        (
-            grad_gate_input_weight,
-            grad_coefficient_weight,
-            grad_step_weight,
-            grad_taps,
-            grad_biases,
-            grad_dt_bias,
-            grad_a_log,
-            grad_d_skip,
-            grad_gate_gain,
-            grad_w_out,
-            grad_norm_gain,
-        ),
-        "seq",
-    )
+    count = lax.axis_size("seq")
+    rows = seq_count * block_len
+
+    def padded(array_in):
+        parts = count * 16
+        return jnp.pad(array_in, ((0, -array_in.shape[0] % parts), (0, 0)))
+
+    normed_t = padded(normalized_input.reshape(rows, width).T)
+    gate_t = padded(normalized_gate_result.reshape(rows, inner_len).T)
+    cot = cotangent.reshape(rows, width)
+    d_gate2 = d_gate.reshape(rows, inner_len)
+    narrow = jnp.concatenate(
+        [
+            d_input.reshape(rows, -1),
+            grad_step_unactivated.reshape(rows, head_count),
+        ],
+        axis=1,
+    )
+    wide = -(-narrow.shape[1] // 128) * 128
+    narrow = jnp.pad(narrow, ((0, 0), (0, wide - narrow.shape[1])))
+    half, ihalf = width // 2, inner_len // 2
+    plan = (
+        (0, 0, 0, half, 1),
+        (0, 0, half, half, -1),
+        (1, 1, 0, ihalf, 1),
+        (1, 1, ihalf, ihalf, -1),
+        (1, 2, 0, ihalf, 1),
+        (1, 2, ihalf, wide - ihalf, -1),
+    )
+    smalls = [
+        grad_taps.reshape(-1),
+        grad_biases,
+        grad_dt_bias,
+        grad_a_log,
+        grad_d_skip,
+        grad_gate_gain,
+        grad_norm_gain,
+    ]
+    sizes = [a.shape[0] for a in smalls]
+    flat = jnp.concatenate(smalls)
+    lanes = -(-flat.shape[0] // 1024) * 8
+    flat = jnp.pad(flat, (0, lanes * 128 - flat.shape[0])).reshape(lanes, 128)
+    *sums, flat = ring_sum(count, plan, (gate_t, normed_t), (cot, d_gate2, narrow), flat)
+    flat = flat.reshape(-1)
+    cuts = []
+    start = 0
+    for size in sizes:
+        cuts.append(flat[start : start + size])
+        start += size
+    taps, bias, g_dt, g_a, g_skip, g_gain, g_norm = cuts
+    taps = taps.reshape(KER, -1)
+    sums = [a.astype(jnp.float32) for a in sums]
+    g_w_out = jnp.concatenate(sums[:2], axis=1)[:inner_len]
+    g_gate = jnp.concatenate(sums[2:4], axis=1)[:width]
+    g_narrow = jnp.concatenate(sums[4:], axis=1)[:width]
+    g_in = jnp.stack([g_gate, g_narrow[:, :inner_len]], axis=1)
+    split = inner_len + 2 * state_part
+    g_coef = g_narrow[:, inner_len:split].reshape(width, 2, state_part)
+    g_step = g_narrow[:, split : split + head_count]
     return (
         block_out,
         grad_input,
-        totals[10],
-        totals[0],
-        totals[1],
-        totals[2],
-        totals[3][:, :inner_len],
-        totals[3][:, inner_len:].reshape(KER, 2, state_part),
-        totals[4][:inner_len],
-        totals[4][inner_len:].reshape(2, state_part),
-        totals[5],
-        totals[6],
-        totals[7],
-        totals[8],
-        totals[9],
+        g_norm,
+        g_in,
+        g_coef,
+        g_step,
+        taps[:, :inner_len],
+        taps[:, inner_len:].reshape(KER, 2, state_part),
+        bias[:inner_len],
+        bias[inner_len:].reshape(2, state_part),
+        g_dt,
+        g_a,
+        g_skip,
+        g_gain,
+        g_w_out,
     )
 
 

time: 1200 us -> 966 us (0.81)
  waiting for transfers between devices: 560 us -> 157 us
  Pallas kernels: 0 us -> 163 us
  blocking collectives: 84.4 us -> 45.7 us
  local copies, waits for them, and re-layouts: 196 us -> 233 us
  other arithmetic: 110 us -> 133 us
  matrix products: 198 us -> 176 us
    psum x1 -> x0, waiting for transfers between devices: 402 us -> none  [body(): lax.psum((grad_gate_input_weight, grad_coefficient_weight, grad_step_weig...]
    pallas_call x0 -> x1, Pallas kernels: none -> 163 us  [ring_sum(): pl.pallas_call(functools.partial(ring_kernel, count, plan), out_shape=[ja...]
    psum x1 -> x0, blocking collectives: 39.7 us -> none  [body(): lax.psum((grad_gate_input_weight, grad_coefficient_weight, grad_step_weig...]
    dot_general x4 -> x0, matrix products: 19.6 us -> none  [the longest x1 8.39 us: body(): jnp.einsum('zgu,zgno->uno', normalized_input, grad_gate_input_projected,...]
    unnamed x149, local copies, waits for them, and re-layouts: 73 us -> 85.9 us
    another operation x27 -> x30, other arithmetic: 20.2 us -> 26.2 us
  transfers between devices with their start and end apart: 8 -> 7, of which waited for: 5 -> 3; matrix products, arithmetic and copies ran while one was open for 14% -> 17% of each run, Pallas kernels for 0% -> 0%
where the time goes in v1:
time: 966 us; the launch traced here: 956 us
  local copies, waits for them, and re-layouts  233 us (24%)
  matrix products  176 us (18%)
  Pallas kernels  163 us (17%)
  waiting for transfers between devices  157 us (16%)
  other arithmetic  133 us (14%)
  blocking collectives  45.7 us (5%)
  loops' own time  27.2 us (3%)
  between operations  15.9 us (2%)
    pallas_call x1, Pallas kernels, ring_sum(): pl.pallas_call(functools.partial(ring_kernel, count, plan), out_shape=[ja...  163 us
    all_gather x2, waiting for transfers between devices, prefix(): gathered = jax.tree.map(lambda a: lax.all_gather(a, axis), part)  155 us
    unnamed x149, local copies, waits for them, and re-layouts  85.9 us
    dot_general x6, matrix products, group_step(): jnp.einsum('sqkh,skhp->sqhp', mixing, x_heads, precision=EXACT_PRECISION)  57.7 us
    dot_general x8, matrix products, group_step(): jnp.einsum('skhp,skn->shpn', weighted, b_rows, precision=EXACT_PRECISION)  26.3 us
    dot_general x8, matrix products, group_step(): jnp.einsum('sqn,shpn->sqhp', c_rows, carry_state, precision=EXACT_PRECISION)  25.1 us
    another operation x27, other arithmetic  20.2 us
    all_gather x1, blocking collectives, prefix(): gathered = jax.tree.map(lambda a: lax.all_gather(a, axis), part)  19.4 us
  transfers between devices with their start and end apart: 7, of which 3 were waited for; matrix products, arithmetic and copies ran while one was open for 17% of the time, Pallas kernels for 0%

profile of v1, /device:TPU:0, one launch (start us, length us, event | category | flops | bytes accessed | tf_op | source)
XLA Modules:
  0.0 955.9 jit_solution(1246853529392947097)
XLA Ops:
  14.1 5.0 fusion.99
  26.7 4.8 collective-permute-start
  46.6 7.5 all_gather.21
  67.3 5.3 reshape_reshape.7
  83.1 38.2 %while.79 = (s32[]{:T(128)}, f32[2,12,64,128]{3,2,1,0:T(8,128)S(1)}, f32[2,2,256,12,64]{2,4,3,1,0:T(8,128)}, f32[2,2,256,12]{2,1,3,0:T(2,128)S(1)}, f32[2,2,256,...) while((s32[]{:T(128)}, ...), condition=%wide.region_4.5_spmd.clone, body=%wide.region_1.4_spmd.clone.sunk | while | flops 2627940352 | bytes 27958208 | solution.py:79
  86.7 9.5 fusion.255
  105.8 9.5 fusion.255
  130.0 19.4 %all-gather.1 = f32[16,1,12]{2,1,0:T(1,128)S(1)} all-gather(f32[2,1,12]{2,1,0:T(1,128)S(1)} %bitcast.586), channel_id=3, replica_groups=mesh['seq'=8,'head'=4] {'seq'}, dimensions={0}, use_global_device_ids=true | all-gather | bytes 864 | tf_op jit(solution)/shard_map/all_gather | solution.py:28
  155.1 66.1 %all-gather.6.cloned.1.call-done = f32[16,12,64,128]{3,2,1,0:T(8,128)} async-done(((f32[2,12,64,128]{3,2,1,0:T(8,128)}), f32[16,12,64,128]{3,2,1,0:T(8,128)}) %all-gather.6.cloned.1.call-update) | async-done | bytes 6291472 | tf_op jit(solution)/shard_map/all_gather | solution.py:28
  221.2 8.9 while.75
  230.2 7.9 multiply_reduce_fusion.12
  241.6 6.0 psum.21
  248.3 10.2 %multiply_reduce_fusion.9 = (f32[768]{0:T(1024)}, f32[2,512]{1,0:T(2,128)S(1)}, f32[2,512,768]{2,1,0:T(8,128)}, f32[2,512,768]{2,1,0:T(8,128)}) fusion(f32[2,512]{1,0:T(2,128)S(1)} %get-tuple-element.952, f32[768]{0:T(1024)S(1)} %copy-done.65, f32[2,512,768]{2,1,0:T(8,128)} %copy.451, f32[2,512,2,768]{3,1,2,0:T(8,128)} %copy-done.19, ...), kind=kOutput, calls=%fused_computation.188 | convolution fusion | flops 2424568064 | bytes 18102272 | tf_op jit(solution)/shard_map/erz,qz->erq/dot_general | solution.py:366
  258.4 6.2 psum.22
  264.6 8.2 multiply_reduce_fusion.10
  276.4 4.4 fusion.118
  280.9 5.2 reshape_reshape.8
  286.0 12.2 %while.77 = (s32[]{:T(128)}, f32[2,12,64,128]{3,2,1,0:T(8,128)S(1)}, f32[2,2,12,64,128]{4,3,2,1,0:T(8,128)}, f32[2,2,256,12]{2,1,3,0:T(2,128)S(1)}, f32[2,2,256,...) while((s32[]{:T(128)}, ...), condition=%wide.region_19.20_spmd, body=%wide.region_16.19_spmd.sunk | while | flops 605564992 | bytes 5476301 | solution.py:79
  298.2 89.1 %all-gather.8.cloned.1.call-done = f32[16,12,64,128]{3,2,1,0:T(8,128)} async-done(((f32[2,12,64,128]{3,2,1,0:T(8,128)}), f32[16,12,64,128]{3,2,1,0:T(8,128)}) %all-gather.8.cloned.1.call-update) | async-done | bytes 6291472 | tf_op jit(solution)/shard_map/all_gather | solution.py:28
  387.4 9.6 %while.76 = (s32[]{:T(128)}, f32[2,12,64,128]{3,2,1,0:T(8,128)S(1)}, s32[]{:T(128)}, f32[8,2,12,64,128]{4,3,2,1,0:T(8,128)}, f32[8,2,12]{2,1,0:T(2,128)S(1)}, /*index=5*/s32[]{:T(128)}, s32[]{:T(128)}, s32[]{:T(128)}, s32[]{:T(128)}) while((s32[]{:T(128)}, f32[2,12,64,128]{3,2,1,0:T(8,128)S(1)}, s32[]{:T(128)}, ...), condition=%wide.region_15.16_spmd, body=%wide.region_14.15_spmd.sunk | while | flops 393222 | bytes 2359731 | solution.py:37
  402.3 173.1 %while.78 = (s32[]{:T(128)}, f32[2,12,64,128]{3,2,1,0:T(8,128)S(1)}, f32[2,2,256,12,64]{2,4,3,1,0:T(8,128)}, f32[2,2,256,128]{3,2,0,1:T(8,128)}, f32[2,2,256,128...) while((s32[]{:T(128)}, ...), condition=%wide.region_33.34_spmd, body=%wide.region_20.33_spmd.sunk | while | flops 6077286400 | bytes 95466648 | solution.py:79
  433.5 12.6 %fusion.238 = (f32[2,256,12]{1,2,0:T(8,128)S(1)}, f32[2,256,12]{1,2,0:T(8,128)}, f32[2,256,12]{1,2,0:T(8,128)}, f32[2,256,256]{2,1,0:T(8,128)}) fusion(f32[2,256,12]{1,2,0:T(8,128)S(1)} %copy.606, f32[2,256,12]{1,2,0:T(8,128)S(1)} %copy.609, f32[2,256,256]{2,1,0:T(8,128)} %fusion.237, pred[256,256]{1,0:T(8,128)(4,1)S(1)} %iota_compare_fusion.5, ...), kind=kOutput, calls=%fused_computation.28.clone.1 | convolution fusion | flops 1231403008 | bytes 4382720 | tf_op jit(solution)/shard_map/transpose(jvp())/while/body/eval_jaxpr/checkpoint/sqkh,skhp->sqhp/dot_general | solution.py:58
  466.7 5.0 reduce-window.90
  473.6 4.3 fusion.244
  488.6 6.7 bitcast_dynamic-update-slice_fusion.11
  511.5 12.6 %fusion.238 = (f32[2,256,12]{1,2,0:T(8,128)S(1)}, f32[2,256,12]{1,2,0:T(8,128)}, f32[2,256,12]{1,2,0:T(8,128)}, f32[2,256,256]{2,1,0:T(8,128)}) fusion(f32[2,256,12]{1,2,0:T(8,128)S(1)} %copy.606, f32[2,256,12]{1,2,0:T(8,128)S(1)} %copy.609, f32[2,256,256]{2,1,0:T(8,128)} %fusion.237, pred[256,256]{1,0:T(8,128)(4,1)S(1)} %iota_compare_fusion.5, ...), kind=kOutput, calls=%fused_computation.28.clone.1 | convolution fusion | flops 1231403008 | bytes 4382720 | tf_op jit(solution)/shard_map/transpose(jvp())/while/body/eval_jaxpr/checkpoint/sqkh,skhp->sqhp/dot_general | solution.py:58
  544.7 5.0 reduce-window.90
  551.6 4.3 fusion.244
  566.6 6.7 bitcast_dynamic-update-slice_fusion.11
  578.2 6.0 convolution_convert_fusion
  584.2 8.7 copy.518
  592.9 4.4 copy.557
  599.3 6.2 copy.464
  605.5 5.5 reshape.389
  615.1 5.0 multiply_add_fusion.1
  623.1 10.2 %fusion.153 = (f32[832]{0:T(1024)S(1)}, f32[832]{0:T(1024)S(1)}, f32[832]{0:T(1024)S(1)}, f32[832]{0:T(1024)S(1)}, f32[832]{0:T(1024)S(1)}, /*index=5*/f32[2,512,832]{2,1,0:T(8,128)}) fusion(f32[2,512,64]{2,1,0:T(8,128)S(1)} %copy-done.22, f32[2,512,768]{2,1,0:T(8,128)} %get-tuple-element.939, f32[2,515,832]{2,1,0:T(8,128)} %copy-done.6, ...), kind=kLoop, calls=%fused_computation.280 | loop fusion | flops 16183232 | bytes 23871744 | tf_op jit(solution)/shard_map/reduce_sum | solution.py:402
  649.0 7.0 fusion.97
  658.7 8.6 copy.520
  667.3 4.4 copy.558
  671.8 5.6 convert_element_type.72
  682.0 4.7 copy.517
  686.7 6.5 copy.477
  693.3 4.3 copy.559
  697.8 5.1 fusion.134.refs_0_
  719.5 162.7 %weight_ring.1 = (bf16[768,768]{1,0:T(8,128)(2,1)}, bf16[768,768]{1,0:T(8,128)(2,1)}, bf16[1536,384]{1,0:T(8,128)(2,1)}, bf16[1536,384]{1,0:T(8,128)(2,1)}, bf16...) custom-call(bf16[768,1024]{1,0:T(8,128)(2,1)} %fusion.134.refs_0_, ...), custom_call_target="tpu_custom_call" | custom-call | tf_op jit(solution)/shard_map/weight_ring/pallas_call | solution.py:244
  899.4 29.3 %copy.483 = f32[1536,2,768]{2,1,0:T(2,128)} copy(f32[1536,2,768]{2,0,1:T(8,128)S(1)} %pad_maximum_fusion) | data formatting | bytes 18874368
  934.1 6.7 psum.23
  940.8 4.5 maximum_convert_fusion
  (554 shorter events, 295.9 us)
Async XLA Ops:
  7.2 241.1 %copy-start = (bf16[768,1536]{1,0:T(8,128)(2,1)S(1)}, bf16[768,1536]{1,0:T(8,128)(2,1)}, u32[]{:S(2)}) copy-start(bf16[768,1536]{1,0:T(8,128)(2,1)} %param.38) | copy-start | bytes 7077892
  7.2 213.9 %all-gather.6.cloned.1.call-start = ((), (), s32[]{:S(2)}) async-start(), calls=%async_computation.2 | async-start | bytes 7077888 | tf_op jit(solution)/shard_map/all_gather | solution.py:28
  14.1 8.5 copy-start.15
  25.0 6.9 copy-start.82
  25.0 7.5 copy-start.50
  25.0 7.5 copy-start.77
  25.2 10.1 %copy-start.20 = (f32[2,512,64]{2,1,0:T(8,128)}, f32[2,512,64]{2,1,0:T(8,128)S(1)}, u32[]{:S(2)}) copy-start(f32[2,512,64]{2,1,0:T(8,128)S(1)} %copy.432) | copy-start | bytes 786436
  25.2 10.2 %copy-start.76 = (f32[768]{0:T(1024)S(1)}, f32[768]{0:T(1024)}, u32[]{:S(2)}) copy-start(f32[768]{0:T(1024)} %param.32) | copy-start | bytes 9220
  26.7 8.9 collective-permute-start
  35.3 87.0 %copy-start.37 = (f32[2,512,12]{1,2,0:T(8,128)}, f32[2,512,12]{1,2,0:T(8,128)S(1)}, u32[]{:S(2)}) copy-start(f32[2,512,12]{1,2,0:T(8,128)S(1)} %get-tuple-element.958) | copy-start | bytes 147460
  122.2 265.1 %all-gather.8.cloned.1.call-start = ((), (), s32[]{:S(2)}) async-start(), calls=%async_computation.3 | async-start | bytes 7077888 | tf_op jit(solution)/shard_map/all_gather | solution.py:28
  126.4 23.0 %copy-start.29 = (bf16[2,512,2,128]{1,2,0,3:T(2,128)(2,1)S(1)}, bf16[2,512,2,128]{1,2,0,3:T(2,128)(2,1)}, u32[]{:S(2)}) copy-start(bf16[2,512,2,128]{1,2,0,3:T(2,128)(2,1)} %copy-done.28) | copy-start | bytes 1572868
  221.2 9.0 copy-start.36
  221.2 9.0 copy-start.79
  238.1 10.2 %copy-start.65 = (f32[768]{0:T(1024)S(1)}, f32[768]{0:T(1024)}, u32[]{:S(2)}) copy-start(f32[768]{0:T(1024)} %param.37) | copy-start | bytes 9220
  248.2 16.4 %copy-start.68 = (f32[2,512]{1,0:T(2,128)}, f32[2,512]{1,0:T(2,128)S(1)}, u32[]{:S(2)}) copy-start(f32[2,512]{1,0:T(2,128)S(1)} %get-tuple-element.952) | copy-start | bytes 12292
  280.8 339.3 %all-reduce.12.cloned.1.call-start = ((), (), s32[]{:S(2)}) async-start(), calls=%async_computation.6 | async-start | bytes 2097152
  432.3 13.7 %copy-start.40 = (f32[2,256,12]{1,2,0:T(8,128)}, f32[2,256,12]{1,2,0:T(8,128)S(1)}, u32[]{:S(2)}) copy-start(f32[2,256,12]{1,2,0:T(8,128)S(1)} %copy.609) | copy-start | bytes 73732 | tf_op jit(solution)/shard_map/transpose(jvp())/while
  433.4 12.6 %copy-start.42 = (f32[2,256,12]{1,2,0:T(8,128)}, f32[2,256,12]{1,2,0:T(8,128)S(1)}, u32[]{:S(2)}) copy-start(f32[2,256,12]{1,2,0:T(8,128)S(1)} %copy.606) | copy-start | bytes 73732 | tf_op jit(solution)/shard_map/transpose(jvp())/while
  433.4 12.6 %copy-start.32 = (pred[256,256]{1,0:T(8,128)(4,1)}, pred[256,256]{1,0:T(8,128)(4,1)S(1)}, u32[]{:S(2)}) copy-start(pred[256,256]{1,0:T(8,128)(4,1)S(1)} %iota_compare_fusion.5) | copy-start | bytes 196612 | tf_op jit(solution)/shard_map/transpose(jvp())/while
  451.7 8.7 copy-start.44
  477.9 10.6 %copy-start.41 = (f32[2,256,12]{1,2,0:T(8,128)S(1)}, f32[2,256,12]{1,2,0:T(8,128)}, u32[]{:S(2)}) copy-start(f32[2,256,12]{1,2,0:T(8,128)} %copy-done.40) | copy-start | bytes 73732 | tf_op jit(solution)/shard_map/transpose(jvp())/while
  481.4 7.1 copy-start.2
  481.4 7.1 copy-start.13
  481.4 7.1 copy-start.23
  481.4 7.1 copy-start.33
  481.4 7.1 copy-start.43
  510.3 13.7 %copy-start.40 = (f32[2,256,12]{1,2,0:T(8,128)}, f32[2,256,12]{1,2,0:T(8,128)S(1)}, u32[]{:S(2)}) copy-start(f32[2,256,12]{1,2,0:T(8,128)S(1)} %copy.609) | copy-start | bytes 73732 | tf_op jit(solution)/shard_map/transpose(jvp())/while
  511.4 12.6 %copy-start.42 = (f32[2,256,12]{1,2,0:T(8,128)}, f32[2,256,12]{1,2,0:T(8,128)S(1)}, u32[]{:S(2)}) copy-start(f32[2,256,12]{1,2,0:T(8,128)S(1)} %copy.606) | copy-start | bytes 73732 | tf_op jit(solution)/shard_map/transpose(jvp())/while
  511.5 12.6 %copy-start.32 = (pred[256,256]{1,0:T(8,128)(4,1)}, pred[256,256]{1,0:T(8,128)(4,1)S(1)}, u32[]{:S(2)}) copy-start(pred[256,256]{1,0:T(8,128)(4,1)S(1)} %iota_compare_fusion.5) | copy-start | bytes 196612 | tf_op jit(solution)/shard_map/transpose(jvp())/while
  529.7 8.7 copy-start.44
  555.9 10.6 %copy-start.41 = (f32[2,256,12]{1,2,0:T(8,128)S(1)}, f32[2,256,12]{1,2,0:T(8,128)}, u32[]{:S(2)}) copy-start(f32[2,256,12]{1,2,0:T(8,128)} %copy-done.40) | copy-start | bytes 73732 | tf_op jit(solution)/shard_map/transpose(jvp())/while
  559.4 7.1 copy-start.2
  559.4 7.1 copy-start.13
  559.4 7.1 copy-start.23
  559.4 7.1 copy-start.33
  559.4 7.1 copy-start.43
  578.1 124.8 %reduce-scatter.7.cloned.1.call-start = ((), (), s32[]{:S(2)}) async-start(), calls=%async_computation.4 | async-start | bytes 3932160
  597.3 113.4 %reduce-scatter.9.cloned.1.call-start = ((), (), s32[]{:S(2)}) async-start(), calls=%async_computation.5 | async-start | bytes 3932160
  615.1 8.0 copy-start.22
  623.1 10.3 %copy-start.58 = (f32[832]{0:T(1024)S(1)}, f32[832]{0:T(1024)}, u32[]{:S(2)}) copy-start(f32[832]{0:T(1024)} %copy-done.57) | copy-start | bytes 9988
  623.1 10.2 %copy-start.60 = (f32[832]{0:T(1024)S(1)}, f32[832]{0:T(1024)}, u32[]{:S(2)}) copy-start(f32[832]{0:T(1024)} %copy-done.59) | copy-start | bytes 9988
  623.1 10.2 %copy-start.62 = (f32[832]{0:T(1024)S(1)}, f32[832]{0:T(1024)}, u32[]{:S(2)}) copy-start(f32[832]{0:T(1024)} %copy-done.61) | copy-start | bytes 9988
  623.1 10.2 %copy-start.64 = (f32[832]{0:T(1024)S(1)}, f32[832]{0:T(1024)}, u32[]{:S(2)}) copy-start(f32[832]{0:T(1024)} %copy-done.63) | copy-start | bytes 9988
  636.4 5.8 collective-permute-start.1
  649.0 7.0 copy-start.51
  888.1 7.2 copy-start.54
  899.4 34.1 %slice-start = ((f32[4,832]{1,0:T(4,128)}), f32[4,64]{1,0:T(4,128)S(1)}, s32[]{:S(2)}) async-start(f32[4,832]{1,0:T(4,128)} %copy-done.54), calls=%async_computation.7 | async-start | bytes 4096 | tf_op jit(solution)/shard_map/slice | solution.py:514
  (67 other events, 259.5 us)
Sparse Core Ops, SparseCore 0:
  122.3 98.7 all-gather.5
  280.9 106.3 all-gather.7
  578.2 33.3 all-reduce.11
  614.1 38.2 reduce-scatter.6
  671.9 36.1 reduce-scatter.8

commit v2 on v1

v2 whole, which is shorter than its diff:
```python
import functools

import jax
import jax.numpy as jnp
from jax import lax
from jax.experimental import pallas as pl
from jax.experimental.pallas import tpu as pltpu
from jax.sharding import PartitionSpec as P

KER = 4
EPSILON = 1e-05
CHUNK = 128
LANES = 128
MESH = pl.DeviceIdType.MESH
F32 = jnp.float32
BF16 = jnp.bfloat16
EXACT = lax.Precision.HIGHEST
VMEM_LIMIT = 60 * 2**20
NN = ((1,), (0,))
NT = ((1,), (1,))
TN = ((0,), (0,))


def mul(left, right, how, precision=None):
    return lax.dot_general(
        left, right, (how, ((), ())), precision=precision, preferred_element_type=F32
    )


def sigmoid(v):
    return 0.5 * jnp.tanh(0.5 * v) + 0.5


def softplus(v):
    e = jnp.exp(-jnp.abs(v))
    u = 1.0 + e
    near = u - 1.0
    log1p = jnp.where(near == 0.0, e, jnp.log(u) * (e / jnp.where(near == 0.0, 1.0, near)))
    return jnp.maximum(v, 0.0) + log1p


def iota(shape, dim):
    return lax.broadcasted_iota(jnp.int32, shape, dim)


def ds(start, size):
    return pl.ds(pl.multiple_of(start, size), size)


def pair_of(values, pair):
    low = values[:, 2 * pair : 2 * pair + 1]
    high = values[:, 2 * pair + 1 : 2 * pair + 2]
    return jnp.where(iota((values.shape[0], LANES), 1) < LANES // 2, low, high)


def spread(values, pairs):
    return jnp.concatenate([pair_of(values, p) for p in range(pairs)], axis=1)


def eights(v):
    return jnp.sum(v.reshape(v.shape[0] // 8, 8, v.shape[1]), axis=0)


def halves_of(v):
    high = v.astype(BF16)
    return high, (v - high.astype(F32)).astype(BF16)


def head_sums(v, gather):
    high, low = halves_of(v)
    return mul(high, gather, NN) + mul(low, gather, NN)


def remote(src, dst, send, recv, place, head):
    return pltpu.make_async_remote_copy(
        src_ref=src,
        dst_ref=dst,
        send_sem=send,
        recv_sem=recv,
        device_id=(place, head),
        device_id_type=MESH,
    )


def meet(count, parts):
    place, head = lax.axis_index("seq"), lax.axis_index("head")
    barrier = pltpu.get_barrier_semaphore()

    def along_seq(i, _):
        other = lax.rem(place + i, count)
        pl.semaphore_signal(barrier, inc=1, device_id=(other, head), device_id_type=MESH)
        return 0

    def along_head(i, _):
        other = lax.rem(head + i, parts)
        pl.semaphore_signal(barrier, inc=1, device_id=(place, other), device_id_type=MESH)
        return 0

    lax.fori_loop(1, count, along_seq, 0)
    lax.fori_loop(1, parts, along_head, 0)
    pl.semaphore_wait(barrier, count - 1 + parts - 1)


def loop(low, high, step):
    def one(i, _):
        step(i)
        return 0

    lax.fori_loop(low, high, one, 0)


def line_copy(count, src, dst, send, recv):
    place, head = lax.axis_index("seq"), lax.axis_index("head")

    def copy(i):
        other = lax.rem(place + i, count)
        return remote(src(other), dst(place), send.at[i], recv.at[i], other, head)

    return copy


def head_copy(parts, src, dst, send, recv):
    place, head = lax.axis_index("seq"), lax.axis_index("head")

    def copy(i):
        other = lax.rem(head + i, parts)
        return remote(src(other), dst(head), send.at[i], recv.at[i], place, other)

    return copy


def cut_of(count, seqs, state, inner):
    rows = max(16, seqs * state // count)
    lane_cuts = count * rows // (seqs * state)
    return rows, lane_cuts, inner // lane_cuts


def piece_of(k, count, seqs, state, inner):
    rows, lane_cuts, lanes = cut_of(count, seqs, state, inner)
    each = count // seqs
    seq, rest = k // each, lax.rem(k, each)
    row = pl.multiple_of(rest // lane_cuts * rows, rows)
    if lane_cuts == 1:
        return seq, pl.ds(row, rows), slice(None)
    lane = pl.multiple_of(lax.rem(rest, lane_cuts) * lanes, lanes)
    return seq, pl.ds(row, rows), pl.ds(lane, lanes)


def carry_exchange(dims, local, arrived, passed, incoming, decay_ref, sems, reverse):
    count, _, seqs, _, inner, _, state = dims
    place, head = lax.axis_index("seq"), lax.axis_index("head")
    send, recv, back_send, back_recv = sems
    piece = functools.partial(piece_of, count=count, seqs=seqs, state=state, inner=inner)
    rows, _, lanes = cut_of(count, seqs, state, inner)

    def at(ref, k):
        seq, row, lane = piece(k)
        return ref.at[seq, row, lane]

    out = line_copy(count, lambda other: at(local, other), lambda k: arrived.at[k], send, recv)

    def back(j):
        i = lax.rem(j - place + count, count)
        return remote(
            passed.at[j], at(incoming, place), back_send.at[i], back_recv.at[i], j, head
        )

    def start():
        loop(1, count, lambda i: out(i).start())
        seq, row, lane = piece(place)
        arrived[place] = local[seq, row, lane]

    def carry():
        seq, row, lane = piece(place)
        held = jnp.zeros((rows, lanes), F32)
        for step in range(count):
            j = count - 1 - step if reverse else step
            i = lax.rem(place - j + count, count)

            @pl.when(j != place)
            def _():
                out(i).wait_recv()

            passed[j] = held.astype(passed.dtype)

            @pl.when(j != place)
            def _():
                back(j).start()

            @pl.when(j == place)
            def _():
                incoming[seq, row, lane] = passed[j]

            decay = decay_ref[seq, pl.ds(j, 1), lane]
            held = decay * held + arrived[j].astype(F32)

    def finish():
        def one(i):
            out(i).wait_send()
            back(lax.rem(place + i, count)).wait()

        loop(1, count, one)

    return start, carry, finish


def forward_kernel(
    dims,
    x_ref,
    gate_ref,
    small_ref,
    chan_ref,
    vec_ref,
    unpack_ref,
    expand_ref,
    gather_ref,
    cot_ref,
    wout_ref,
    xact_ref,
    bc_ref,
    conv_ref,
    convbc_ref,
    dt_ref,
    cum_ref,
    states_ref,
    ng_ref,
    dgate_ref,
    dy_ref,
    dyy_ref,
    decay_ref,
    sums_ref,
    edge_x,
    edge_s,
    ext,
    extbc,
    bc_all,
    fresh,
    y_ref,
    dng_ref,
    gated_ref,
    decays,
    local,
    arrived,
    passed,
    incoming,
    rowsum,
    edge_send,
    edge_recv,
    dec_send,
    dec_recv,
    bc_send,
    bc_recv,
    st_send,
    st_recv,
    back_send,
    back_recv,
    row_send,
    row_recv,
):
    count, parts, seqs, block, inner, heads, state = dims
    place, head = lax.axis_index("seq"), lax.axis_index("head")
    chunks = block // CHUNK
    pairs = heads // 2
    total = seqs * chunks
    meet(count, parts)

    def edge_copies(ahead):
        copies = []
        for s in range(seqs):
            rows = pl.ds(s * block + block - 8, 8)
            for k, (src, dst) in enumerate(((x_ref, edge_x), (small_ref, edge_s))):
                copies.append(
                    remote(
                        src.at[rows], dst.at[s], edge_send.at[k, s], edge_recv.at[k, s], ahead, head
                    )
                )
        return copies

    after = lax.rem(place + 1, count)

    @pl.when(place < count - 1)
    def _():
        for c in edge_copies(after):
            c.start()

    lower = (iota((CHUNK, CHUNK), 0) >= iota((CHUNK, CHUNK), 1)).astype(F32)
    for s in range(seqs):

        def steps(c, logs):
            rows = ds((s * chunks + c) * CHUNK, CHUNK)
            dt = softplus(small_ref[rows, :] + vec_ref[5:6, :])
            cum = mul(lower, dt * vec_ref[6:7, :], NN, EXACT)
            dt_ref[rows, :] = dt
            cum_ref[rows, :] = cum
            return logs + cum[CHUNK - 1 :, :]

        logs = lax.fori_loop(0, chunks, steps, jnp.zeros((1, LANES), F32))
        decays[place, s : s + 1, :] = jnp.exp(logs)

    dec = line_copy(count, lambda _: decays.at[place], lambda k: decays.at[k], dec_send, dec_recv)
    loop(1, count, lambda i: dec(i).start())

    @pl.when(place > 0)
    def _():
        for c in edge_copies(after):
            c.wait_recv()

    @pl.when(place == 0)
    def _():
        edge_x[...] = jnp.zeros_like(edge_x)
        edge_s[...] = jnp.zeros_like(edge_s)

    def packed(low, high):
        return jnp.where(
            iota(low.shape, 1) < LANES // 2, pltpu.roll(low, LANES // 2, 1), high
        )

    extbc[0:8, :] = packed(edge_s[0], edge_s[1])
    extbc[8:, :] = packed(small_ref[0:block, :], small_ref[block:, :])
    conv = vec_ref[4:5, :]
    for k in range(KER):
        conv = conv + vec_ref[k : k + 1, :] * extbc[pl.ds(8 - (KER - 1) + k, block), :]
    convbc_ref[...] = conv
    bc_all[head] = (conv * sigmoid(conv)).astype(BF16)
    share = head_copy(parts, lambda _: bc_all.at[head], lambda k: bc_all.at[k], bc_send, bc_recv)
    loop(1, parts, lambda i: share(i).start())

    def x_chunk(t):
        rows = ds(t * CHUNK, CHUNK)
        s, c = t // chunks, lax.rem(t, chunks)
        before = pl.ds(pl.multiple_of(jnp.maximum(t * CHUNK - 8, 0), 8), 8)
        for b in range(inner // LANES):
            lane = slice(b * LANES, (b + 1) * LANES)
            ext[0:8, lane] = jnp.where(c == 0, edge_x[s, :, lane], x_ref[before, lane])
            ext[8:, lane] = x_ref[rows, lane]
            conv = chan_ref[4:5, lane]
            for k in range(KER):
                conv = conv + chan_ref[k : k + 1, lane] * ext[pl.ds(8 - (KER - 1) + k, CHUNK), lane]
            conv_ref[rows, lane] = conv
            xact_ref[rows, lane] = (conv * sigmoid(conv)).astype(BF16)

    loop(0, total, x_chunk)

    loop(1, parts, lambda i: share(i).wait())
    everything = jnp.concatenate([bc_all[k] for k in range(parts)], axis=1)
    for s in range(seqs):
        bc_ref[s * block : (s + 1) * block, :] = mul(everything, unpack_ref[s], NN).astype(BF16)

    for s in range(seqs):

        def add(c, held):
            t = s * chunks + c
            rows = ds(t * CHUNK, CHUNK)
            cum, dt = cum_ref[rows, :], dt_ref[rows, :]
            end = cum[CHUNK - 1 :, :]
            tail = jnp.exp(end - cum) * dt
            weighted = jnp.concatenate(
                [
                    (
                        xact_ref[rows, p * LANES : (p + 1) * LANES].astype(F32) * pair_of(tail, p)
                    ).astype(BF16)
                    for p in range(pairs)
                ],
                axis=1,
            )
            new = mul(bc_ref[rows, 0:state], weighted, TN)
            fresh[t] = new
            return spread(jnp.exp(end), pairs) * held + new

        held = lax.fori_loop(0, chunks, add, jnp.zeros((state, inner), F32))
        local[s] = held

    start, carry, finish = carry_exchange(
        dims,
        local,
        arrived,
        passed,
        incoming,
        decay_ref,
        (st_send, st_recv, back_send, back_recv),
        False,
    )
    start()

    def within(t):
        rows = ds(t * CHUNK, CHUNK)
        cum, dt = cum_ref[rows, :], dt_ref[rows, :]
        cum_t = cum.T
        scores = mul(bc_ref[rows, state:], bc_ref[rows, 0:state], NT)
        seen = iota((CHUNK, CHUNK), 0) >= iota((CHUNK, CHUNK), 1)
        side = iota((CHUNK, LANES), 1) < LANES // 2
        for p in range(pairs):
            lane = slice(p * LANES, (p + 1) * LANES)
            stepped = (xact_ref[rows, lane].astype(F32) * pair_of(dt, p)).astype(BF16)
            halves = []
            for h in (2 * p, 2 * p + 1):
                gap = cum[:, h : h + 1] - cum_t[h : h + 1, :]
                mixing = (scores * jnp.exp(jnp.where(seen, gap, -1e30))).astype(BF16)
                halves.append(mul(mixing, stepped, NN))
            y_ref[rows, lane] = jnp.where(side, halves[0], halves[1])

    loop(0, total, within)

    loop(1, count, lambda i: dec(i).wait())
    for s in range(seqs):
        decay_ref[s] = mul(decays[:, s, :], expand_ref[...], NN, EXACT)
    carry()

    wide = 2 * LANES

    def back_project(i):
        s, b = i // (inner // wide), lax.rem(i, inner // wide)
        rows, lane = ds(s * block, block), ds(b * wide, wide)
        dng_ref[rows, lane] = mul(cot_ref[rows, :], wout_ref[lane, :], NT)

    loop(0, seqs * (inner // wide), back_project)
    finish()

    for s in range(seqs):

        def gate(c, held):
            t = s * chunks + c
            rows = ds(t * CHUNK, CHUNK)
            cum = cum_ref[rows, :]
            grown = jnp.exp(cum)
            states_ref[t] = held
            high, low = halves_of(held)
            c_rows = bc_ref[rows, state:]
            carried = mul(c_rows, high, NN) + mul(c_rows, low, NN)
            square = jnp.zeros((CHUNK, LANES), F32)
            cross = jnp.zeros((CHUNK, LANES), F32)
            for p in range(pairs):
                lane = slice(p * LANES, (p + 1) * LANES)
                y = y_ref[rows, lane] + carried[:, lane] * pair_of(grown, p)
                y_ref[rows, lane] = y
                out = y + chan_ref[6:7, lane] * xact_ref[rows, lane].astype(F32)
                pre = gate_ref[rows, lane]
                gated = out * (pre * sigmoid(pre))
                gated_ref[rows, lane] = gated
                square = square + gated * gated
                cross = cross + dng_ref[rows, lane] * chan_ref[5:6, lane] * gated
            at = iota((CHUNK, LANES), 1)
            both = jnp.where(
                at == 0,
                jnp.sum(square, axis=1, keepdims=True),
                jnp.where(at == 1, jnp.sum(cross, axis=1, keepdims=True), 0.0),
            )
            rowsum[head, t] = both.T[0:8, :]
            return spread(grown[CHUNK - 1 :, :], pairs) * held + fresh[t]

        lax.fori_loop(0, chunks, gate, incoming[s].astype(F32))

    rows_copy = head_copy(
        parts, lambda _: rowsum.at[head], lambda k: rowsum.at[k], row_send, row_recv
    )
    loop(1, parts, lambda i: rows_copy(i).start())
    loop(1, parts, lambda i: rows_copy(i).wait())
    sums_ref[...] = jnp.zeros_like(sums_ref)
    channels = inner * parts

    def outputs(t):
        rows = ds(t * CHUNK, CHUNK)
        sums = rowsum[0, t]
        for k in range(1, parts):
            sums = sums + rowsum[k, t]
        turned = jnp.concatenate([sums, jnp.zeros((CHUNK - 8, LANES), F32)], axis=0).T
        scale = lax.rsqrt(turned[:, 0:1] / channels + EPSILON)
        pull = scale * scale * scale * (turned[:, 1:2] / channels)
        dyy = jnp.zeros((CHUNK, LANES), F32)
        for p in range(pairs):
            lane = slice(p * LANES, (p + 1) * LANES)
            pre = gate_ref[rows, lane]
            sg = sigmoid(pre)
            gated, y = gated_ref[rows, lane], y_ref[rows, lane]
            x = xact_ref[rows, lane].astype(F32)
            gain = chan_ref[5:6, lane]
            scaled = gated * scale
            ng_ref[rows, lane] = (scaled * gain).astype(BF16)
            dng = dng_ref[rows, lane]
            d_gated = scale * (dng * gain) - gated * pull
            d_ssd = d_gated * (pre * sg)
            out = y + chan_ref[6:7, lane] * x
            dgate_ref[rows, lane] = (d_gated * out * (sg * (1.0 + pre * (1.0 - sg)))).astype(BF16)
            dy = d_ssd.astype(BF16)
            dy_ref[rows, lane] = dy
            sums_ref[0:8, lane] += eights(dng * scaled)
            sums_ref[8:16, lane] += eights(d_ssd * x)
            dyy = dyy + head_sums(dy.astype(F32) * y, gather_ref[lane, :])
        dyy_ref[rows, :] = dyy

    loop(0, total, outputs)

    @pl.when(place < count - 1)
    def _():
        for c in edge_copies(after):
            c.wait_send()


def vmem(shape, kind):
    return pltpu.VMEM(shape, kind)


def forward(dims, *operands):
    count, parts, seqs, block, inner, heads, state = dims
    rows = seqs * block
    chunks = rows // CHUNK
    cut_rows, _, cut_lanes = cut_of(count, seqs, state, inner)
    spec = pl.BlockSpec(memory_space=pltpu.VMEM)
    line, ring = pltpu.SemaphoreType.DMA((count,)), pltpu.SemaphoreType.DMA((parts,))
    edge = pltpu.SemaphoreType.DMA((2, seqs))
    outs = [
        ((rows, inner), BF16),
        ((rows, 2 * state), BF16),
        ((rows, inner), F32),
        ((block, LANES), F32),
        ((rows, LANES), F32),
        ((rows, LANES), F32),
        ((chunks, state, inner), F32),
        ((rows, inner), BF16),
        ((rows, inner), BF16),
        ((rows, inner), BF16),
        ((rows, LANES), F32),
        ((seqs, count, inner), F32),
        ((16, inner), F32),
    ]
    return pl.pallas_call(
        functools.partial(forward_kernel, dims),
        out_shape=[jax.ShapeDtypeStruct(*o) for o in outs],
        in_specs=[spec] * len(operands),
        out_specs=[spec] * len(outs),
        scratch_shapes=[
            vmem((seqs, 8, inner), F32),
            vmem((seqs, 8, LANES), F32),
            vmem((CHUNK + 8, inner), F32),
            vmem((block + 8, LANES), F32),
            vmem((parts, block, LANES), BF16),
            vmem((chunks, state, inner), F32),
            vmem((rows, inner), F32),
            vmem((rows, inner), F32),
            vmem((rows, inner), F32),
            vmem((count, 8, LANES), F32),
            vmem((seqs, state, inner), F32),
            vmem((count, cut_rows, cut_lanes), F32),
            vmem((count, cut_rows, cut_lanes), F32),
            vmem((seqs, state, inner), F32),
            vmem((parts, chunks, 8, LANES), F32),
            edge,
            edge,
            line,
            line,
            ring,
            ring,
            line,
            line,
            line,
            line,
            ring,
            ring,
        ],
        compiler_params=pltpu.CompilerParams(
            collective_id=2, has_side_effects=True, vmem_limit_bytes=VMEM_LIMIT
        ),
        name="mixer_forward",
    )(*operands)


def backward_kernel(
    dims,
    dy_ref,
    xact_ref,
    bc_ref,
    conv_ref,
    convbc_ref,
    dt_ref,
    cum_ref,
    states_ref,
    dyy_ref,
    decay_ref,
    x_ref,
    small_ref,
    chan_ref,
    vec_ref,
    pack_ref,
    gather_ref,
    dx_ref,
    dsmall_ref,
    gx_ref,
    gbc_ref,
    gdt_ref,
    dconv,
    dconvbc,
    prebc,
    dbc,
    ddt,
    added,
    local,
    arrived,
    passed,
    incoming,
    bc_out,
    bc_in,
    edge_send,
    edge_recv,
    bc_send,
    bc_recv,
    st_send,
    st_recv,
    back_send,
    back_recv,
):
    count, parts, seqs, block, inner, heads, state = dims
    place, head = lax.axis_index("seq"), lax.axis_index("head")
    chunks = block // CHUNK
    pairs = heads // 2
    total = seqs * chunks
    meet(count, parts)
    gdt_ref[...] = jnp.zeros_like(gdt_ref)

    for s in range(seqs):

        def alone(i, held):
            t = s * chunks + chunks - 1 - i
            rows = ds(t * CHUNK, CHUNK)
            grown = jnp.exp(cum_ref[rows, :])
            weighted = jnp.concatenate(
                [
                    (
                        dy_ref[rows, p * LANES : (p + 1) * LANES].astype(F32) * pair_of(grown, p)
                    ).astype(BF16)
                    for p in range(pairs)
                ],
                axis=1,
            )
            new = mul(bc_ref[rows, state:], weighted, TN)
            added[t] = new
            return spread(grown[CHUNK - 1 :, :], pairs) * held + new

        held = lax.fori_loop(0, chunks, alone, jnp.zeros((state, inner), F32))
        local[s] = held.astype(BF16)

    start, carry, finish = carry_exchange(
        dims,
        local,
        arrived,
        passed,
        incoming,
        decay_ref,
        (st_send, st_recv, back_send, back_recv),
        True,
    )
    start()
    carry()
    finish()

    side = iota((CHUNK, LANES), 1) < LANES // 2
    seen = iota((CHUNK, CHUNK), 0) <= iota((CHUNK, CHUNK), 1)
    upper = seen.astype(F32)
    for s in range(seqs):

        def chunk(i, held):
            t = s * chunks + chunks - 1 - i
            rows = ds(t * CHUNK, CHUNK)
            out_rows = ds((s * chunks + chunks - 1 - i) * CHUNK, CHUNK)
            cum, dt = cum_ref[rows, :], dt_ref[rows, :]
            cum_t = cum.T
            grown = jnp.exp(cum)
            end = cum[CHUNK - 1 :, :]
            tail = jnp.exp(end - cum)
            b_rows, c_rows = bc_ref[rows, 0:state], bc_ref[rows, state:]
            scores = mul(b_rows, c_rows, NT)
            low = held.astype(BF16)
            begun = states_ref[t]
            begun_high, begun_low = halves_of(begun)
            pulled = mul(b_rows, low, NN)
            grad_scores = jnp.zeros((CHUNK, CHUNK), F32)
            d_x_sum = jnp.zeros((CHUNK, LANES), F32)
            d_fall = jnp.zeros((CHUNK, LANES), F32)
            into_x = []
            into_y = []
            last = []
            for p in range(pairs):
                lane = slice(p * LANES, (p + 1) * LANES)
                x, dy = xact_ref[rows, lane], dy_ref[rows, lane]
                xf, dyf = x.astype(F32), dy.astype(F32)
                dt_p, tail_p = pair_of(dt, p), pair_of(tail, p)
                stepped = xf * dt_p
                low_step = stepped.astype(BF16)
                halves = []
                for k, h in enumerate((2 * p, 2 * p + 1)):
                    gap = cum_t[h : h + 1, :] - cum[:, h : h + 1]
                    fade = jnp.exp(jnp.where(seen, gap, -1e30))
                    own = jnp.where(side if k == 0 else ~side, low_step, jnp.zeros_like(low_step))
                    grad_scores = grad_scores + mul(own, dy, NT) * fade
                    halves.append(mul((scores * fade).astype(BF16), dy, NN))
                from_state = pulled[:, lane] * tail_p
                d_step_x = jnp.where(side, halves[0], halves[1]) + from_state
                rounded = low_step.astype(F32)
                d_x_sum = d_x_sum + head_sums(xf * d_step_x, gather_ref[lane, :])
                d_fall = d_fall + head_sums(rounded * d_step_x, gather_ref[lane, :])
                into_x.append((stepped * tail_p).astype(BF16))
                into_y.append((dyf * pair_of(grown, p)).astype(BF16))
                last.append(jnp.sum(rounded * from_state, axis=0, keepdims=True))
                conv = conv_ref[rows, lane]
                sg = sigmoid(conv)
                d_act = dt_p * d_step_x + chan_ref[6:7, lane] * dyf
                dconv[s, ds((chunks - 1 - i) * CHUNK, CHUNK), lane] = d_act * (
                    sg * (1.0 + conv * (1.0 - sg))
                )
            low_scores = grad_scores.astype(BF16)
            d_b = mul(low_scores, c_rows, NN) + mul(jnp.concatenate(into_x, axis=1), low, NT)
            into_y = jnp.concatenate(into_y, axis=1)
            d_c = mul(low_scores, b_rows, TN) + mul(into_y, begun_high, NT)
            d_c = d_c + mul(into_y, begun_low, NT)
            dbc[out_rows, 0:state] = d_b.astype(BF16)
            dbc[out_rows, state:] = d_c.astype(BF16)
            fall = spread(grown[CHUNK - 1 :, :], pairs)
            ends = jnp.concatenate(last, axis=1) + fall * jnp.sum(
                held * begun, axis=0, keepdims=True
            )
            ends = head_sums(jnp.broadcast_to(ends, (8, inner)), gather_ref[...])[0:1, :]
            d_log = mul(upper, dyy_ref[rows, :] - d_fall, NN, EXACT) + ends
            d_step = d_x_sum + vec_ref[6:7, :] * d_log
            d_dt = d_step * sigmoid(small_ref[rows, :] + vec_ref[5:6, :])
            gdt_ref[0:8, :] += eights(d_dt)
            gdt_ref[8:16, :] += eights(d_log * (dt * vec_ref[6:7, :]))
            ddt[out_rows, :] = d_dt
            return fall * held + added[t]

        lax.fori_loop(0, chunks, chunk, incoming[s].astype(F32))

    def pack(k):
        piece = mul(dbc[0:block, :], pack_ref[k, 0], NN)
        return (piece + mul(dbc[block:, :], pack_ref[k, 1], NN)).astype(BF16)

    def pack_one(k):
        bc_out[k] = pack(k)

    loop(0, parts, pack_one)
    share = head_copy(parts, lambda k: bc_out.at[k], lambda k: bc_in.at[k], bc_send, bc_recv)
    loop(1, parts, lambda i: share(i).start())

    before = lax.rem(place + count - 1, count)

    def edge_copy(s):
        return remote(
            dconv.at[s, pl.ds(0, 8)],
            dconv.at[s, pl.ds(block, 8)],
            edge_send.at[s],
            edge_recv.at[s],
            before,
            head,
        )

    def edge_bc():
        return remote(
            dconvbc.at[pl.ds(0, 8)],
            dconvbc.at[pl.ds(block, 8)],
            edge_send.at[seqs],
            edge_recv.at[seqs],
            before,
            head,
        )

    @pl.when(place > 0)
    def _():
        for s in range(seqs):
            edge_copy(s).start()

    loop(1, parts, lambda i: share(i).wait())
    bc_in[head] = bc_out[head]
    d_act = bc_in[0].astype(F32)
    for k in range(1, parts):
        d_act = d_act + bc_in[k].astype(F32)
    conv = convbc_ref[...]
    sg = sigmoid(conv)
    dconvbc[0:block, :] = d_act * (sg * (1.0 + conv * (1.0 - sg)))

    @pl.when(place > 0)
    def _():
        edge_bc().start()

    @pl.when(place < count - 1)
    def _():
        for s in range(seqs):
            edge_copy(s).wait_recv()

    @pl.when(place == count - 1)
    def _():
        for s in range(seqs):
            dconv[s, block : block + 8, :] = jnp.zeros((8, inner), F32)

    gx_ref[...] = jnp.zeros_like(gx_ref)

    def x_chunk(t):
        rows = ds(t * CHUNK, CHUNK)
        s, c = t // chunks, lax.rem(t, chunks)
        for p in range(pairs):
            lane = slice(p * LANES, (p + 1) * LANES)
            x = x_ref[rows, lane]
            pre = jnp.zeros((CHUNK, LANES), F32)
            here = dconv[s, pl.ds(pl.multiple_of(c * CHUNK, CHUNK), CHUNK + 8), lane]
            for k in range(KER):
                off = KER - 1 - k
                d = pltpu.roll(here, CHUNK + 8 - off, 0)[:CHUNK] if off else here[:CHUNK]
                pre = pre + chan_ref[k : k + 1, lane] * d
                gx_ref[8 * k : 8 * k + 8, lane] += eights(x * d)
                if k == KER - 1:
                    gx_ref[8 * KER : 8 * KER + 8, lane] += eights(d)
            dx_ref[rows, lane] = pre.astype(BF16)

    loop(0, total, x_chunk)

    @pl.when(place < count - 1)
    def _():
        edge_bc().wait_recv()

    @pl.when(place == count - 1)
    def _():
        dconvbc[block : block + 8, :] = jnp.zeros((8, LANES), F32)

    low, high = small_ref[0:block, :], small_ref[block:, :]
    prebc[...] = jnp.where(
        iota(low.shape, 1) < LANES // 2, pltpu.roll(low, LANES // 2, 1), high
    )
    pre = jnp.zeros((block, LANES), F32)
    for k in range(KER):
        d = dconvbc[pl.ds(KER - 1 - k, block), :]
        pre = pre + vec_ref[k : k + 1, :] * d
        gbc_ref[8 * k : 8 * k + 8, :] = eights(prebc[...] * d)
    gbc_ref[8 * KER : 8 * KER + 8, :] = eights(dconvbc[0:block, :])
    at = iota((block, LANES), 1)
    for s in range(seqs):
        rows = slice(s * block, (s + 1) * block)
        mine = pre if s == seqs - 1 else pltpu.roll(pre, LANES // 2, 1)
        step = jnp.where(at < heads, ddt[rows, :], 0.0)
        dsmall_ref[rows, :] = jnp.where(at < LANES // 2, step, mine).astype(BF16)

    @pl.when(place > 0)
    def _():
        for s in range(seqs):
            edge_copy(s).wait_send()
        edge_bc().wait_send()


def backward(dims, *operands):
    count, parts, seqs, block, inner, heads, state = dims
    rows = seqs * block
    chunks = rows // CHUNK
    cut_rows, _, cut_lanes = cut_of(count, seqs, state, inner)
    spec = pl.BlockSpec(memory_space=pltpu.VMEM)
    line, ring = pltpu.SemaphoreType.DMA((count,)), pltpu.SemaphoreType.DMA((parts,))
    edge = pltpu.SemaphoreType.DMA((seqs + 1,))
    outs = [
        ((rows, inner), BF16),
        ((rows, LANES), BF16),
        ((8 * (KER + 1), inner), F32),
        ((8 * (KER + 1), LANES), F32),
        ((16, LANES), F32),
    ]
    return pl.pallas_call(
        functools.partial(backward_kernel, dims),
        out_shape=[jax.ShapeDtypeStruct(*o) for o in outs],
        in_specs=[spec] * len(operands),
        out_specs=[spec] * len(outs),
        scratch_shapes=[
            vmem((seqs, block + 8, inner), F32),
            vmem((block + 8, LANES), F32),
            vmem((block, LANES), F32),
            vmem((rows, 2 * state), BF16),
            vmem((rows, LANES), F32),
            vmem((chunks, state, inner), F32),
            vmem((seqs, state, inner), BF16),
            vmem((count, cut_rows, cut_lanes), BF16),
            vmem((count, cut_rows, cut_lanes), BF16),
            vmem((seqs, state, inner), BF16),
            vmem((parts, block, LANES), BF16),
            vmem((parts, block, LANES), BF16),
            edge,
            edge,
            ring,
            ring,
            line,
            line,
            line,
            line,
        ],
        compiler_params=pltpu.CompilerParams(
            collective_id=3, has_side_effects=True, vmem_limit_bytes=VMEM_LIMIT
        ),
        name="mixer_backward",
    )(*operands)


def ring_place(count):
    place = lax.axis_index("seq")
    row, col = place // 2, place % 2
    return jnp.where(col == 0, row, count - 1 - row)


def ring_device(rank, count):
    return jnp.where(rank < count // 2, 2 * rank, 2 * (count - 1 - rank) + 1)


def ring_kernel(count, plan, *refs):
    n_lhs = 1 + max(p[0] for p in plan)
    n_rhs = 1 + max(p[1] for p in plan)
    streams = len(plan)
    lhs, refs = refs[:n_lhs], refs[n_lhs:]
    rhs, refs = refs[:n_rhs], refs[n_rhs:]
    small_ref, refs = refs[0], refs[1:]
    outs, refs = refs[:streams], refs[streams:]
    small_out, refs = refs[0], refs[1:]
    bufs, refs = refs[:streams], refs[streams:]
    small_buf, rs_send, rs_recv, ag_send, ag_recv, sm_send, sm_recv = refs
    head = lax.axis_index("head")
    place = lax.axis_index("seq")
    rank = ring_place(count)
    peers = {
        1: (ring_device(lax.rem(rank + 1, count), count), head),
        -1: (ring_device(lax.rem(rank + count - 1, count), count), head),
    }
    barrier = pltpu.get_barrier_semaphore()

    def greet(i, _):
        other = lax.rem(place + i, count)
        pl.semaphore_signal(barrier, inc=1, device_id=(other, head), device_id_type=MESH)
        return 0

    lax.fori_loop(1, count, greet, 0)
    pl.semaphore_wait(barrier, count - 1)

    small_buf[place] = small_ref[...]

    def small_copy(i):
        other = lax.rem(place + i, count)
        return pltpu.make_async_remote_copy(
            src_ref=small_ref,
            dst_ref=small_buf.at[place],
            send_sem=sm_send.at[i],
            recv_sem=sm_recv.at[i],
            device_id=(other, head),
            device_id_type=MESH,
        )

    def small_start(i, _):
        small_copy(i).start()
        return 0

    lax.fori_loop(1, count, small_start, 0)

    def chunk_of(direction, step):
        return lax.rem(rank - direction * step + 2 * count, count)

    def partial(i, chunk):
        l, r, first, cols, _ = plan[i]
        rows = lhs[l].shape[0] // count
        left = lhs[l][pl.ds(pl.multiple_of(chunk * rows, rows), rows), :]
        return jnp.dot(left, rhs[r][:, first : first + cols], preferred_element_type=jnp.float32)

    def rs_copy(i, step):
        return pltpu.make_async_remote_copy(
            src_ref=bufs[i].at[step],
            dst_ref=bufs[i].at[step + 1],
            send_sem=rs_send.at[i, step],
            recv_sem=rs_recv.at[i, step],
            device_id=peers[plan[i][4]],
            device_id_type=MESH,
        )

    def ag_copy(i, step):
        rows = bufs[i].shape[1]
        chunk = chunk_of(plan[i][4], step - 1)
        block = outs[i].at[pl.ds(pl.multiple_of(chunk * rows, rows), rows)]
        return pltpu.make_async_remote_copy(
            src_ref=block,
            dst_ref=block,
            send_sem=ag_send.at[i, step],
            recv_sem=ag_recv.at[i, step],
            device_id=peers[plan[i][4]],
            device_id_type=MESH,
        )

    for i in range(streams):
        bufs[i][0] = partial(i, chunk_of(plan[i][4], 0)).astype(jnp.bfloat16)
        rs_copy(i, 0).start()

    def rs_step(step, _):
        for i in range(streams):
            own = partial(i, chunk_of(plan[i][4], step))
            rs_copy(i, step - 1).wait_recv()
            bufs[i][step] = (own + bufs[i][step].astype(jnp.float32)).astype(jnp.bfloat16)
            rs_copy(i, step).start()
        return 0

    lax.fori_loop(1, count - 1, rs_step, 0)
    for i in range(streams):
        chunk = chunk_of(plan[i][4], count - 1)
        rows = bufs[i].shape[1]
        own = partial(i, chunk)
        rs_copy(i, count - 2).wait_recv()
        done = (own + bufs[i][count - 1].astype(jnp.float32)).astype(jnp.bfloat16)
        outs[i][pl.ds(pl.multiple_of(chunk * rows, rows), rows), :] = done
        ag_copy(i, 0).start()

    def ag_step(step, _):
        for i in range(streams):
            ag_copy(i, step - 1).wait_recv()
            ag_copy(i, step).start()
        return 0

    lax.fori_loop(1, count - 1, ag_step, 0)
    for i in range(streams):
        ag_copy(i, count - 2).wait_recv()

    def small_wait(i, _):
        small_copy(i).wait()
        return 0

    lax.fori_loop(1, count, small_wait, 0)
    total = small_buf[0]
    for i in range(1, count):
        total = total + small_buf[i]
    small_out[...] = total

    def drain(step, _):
        for i in range(streams):
            rs_copy(i, step).wait_send()
            ag_copy(i, step).wait_send()
        return 0

    lax.fori_loop(0, count - 1, drain, 0)


def ring_sum(count, plan, lhs, rhs, small):
    rows = [lhs[p[0]].shape[0] for p in plan]
    vmem = pl.BlockSpec(memory_space=pltpu.VMEM)
    streams = len(plan)
    sems = pltpu.SemaphoreType.DMA((streams, count))
    return pl.pallas_call(
        functools.partial(ring_kernel, count, plan),
        out_shape=[jax.ShapeDtypeStruct((r, p[3]), jnp.bfloat16) for r, p in zip(rows, plan)]
        + [jax.ShapeDtypeStruct(small.shape, jnp.float32)],
        in_specs=[vmem] * (len(lhs) + len(rhs) + 1),
        out_specs=[vmem] * (streams + 1),
        scratch_shapes=[
            pltpu.VMEM((count, r // count, p[3]), jnp.bfloat16) for r, p in zip(rows, plan)
        ]
        + [
            pltpu.VMEM((count,) + small.shape, jnp.float32),
            sems,
            sems,
            sems,
            sems,
            pltpu.SemaphoreType.DMA((count,)),
            pltpu.SemaphoreType.DMA((count,)),
        ],
        compiler_params=pltpu.CompilerParams(
            collective_id=1, has_side_effects=True, vmem_limit_bytes=56 * 2**20
        ),
        name="weight_ring",
    )(*lhs, *rhs, small)


def body(
    tokens,
    norm_gain,
    gate_input_weight,
    coefficient_weight,
    step_weight,
    conv_x,
    conv_bc,
    conv_bias_x,
    conv_bias_bc,
    dt_bias,
    a_log,
    d_skip,
    gate_gain,
    output_weight,
    cotangent,
):
    seqs, block, width = tokens.shape
    inner = gate_input_weight.shape[2]
    state_part = coefficient_weight.shape[2]
    heads = step_weight.shape[1]
    count, parts = lax.axis_size("seq"), lax.axis_size("head")
    my_head = lax.axis_index("head")
    state = state_part * parts
    rows = seqs * block
    col_count = width // parts
    half = LANES // 2
    dims = (count, parts, seqs, block, inner, heads, state)

    input_batch = tokens.astype(F32).reshape(rows, width)
    row_scale = lax.rsqrt(jnp.mean(input_batch * input_batch, axis=-1, keepdims=True) + EPSILON)
    normed = (input_batch * row_scale * norm_gain).astype(BF16)
    projected = jnp.einsum(
        "rp,pkw->krw", normed, gate_input_weight, preferred_element_type=F32
    )
    gate_pre, x_pre = projected[0], projected[1]
    small_weight = jnp.concatenate(
        [
            step_weight,
            jnp.zeros((width, half - heads), BF16),
            coefficient_weight.reshape(width, 2 * state_part),
        ],
        axis=1,
    )
    small = jnp.dot(normed, small_weight, preferred_element_type=F32)

    chan = jnp.concatenate(
        [
            conv_x,
            conv_bias_x[None],
            gate_gain[None],
            jnp.repeat(d_skip, inner // heads)[None],
            jnp.zeros((1, inner), F32),
        ]
    )
    twice = jnp.concatenate(
        [conv_bc.reshape(KER, 2 * state_part), conv_bias_bc.reshape(1, 2 * state_part)]
    )
    per_head = jnp.stack([dt_bias, -jnp.exp(a_log), jnp.zeros_like(a_log)])
    vec = jnp.concatenate(
        [
            jnp.concatenate([twice, twice], axis=1),
            jnp.pad(per_head, ((0, 0), (0, LANES - heads))),
        ]
    )
    device, lane, channel = jnp.meshgrid(
        jnp.arange(parts), jnp.arange(LANES), jnp.arange(2 * state), indexing="ij"
    )
    is_c, at = channel // state, channel % state
    unpack = jnp.stack(
        [
            (lane == s * half + is_c * state_part + at - device * state_part)
            & (at // state_part == device)
            for s in range(seqs)
        ]
    ).astype(BF16)
    pack = unpack.transpose(1, 0, 3, 2)
    unpack = unpack.reshape(seqs, parts * LANES, 2 * state)
    expand = jnp.arange(LANES)[:, None] == jnp.arange(inner)[None, :] // (inner // heads)
    gather = expand.T.astype(BF16)
    expand = expand.astype(F32)
    cot = cotangent.reshape(rows, width)

    xact, bc, conv, convbc, dt, cum, states, ng, dgate, dy, dyy, decay, sums = forward(
        dims,
        x_pre,
        gate_pre,
        small,
        chan,
        vec,
        unpack,
        expand,
        gather,
        cot,
        output_weight,
    )
    dx, dsmall, gx, gbc, gdt = backward(
        dims,
        dy,
        xact,
        bc,
        conv,
        convbc,
        dt,
        cum,
        states,
        dyy,
        decay,
        x_pre,
        small,
        chan,
        vec,
        pack,
        gather,
    )

    mixer = jnp.dot(ng, output_weight, preferred_element_type=F32)
    mixed = lax.psum_scatter(
        mixer.astype(BF16), "head", scatter_dimension=1, tiled=True
    ).astype(F32)
    own_inputs = lax.dynamic_slice_in_dim(input_batch, my_head * col_count, col_count, 1)
    block_out = (own_inputs + mixed).astype(BF16)

    d_both = jnp.stack([dgate, dx], axis=1)
    grad_normed = jnp.einsum(
        "rkw,pkw->rp", d_both, gate_input_weight, preferred_element_type=F32
    ) + lax.dot_general(dsmall, small_weight, (((1,), (1,)), ((), ())), preferred_element_type=F32)
    d_own = lax.psum_scatter(
        grad_normed.astype(BF16), "head", scatter_dimension=1, tiled=True
    ).astype(F32)
    own_gain = lax.dynamic_slice_in_dim(norm_gain, my_head * col_count, col_count, 0)
    grad_norm_gain = jnp.sum(d_own * own_inputs * row_scale, axis=0)
    d_units = d_own * own_gain
    row_sum = lax.psum(jnp.sum(d_units * own_inputs, axis=-1, keepdims=True), "head")
    own_cot = lax.dynamic_slice_in_dim(cot, my_head * col_count, col_count, 1).astype(F32)
    grad_input = row_scale * d_units - own_inputs * row_scale**3 * (row_sum / width) + own_cot

    def padded(array_in):
        return jnp.pad(array_in, ((0, -array_in.shape[0] % (count * 16)), (0, 0)))

    normed_t, ng_t = padded(normed.T), padded(ng.T)
    narrow = jnp.concatenate([dx, dsmall], axis=1)
    hw, hi = width // 2, inner // 2
    plan = (
        (0, 0, 0, hw, 1),
        (0, 0, hw, hw, -1),
        (1, 1, 0, hi, 1),
        (1, 1, hi, hi, -1),
        (1, 2, 0, hi, 1),
        (1, 2, hi, hi + LANES, -1),
    )
    taps = gx.reshape(KER + 1, 8, inner).sum(1)
    taps_bc = gbc.reshape(KER + 1, 8, 2, half).sum((1, 2))
    gdt = gdt.reshape(2, 8, LANES).sum(1)[:, :heads]
    sums = sums.reshape(2, 8, inner).sum(1)
    skip = sums[1].reshape(heads, inner // heads).sum(1)
    smalls = [taps.reshape(-1), taps_bc.reshape(-1), gdt.reshape(-1), skip, sums[0], grad_norm_gain]
    sizes = [a.shape[0] for a in smalls]
    flat = jnp.concatenate(smalls)
    lines = -(-flat.shape[0] // 1024) * 8
    flat = jnp.pad(flat, (0, lines * LANES - flat.shape[0])).reshape(lines, LANES)
    *wide, flat = ring_sum(count, plan, (ng_t, normed_t), (cot, dgate, narrow), flat)
    flat = flat.reshape(-1)
    cuts = []
    begin = 0
    for size in sizes:
        cuts.append(flat[begin : begin + size])
        begin += size
    taps, taps_bc = cuts[0].reshape(KER + 1, inner), cuts[1].reshape(KER + 1, 2, state_part)
    g_dt, g_a = cuts[2].reshape(2, heads)
    wide = [a.astype(F32) for a in wide]
    g_w_out = jnp.concatenate(wide[:2], axis=1)[:inner]
    g_gate = jnp.concatenate(wide[2:4], axis=1)[:width]
    g_narrow = jnp.concatenate(wide[4:], axis=1)[:width]
    g_small = g_narrow[:, inner:]
    return (
        block_out.reshape(seqs, block, col_count),
        grad_input.reshape(seqs, block, col_count),
        cuts[5],
        jnp.stack([g_gate, g_narrow[:, :inner]], axis=1),
        g_small[:, half:].reshape(width, 2, state_part),
        g_small[:, :heads],
        taps[:KER],
        taps_bc[:KER],
        taps[KER],
        taps_bc[KER],
        g_dt,
        g_a,
        cuts[3],
        cuts[4],
        g_w_out,
    )


def solution(mesh):
    placed = (
        P(None, "seq", None),
        P(),
        P(None, None, "head"),
        P(None, None, "head"),
        P(None, "head"),
        P(None, "head"),
        P(None, None, "head"),
        P("head"),
        P(None, "head"),
        P("head"),
        P("head"),
        P("head"),
        P("head"),
        P("head", None),
        P(None, "seq", None),
    )
    return jax.shard_map(
        body,
        mesh=mesh,
        in_specs=placed,
        out_specs=(
            P(None, "seq", "head"),
            P(None, "seq", "head"),
            P("head"),
            P(None, None, "head"),
            P(None, None, "head"),
            P(None, "head"),
            P(None, "head"),
            P(None, None, "head"),
            P("head"),
            P(None, "head"),
            P("head"),
            P("head"),
            P("head"),
            P("head"),
            P("head", None),
        ),
        check_vma=False,
    )
```

time: 966 us -> 468 us (0.48)
  local copies, waits for them, and re-layouts: 233 us -> 59.9 us
  matrix products: 176 us -> 22.1 us
  Pallas kernels: 163 us -> 309 us
  waiting for transfers between devices: 157 us -> 16.6 us
  other arithmetic: 133 us -> 30.5 us
  blocking collectives: 45.7 us -> 6.14 us
  loops' own time: 27.2 us -> 0 us
    all_gather x2 -> x0, waiting for transfers between devices: 155 us -> none  [prefix(): gathered = jax.tree.map(lambda a: lax.all_gather(a, axis), part)]
    dot_general x40 -> x5, matrix products: 176 us -> 22.1 us  [the longest x1 7.5 us: body(): jnp.einsum('rkw,pkw->rp', d_both, gate_input_weight, preferred_element_ty...]
    pallas_call x0 -> x2, Pallas kernels: none -> 144 us  [the longest x1 74.2 us: forward(): pl.pallas_call(functools.partial(forward_kernel, dims), out_shape=[jax.Sh...]
    unnamed x149 -> x73, local copies, waits for them, and re-layouts: 85.9 us -> 40.8 us
    another operation x73 -> x3, local copies, waits for them, and re-layouts: 34.3 us -> 0.22 us  [the longest x1 0.08 us: body(): jnp.repeat(d_skip, inner // heads)[None]]
    another operation x5 -> x0, loops' own time: 27.2 us -> none  [the longest x3 18 us: ssd_scan(): lax.scan(jax.checkpoint(group_step), carry_state, (grouped(x_heads), grou...]
    all_gather x2 -> x0, blocking collectives: 26.8 us -> none  [the longest x1 19.4 us: prefix(): gathered = jax.tree.map(lambda a: lax.all_gather(a, axis), part)]
    another operation x32 -> x5, other arithmetic: 27.5 us -> 1.43 us  [the longest x3 1.36 us: body(): jnp.stack([g_gate, g_narrow[:, :inner]], axis=1)]
  transfers between devices with their start and end apart: 7 -> 2, of which waited for: 3 -> 1; matrix products, arithmetic and copies ran while one was open for 17% -> 6% of each run, Pallas kernels for 0% -> 36%
where the time goes in v2:
time: 468 us; the launch traced here: 460 us
  Pallas kernels  309 us (66%)
  local copies, waits for them, and re-layouts  59.9 us (13%)
  other arithmetic  30.5 us (7%)
  matrix products  22.1 us (5%)
  waiting for transfers between devices  16.6 us (4%)
  between operations  15 us (3%)
  blocking collectives  6.14 us (1%)
    pallas_call x1, Pallas kernels, ring_sum(): pl.pallas_call(functools.partial(ring_kernel, count, plan), out_shape=[ja...  165 us
    pallas_call x1, Pallas kernels, forward(): pl.pallas_call(functools.partial(forward_kernel, dims), out_shape=[jax.Sh...  74.2 us
    pallas_call x1, Pallas kernels, backward(): pl.pallas_call(functools.partial(backward_kernel, dims), out_shape=[jax.S...  69.9 us
    unnamed x73, local copies, waits for them, and re-layouts  40.8 us
    unnamed x4, waiting for transfers between devices  16.6 us
  transfers between devices with their start and end apart: 2, of which 1 were waited for; matrix products, arithmetic and copies ran while one was open for 6% of the time, Pallas kernels for 36%

profile of v2, /device:TPU:0, one launch (start us, length us, event | category | flops | bytes accessed | tf_op | source)
XLA Modules:
  0.0 459.8 jit_solution(14483480950831022409)
XLA Ops:
  7.3 0.8 fusion.48.expand_ref
  8.1 0.8 fusion.49.gather_ref
  8.9 2.7 multiply_reduce_fusion
  11.7 3.4 multiply_convert_fusion
  15.2 5.0 %fusion.10 = f32[2,1024,768]{2,1,0:T(8,128)S(1)} fusion(bf16[1536,2,768]{2,1,0:T(2,128)(2,1)S(1)} %bitcast.100, bf16[1024,1536]{1,0:T(8,128)(2,1)S(1)} %get-tuple-element.129), kind=kOutput, calls=%fused_computation.18 | convolution fusion | flops 4831838208 | bytes 14155776 | tf_op jit(solution)/shard_map/rp,pkw->krw/dot_general | solution.py:1096
  20.3 3.1 slice_bitcast_fusion
  24.8 0.9 add_convert_fusion.1.unpack_ref
  25.7 0.9 fusion.27.pack_ref
  26.6 3.7 fusion.50.small_ref
  30.4 0.7 select_maximum_fusion.vec_ref
  31.1 0.6 concatenate.36.chan_ref
  31.8 74.2 %mixer_forward.1 = (bf16[1024,768]{1,0:T(8,128)(2,1)}, bf16[1024,256]{1,0:T(8,128)(2,1)}, f32[1024,768]{1,0:T(8,128)}, f32[512,128]{1,0:T(8,128)}, f32[1024,128]...) custom-call(f32[1024,768]{1,0:T(8,128)} %get-tuple-element.134.x_ref, ...), custom_call_target="tpu_custom_call" | custom-call | tf_op jit(solution)/shard_map/mixer_forward/pallas_call | solution.py:526
  106.0 69.9 %mixer_backward.1 = (bf16[1024,768]{1,0:T(8,128)(2,1)}, bf16[1024,128]{1,0:T(8,128)(2,1)}, f32[40,768]{1,0:T(8,128)}, f32[40,128]{1,0:T(8,128)}, f32[16,128]{1,0:T(8,128)}) custom-call(bf16[1024,768]{1,0:T(8,128)(2,1)} %get-tuple-element.42.dy_ref, bf16[1024,768]{1,0:T(8,128)(2,1)} %get-tuple-element.43.xact_ref, ...), custom_call_target="tpu_custom_call" | custom-call | tf_op jit(solution)/shard_map/mixer_backward/pallas_call | solution.py:860
  176.0 7.5 %fusion.2 = f32[1024,1536,1]{1,0,2:T(8,128)S(1)} fusion(bf16[1536,2,768]{2,1,0:T(2,128)(2,1)} %param.17, bf16[1024,1,768]{2,0,1:T(8,128)(2,1)} %bitcast.80, bf16[1024,1,768]{2,0,1:T(8,128)(2,1)S(1)} %bitcast.79), kind=kOutput, calls=%fused_computation.7 | convolution fusion | flops 4833411072 | bytes 14155776 | tf_op jit(solution)/shard_map/rkw,pkw->rp/dot_general | solution.py:1188
  183.5 1.1 fusion
  184.6 2.9 copy.60
  187.7 4.7 %convolution_convert_fusion = bf16[1024,1536]{1,0:T(8,128)(2,1)S(1)} fusion(bf16[1024,768]{1,0:T(8,128)(2,1)} %get-tuple-element.40, bf16[768,1536]{1,0:T(8,128)(2,1)} %wout_ref.1), kind=kOutput, calls=%fused_computation.11 | convolution fusion | flops 2417491968 | bytes 7077888 | tf_op jit(solution)/shard_map/dot_general | solution.py:1180
  192.5 2.9 copy.58
  195.4 2.7 copy.53
  198.1 0.7 dynamic_slice.10
  198.8 3.0 copy.54.refs_1_
  202.0 0.7 bitcast_reduce_fusion.2
  202.8 0.8 bitcast_reduce_fusion.1
  203.9 2.8 pad_maximum_fusion.2.refs_4_
  206.7 16.5 %reduce-scatter.9.cloned.1.call-done = bf16[384,1024]{1,0:T(8,128)(2,1)} async-done(((bf16[1536,1024]{1,0:T(8,128)(2,1)}), bf16[384,1024]{1,0:T(8,128)(2,1)}) %reduce-scatter.9.cloned.1.call-update) | async-done | bytes 786448
  223.2 1.5 copy.61
  224.7 2.3 fusion.22
  227.1 0.6 pad_bitcast_fusion.refs_5_
  227.7 165.1 %weight_ring.1 = (bf16[768,768]{1,0:T(8,128)(2,1)}, bf16[768,768]{1,0:T(8,128)(2,1)}, bf16[1536,384]{1,0:T(8,128)(2,1)}, bf16[1536,384]{1,0:T(8,128)(2,1)}, bf16...) custom-call(bf16[768,1024]{1,0:T(8,128)(2,1)} %bitcast.78, bf16[1536,1024]{1,0:T(8,128)(2,1)} %copy.54.refs_1_, ...), custom_call_target="tpu_custom_call" | custom-call | tf_op jit(solution)/shard_map/weight_ring/pallas_call | solution.py:1039
  392.8 2.0 convert_element_type.62
  394.8 1.1 slice.98
  395.9 0.9 slice.99
  396.9 0.7 slice.97
  397.6 0.7 slice.102
  398.2 6.1 %psum.7 = f32[1024,1]{0,1:T(1,128)S(1)} all-reduce(f32[1024,1]{0,1:T(1,128)S(1)} %bitcast.95), channel_id=1, replica_groups=mesh['seq'=8,'head'=4] {'head'}, use_global_device_ids=true, to_apply=%region_4.5 | all-reduce | flops 1024 | bytes 8192 | tf_op jit(solution)/shard_map/psum | solution.py:1197
  404.4 0.6 fusion.61
  405.0 0.6 slice_bitcast_fusion.2
  405.6 2.3 copy.59
  407.9 1.4 convert_element_type.61
  409.7 0.8 copy-done.11
  411.2 0.6 pad_maximum_fusion
  411.9 29.1 %copy.56 = f32[1536,2,768]{2,1,0:T(2,128)} copy(f32[1536,2,768]{2,0,1:T(8,128)S(1)} %pad_maximum_fusion) | data formatting | bytes 18874368
  441.0 1.0 copy.55
  442.0 0.9 copy.57
  442.9 0.6 slice.85
  443.5 0.7 slice.87
  444.7 4.2 maximum_convert_fusion
  448.9 3.6 fusion.19
  (112 shorter events, 4.3 us)
Async XLA Ops:
  7.2 4.5 copy-start
  7.2 4.5 copy-start.22
  7.2 216.0 %reduce-scatter.9.cloned.1.call-start = ((), (), s32[]{:S(2)}) async-start(), calls=%async_computation.3 | async-start | bytes 3932160
  8.9 6.2 %slice-start = ((s8[4718592]{0:T(1024)(128)(4,1)}), s8[4194304]{0:T(1024)(128)(4,1)S(1)}, s32[]{:S(2)}) async-start(s8[4718592]{0:T(1024)(128)(4,1)} %bitcast.99), calls=%async_computation.4 | async-start | bytes 8388608
  11.7 3.5 slice-start.1
  15.2 5.0 %copy-start.1 = (bf16[1024,1536]{1,0:T(8,128)(2,1)}, bf16[1024,1536]{1,0:T(8,128)(2,1)S(1)}, u32[]{:S(2)}) copy-start(bf16[1024,1536]{1,0:T(8,128)(2,1)S(1)} %get-tuple-element.129) | copy-start | bytes 9437188
  20.2 3.2 copy-start.24
  20.2 3.2 copy-start.25
  20.2 3.2 copy-start.27
  20.3 3.4 copy-start.30
  20.3 3.4 copy-start.29
  20.3 3.4 copy-start.26
  20.3 6.3 %copy-start.14 = (bf16[1536,2,32]{0,2,1:T(8,128)(2,1)S(1)}, bf16[1536,2,32]{0,2,1:T(8,128)(2,1)}, u32[]{:S(2)}) copy-start(bf16[1536,2,32]{0,2,1:T(8,128)(2,1)} %param.18) | copy-start | bytes 589828
  20.3 6.3 %copy-start.18 = (bf16[1536,12]{0,1:T(8,128)(2,1)S(1)}, bf16[1536,12]{0,1:T(8,128)(2,1)}, u32[]{:S(2)}) copy-start(bf16[1536,12]{0,1:T(8,128)(2,1)} %param.19) | copy-start | bytes 110596
  25.7 4.7 %copy-start.28 = (f32[12]{0:T(128)S(1)}, f32[12]{0:T(128)}, u32[]{:S(2)}) copy-start(f32[12]{0:T(128)} %param.24) | copy-start | bytes 148
  25.7 5.4 %copy-start.23 = (f32[4,768]{1,0:T(4,128)S(1)}, f32[4,768]{1,0:T(4,128)}, u32[]{:S(2)}) copy-start(f32[4,768]{1,0:T(4,128)} %param.20) | copy-start | bytes 36868
  106.0 69.9 %copy-start.9 = (bf16[1024,768]{1,0:T(8,128)(2,1)S(1)}, bf16[1024,768]{1,0:T(8,128)(2,1)}, u32[]{:S(2)}) copy-start(bf16[1024,768]{1,0:T(8,128)(2,1)} %get-tuple-element.41.refs_3_) | copy-start | bytes 4718596
  176.0 7.5 %copy-start.13 = (bf16[1024,128]{1,0:T(8,128)(2,1)S(1)}, bf16[1024,128]{1,0:T(8,128)(2,1)}, u32[]{:S(2)}) copy-start(bf16[1024,128]{1,0:T(8,128)(2,1)} %get-tuple-element.53) | copy-start | bytes 786436
  176.0 7.5 %copy-start.15 = (bf16[1536,2,32]{0,2,1:T(8,128)(2,1)S(1)}, bf16[1536,2,32]{0,2,1:T(8,128)(2,1)}, u32[]{:S(2)}) copy-start(bf16[1536,2,32]{0,2,1:T(8,128)(2,1)} %param.18) | copy-start | bytes 589828
  187.5 218.1 %reduce-scatter.7.cloned.1.call-start = ((), (), s32[]{:S(2)}) async-start(), calls=%async_computation.2 | async-start | bytes 3932160
  195.3 3.4 copy-start.2
  198.8 3.0 copy-start.16
  198.8 3.0 copy-start.19
  201.7 23.0 %copy-start.20 = (f32[384]{0:T(512)S(1)}, f32[384]{0:T(512)}, u32[]{:S(2)}) copy-start(f32[384]{0:T(512)} %dynamic_slice.10) | copy-start | bytes 4612
  224.7 168.1 %copy-start.3 = (bf16[1024,384]{1,0:T(8,128)(2,1)}, bf16[1024,384]{1,0:T(8,128)(2,1)S(1)}, u32[]{:S(2)}) copy-start(bf16[1024,384]{1,0:T(8,128)(2,1)S(1)} %copy.61) | copy-start | bytes 2359300
  392.8 2.0 copy-start.5
  392.8 4.0 copy-start.17
  409.3 1.3 copy-start.11
  409.3 1.6 copy-start.12
  411.9 29.1 %copy-start.7 = (f32[1536,64]{1,0:T(8,128)S(1)}, f32[1536,64]{1,0:T(8,128)}, u32[]{:S(2)}) copy-start(f32[1536,64]{1,0:T(8,128)} %slice.98) | copy-start | bytes 1179652
  411.9 30.1 %copy-start.6 = (f32[1536,12]{1,0:T(8,128)S(1)}, f32[1536,12]{1,0:T(8,128)}, u32[]{:S(2)}) copy-start(f32[1536,12]{1,0:T(8,128)} %slice.99) | copy-start | bytes 221188
  411.9 32.8 %copy-start.10 = (bf16[768,768]{1,0:T(8,128)(2,1)S(1)}, bf16[768,768]{1,0:T(8,128)(2,1)}, u32[]{:S(2)}) copy-start(bf16[768,768]{1,0:T(8,128)(2,1)} %get-tuple-element.63) | copy-start | bytes 3538948
  444.7 4.2 copy-start.4
  444.7 4.2 copy-start.8
  444.7 4.2 copy-start.21
Sparse Core Ops, SparseCore 0:
  187.6 35.5 reduce-scatter.8
  226.5 37.9 reduce-scatter.6

commit v3 on v2

--- a/solution.py
+++ b/solution.py
@@ -564,6 +564,146 @@
     )(*operands)
 
 
+def ring_place(count):
+    place = lax.axis_index("seq")
+    row, col = place // 2, place % 2
+    return jnp.where(col == 0, row, count - 1 - row)
+
+
+def ring_device(rank, count):
+    return jnp.where(rank < count // 2, 2 * rank, 2 * (count - 1 - rank) + 1)
+
+
+def ring_steps(count, plan, outs, bufs, sems):
+    rs_send, rs_recv, ag_send, ag_recv, keep_sem = sems
+    head = lax.axis_index("head")
+    rank = ring_place(count)
+    peers = {
+        1: ring_device(lax.rem(rank + 1, count), count),
+        -1: ring_device(lax.rem(rank + count - 1, count), count),
+    }
+
+    def chunk_of(direction, step):
+        return lax.rem(rank - direction * step + 2 * count, count)
+
+    def partial(i, chunk):
+        left, right, first, cols, _ = plan[i]
+        rows = left.shape[0] // count
+        return mul(left[ds(chunk * rows, rows), :], right[:, first : first + cols], NN)
+
+    def block_of(i, chunk):
+        return outs[i].at[ds(chunk * bufs[i].shape[1], bufs[i].shape[1])]
+
+    def rs(i, step):
+        return remote(
+            bufs[i].at[step],
+            bufs[i].at[step + 1],
+            rs_send.at[i, step],
+            rs_recv.at[i, step],
+            peers[plan[i][4]],
+            head,
+        )
+
+    def ag(i, step, first=False):
+        there = block_of(i, chunk_of(plan[i][4], step - 1))
+        here = bufs[i].at[count - 1] if first else there
+        return remote(
+            here, there, ag_send.at[i, step], ag_recv.at[i, step], peers[plan[i][4]], head
+        )
+
+    def keep(i):
+        block = block_of(i, chunk_of(plan[i][4], count - 1))
+        return pltpu.make_async_copy(bufs[i].at[count - 1], block, keep_sem.at[i])
+
+    def begin(i):
+        bufs[i][0] = partial(i, chunk_of(plan[i][4], 0)).astype(BF16)
+        rs(i, 0).start()
+
+    def bounds(slot, slots, steps):
+        low = lax.div(steps * slot + slots - 1, slots)
+        return 1 + low, 1 + lax.div(steps * (slot + 1) + slots - 1, slots)
+
+    def advance(streams, slot, slots):
+        def step_of(step):
+            for i in streams:
+                own = partial(i, chunk_of(plan[i][4], step))
+                rs(i, step - 1).wait_recv()
+                bufs[i][step] = (own + bufs[i][step].astype(F32)).astype(BF16)
+
+                @pl.when(step < count - 1)
+                def _():
+                    rs(i, step).start()
+
+                @pl.when(step == count - 1)
+                def _():
+                    ag(i, 0, True).start()
+                    keep(i).start()
+
+        loop(*bounds(slot, slots, count - 1), step_of)
+
+    def pass_on(streams, slot, slots):
+        def step_of(step):
+            for i in streams:
+                ag(i, step - 1).wait_recv()
+                ag(i, step).start()
+
+        loop(*bounds(slot, slots, count - 2), step_of)
+
+    def pass_end(streams):
+        for i in streams:
+            ag(i, count - 2).wait_recv()
+
+    def drain(streams):
+        def one(step):
+            for i in streams:
+                rs(i, step).wait_send()
+                ag(i, step).wait_send()
+
+        loop(0, count - 1, one)
+        for i in streams:
+            keep(i).wait()
+
+    return begin, advance, pass_on, pass_end, drain
+
+
+def finish_kernel(gr, gl, xr, xl, wr, wl, gin_ref, wout_ref, small_ref):
+    ihalf, half = gr.shape[1], wr.shape[1]
+    gin_ref[:, 0, 0:ihalf] = gr[...].astype(F32)
+    gin_ref[:, 0, ihalf:] = gl[...].astype(F32)
+    gin_ref[:, 1, 0:ihalf] = xr[...].astype(F32)
+    gin_ref[:, 1, ihalf:] = xl[:, 0:ihalf].astype(F32)
+    small_ref[...] = xl[:, ihalf:].astype(F32).T
+    wout_ref[:, 0:half] = wr[...].astype(F32)
+    wout_ref[:, half:] = wl[...].astype(F32)
+
+
+def finish_weights(width, inner, streams):
+    steps = width // (2 * LANES)
+    tall, low = width // steps, inner // steps
+    wr, wl, gr, gl, xr, xl = streams
+
+    def block(array_in, rows):
+        return pl.BlockSpec((rows, array_in.shape[1]), lambda i: (i, 0))
+
+    return pl.pallas_call(
+        finish_kernel,
+        grid=(steps,),
+        in_specs=[block(a, tall) for a in (gr, gl, xr, xl)] + [block(a, low) for a in (wr, wl)],
+        out_specs=[
+            pl.BlockSpec((tall, 2, inner), lambda i: (i, 0, 0)),
+            pl.BlockSpec((low, width), lambda i: (i, 0)),
+            pl.BlockSpec((LANES, tall), lambda i: (0, i)),
+        ],
+        out_shape=[
+            jax.ShapeDtypeStruct((width, 2, inner), F32),
+            jax.ShapeDtypeStruct((inner, width), F32),
+            jax.ShapeDtypeStruct((LANES, width), F32),
+        ],
+        compiler_params=pltpu.CompilerParams(vmem_limit_bytes=VMEM_LIMIT),
+        name="finish_weights",
+    )(gr, gl, xr, xl, wr, wl)
+
+
 def backward_kernel(
     dims,
     dy_ref,
@@ -582,39 +722,120 @@
     vec_ref,
     pack_ref,
     gather_ref,
-    dx_ref,
-    dsmall_ref,
-    gx_ref,
-    gbc_ref,
-    gdt_ref,
-    dconv,
-    dconvbc,
-    prebc,
-    dbc,
-    ddt,
-    added,
-    local,
-    arrived,
-    passed,
-    incoming,
-    bc_out,
-    bc_in,
-    edge_send,
-    edge_recv,
-    bc_send,
-    bc_recv,
-    st_send,
-    st_recv,
-    back_send,
-    back_recv,
+    normed_t_ref,
+    ng_t_ref,
+    cot_ref,
+    dgate_ref,
+    small_weight_ref,
+    sums_ref,
+    gain_ref,
+    row_scale_ref,
+    tokens_ref,
+    weight_ref,
+    *rest,
 ):
     count, parts, seqs, block, inner, heads, state = dims
+    outs, rest = rest[:6], rest[6:]
+    grad_ref, total_ref, *rest = rest
+    bufs, rest = rest[:6], rest[6:]
+    (
+        dx_ref,
+        gx_ref,
+        gbc_ref,
+        gdt_ref,
+        weights,
+        conv_buf,
+        dn_out,
+        dn_in,
+        token_buf,
+        rowsum,
+        shared,
+        rs_send,
+        rs_recv,
+        ag_send,
+        ag_recv,
+        keep_sem,
+        weight_sem,
+        conv_sem,
+        token_sem,
+        dn_send,
+        dn_recv,
+        row_send,
+        row_recv,
+        sum_send,
+        sum_recv,
+        *rest,
+    ) = rest
+    (
+        dconv,
+        dconvbc,
+        prebc,
+        dbc,
+        ddt,
+        added,
+        local,
+        arrived,
+        passed,
+        incoming,
+        bc_out,
+        bc_in,
+        edge_send,
+        edge_recv,
+        bc_send,
+        bc_recv,
+        st_send,
+        st_recv,
+        back_send,
+        back_recv,
+    ) = rest
     place, head = lax.axis_index("seq"), lax.axis_index("head")
+    rank = ring_place(count)
     chunks = block // CHUNK
     pairs = heads // 2
     total = seqs * chunks
+    rows_all = seqs * block
+    width = cot_ref.shape[1]
+    cols = width // parts
+    half, ihalf = width // 2, inner // 2
+    plan = (
+        (ng_t_ref, cot_ref, 0, half, 1),
+        (ng_t_ref, cot_ref, half, half, -1),
+        (normed_t_ref, dgate_ref, 0, ihalf, 1),
+        (normed_t_ref, dgate_ref, ihalf, ihalf, -1),
+        (normed_t_ref, dx_ref, 0, ihalf, 1),
+        (normed_t_ref, dx_ref, ihalf, ihalf + LANES, -1),
+    )
+    begin, advance, pass_on, pass_end, drain = ring_steps(
+        count, plan, outs, bufs, (rs_send, rs_recv, ag_send, ag_recv, keep_sem)
+    )
+    out_streams, gate_streams, x_streams = (0, 1), (2, 3), (4, 5)
     meet(count, parts)
     gdt_ref[...] = jnp.zeros_like(gdt_ref)
+
+    token_copy = pltpu.make_async_copy(
+        tokens_ref.at[:, pl.ds(pl.multiple_of(head * cols, cols), cols)], token_buf, token_sem
+    )
+    token_copy.start()
+
+    def weight_copy(i):
+        other = lax.rem(head + i, parts)
+        return pltpu.make_async_copy(
+            weight_ref.at[:, pl.ds(pl.multiple_of(other * cols, cols), cols)],
+            weights.at[lax.rem(i + 1, 2)],
+            weight_sem.at[lax.rem(i + 1, 2)],
+        )
+
+    def conv_copy(q):
+        t = q // chunks * chunks + chunks - 1 - lax.rem(q, chunks)
+        slot = lax.rem(q, 2)
+        return pltpu.make_async_copy(
+            conv_ref.at[ds(t * CHUNK, CHUNK)], conv_buf.at[slot], conv_sem.at[slot]
+        )
+
+    conv_copy(0).start()
+    weight_copy(1).start()
+    for i in out_streams + gate_streams:
+        begin(i)
 
     for s in range(seqs):
 
@@ -648,8 +869,12 @@
         (st_send, st_recv, back_send, back_recv),
         True,
     )
+    first = out_streams + gate_streams
+    slots = 2 + total
     start()
+    advance(first, 0, slots)
     carry()
+    advance(first, 1, slots)
     finish()
 
     side = iota((CHUNK, LANES), 1) < LANES // 2
@@ -661,6 +886,13 @@
             t = s * chunks + chunks - 1 - i
             rows = ds(t * CHUNK, CHUNK)
             out_rows = ds((s * chunks + chunks - 1 - i) * CHUNK, CHUNK)
+            turn = s * chunks + i
+            conv_copy(turn).wait()
+
+            @pl.when(turn + 1 < total)
+            def _():
+                conv_copy(turn + 1).start()
+
             cum, dt = cum_ref[rows, :], dt_ref[rows, :]
             cum_t = cum.T
             grown = jnp.exp(cum)
@@ -700,7 +932,7 @@
                 into_x.append((stepped * tail_p).astype(BF16))
                 into_y.append((dyf * pair_of(grown, p)).astype(BF16))
                 last.append(jnp.sum(rounded * from_state, axis=0, keepdims=True))
-                conv = conv_ref[rows, lane]
+                conv = conv_buf[lax.rem(turn, 2), :, lane]
                 sg = sigmoid(conv)
                 d_act = dt_p * d_step_x + chan_ref[6:7, lane] * dyf
                 dconv[s, ds((chunks - 1 - i) * CHUNK, CHUNK), lane] = d_act * (
@@ -724,6 +956,7 @@
             gdt_ref[0:8, :] += eights(d_dt)
             gdt_ref[8:16, :] += eights(d_log * (dt * vec_ref[6:7, :]))
             ddt[out_rows, :] = d_dt
+            advance(first, 2 + s * chunks + i, slots)
             return fall * held + added[t]
 
         lax.fori_loop(0, chunks, chunk, incoming[s].astype(F32))
@@ -807,6 +1040,7 @@
                 if k == KER - 1:
                     gx_ref[8 * KER : 8 * KER + 8, lane] += eights(d)
             dx_ref[rows, lane] = pre.astype(BF16)
+        pass_on(out_streams, t, 2 * total)
 
     loop(0, total, x_chunk)
 
@@ -833,7 +1067,121 @@
         rows = slice(s * block, (s + 1) * block)
         mine = pre if s == seqs - 1 else pltpu.roll(pre, LANES // 2, 1)
         step = jnp.where(at < heads, ddt[rows, :], 0.0)
-        dsmall_ref[rows, :] = jnp.where(at < LANES // 2, step, mine).astype(BF16)
+        dx_ref[rows, inner:] = jnp.where(at < LANES // 2, step, mine).astype(BF16)
+
+    for i in x_streams:
+        begin(i)
+
+    tall = 2 * CHUNK
+
+    def dn_copy(i):
+        other = lax.rem(head + i, parts)
+        return remote(
+            dn_out.at[other], dn_in.at[head], dn_send.at[i], dn_recv.at[i], place, other
+        )
+
+    def d_normed(i):
+        other = lax.rem(head + i, parts)
+        slot = lax.rem(i + 1, 2)
+
+        @pl.when(i < parts)
+        def _():
+            weight_copy(i + 1).start()
+
+        weight_copy(i).wait()
+        mine = small_weight_ref[pl.ds(pl.multiple_of(other * cols, cols), cols), :]
+
+        def some(r):
+            rows = ds(r * tall, tall)
+            part = mul(dgate_ref[rows, :], weights[slot, 0], NT)
+            part = part + mul(dx_ref[rows, 0:inner], weights[slot, 1], NT)
+            part = part + mul(dx_ref[rows, inner:], mine, NT)
+            dn_out[other, rows, :] = part.astype(BF16)
+
+        loop(0, rows_all // tall, some)
+
+        @pl.when(i < parts)
+        def _():
+            dn_copy(i).start()
+
+    def d_normed_step(i):
+        d_normed(i)
+        advance(x_streams, i - 1, parts)
+        pass_on(out_streams, total + i - 1, 2 * total)
+
+    loop(1, parts + 1, d_normed_step)
+    for i in range(parts, total):
+        pass_on(out_streams, total + i, 2 * total)
+    slots = 2 * total + 2
+    pass_on(gate_streams + x_streams, 0, slots)
+
+    loop(1, parts, lambda i: dn_copy(i).wait())
+    dn_in[head] = dn_out[head]
+    token_copy.wait()
+    my_cols = pl.ds(pl.multiple_of(head * cols, cols), cols)
+
+    def own(t, grads):
+        rows = ds(t * CHUNK, CHUNK)
+        d = dn_in[0, rows, :].astype(F32)
+        for k in range(1, parts):
+            d = d + dn_in[k, rows, :].astype(F32)
+        token = token_buf[rows, :].astype(F32)
+        grads = grads + eights(d * (token * row_scale_ref[rows, :]))
+        d = d * gain_ref[:, my_cols]
+        grad_ref[rows, :] = d
+        line = jnp.sum(d * token, axis=1, keepdims=True)
+        line = jnp.where(iota((CHUNK, LANES), 1) == 0, line, 0.0)
+        rowsum[head, t] = line.T[0:8, :]
+        pass_on(gate_streams + x_streams, 1 + t, slots)
+        return grads
+
+    norm_grads = lax.fori_loop(0, total, own, jnp.zeros((8, cols), F32))
+    rows_copy = head_copy(
+        parts, lambda _: rowsum.at[head], lambda k: rowsum.at[k], row_send, row_recv
+    )
+    loop(1, parts, lambda i: rows_copy(i).start())
+
+    def summed(ref, k):
+        return jnp.sum(ref[8 * k : 8 * k + 8, :], axis=0, keepdims=True)
+
+    shared[place] = jnp.zeros(shared.shape[1:], F32)
+    for k in range(KER + 1):
+        shared[place, k : k + 1, 0:inner] = summed(gx_ref, k)
+        shared[place, k : k + 1, inner:] = summed(gbc_ref, k)
+    for k in range(2):
+        shared[place, KER + 1 + k : KER + 2 + k, 0:inner] = summed(sums_ref, k)
+        shared[place, KER + 1 + k : KER + 2 + k, inner:] = summed(gdt_ref, k)
+    shared[place, 7:8, 0:cols] = jnp.sum(norm_grads, axis=0, keepdims=True)
+    sums_copy = line_copy(
+        count, lambda _: shared.at[place], lambda k: shared.at[k], sum_send, sum_recv
+    )
+    loop(1, count, lambda i: sums_copy(i).start())
+    pass_on(gate_streams + x_streams, 1 + total, slots)
+    loop(1, parts, lambda i: rows_copy(i).wait())
+
+    def finish_rows(t):
+        rows = ds(t * CHUNK, CHUNK)
+        sums = rowsum[0, t]
+        for k in range(1, parts):
+            sums = sums + rowsum[k, t]
+        turned = jnp.concatenate([sums, jnp.zeros((CHUNK - 8, LANES), F32)], axis=0).T
+        scale = row_scale_ref[rows, :]
+        pull = scale * scale * scale * (turned[:, 0:1] / width)
+        grad_ref[rows, :] = (
+            scale * grad_ref[rows, :]
+            - token_buf[rows, :].astype(F32) * pull
+            + cot_ref[rows, my_cols].astype(F32)
+        )
+        pass_on(gate_streams + x_streams, 2 + total + t, slots)
+
+    loop(0, total, finish_rows)
+    loop(1, count, lambda i: sums_copy(i).wait())
+    everything = shared[0]
+    for k in range(1, count):
+        everything = everything + shared[k]
+    total_ref[...] = everything
+    pass_end(out_streams + gate_streams + x_streams)
+    drain(out_streams + gate_streams + x_streams)
 
     @pl.when(place > 0)
     def _():
@@ -847,22 +1195,56 @@
     rows = seqs * block
     chunks = rows // CHUNK
     cut_rows, _, cut_lanes = cut_of(count, seqs, state, inner)
+    normed_rows, ng_rows, width = (operands[k].shape[d] for k, d in ((16, 0), (17, 0), (18, 1)))
+    cols = width // parts
     spec = pl.BlockSpec(memory_space=pltpu.VMEM)
+    far = pl.BlockSpec(memory_space=pl.ANY)
     line, ring = pltpu.SemaphoreType.DMA((count,)), pltpu.SemaphoreType.DMA((parts,))
     edge = pltpu.SemaphoreType.DMA((seqs + 1,))
-    outs = [
-        ((rows, inner), BF16),
-        ((rows, LANES), BF16),
-        ((8 * (KER + 1), inner), F32),
-        ((8 * (KER + 1), LANES), F32),
-        ((16, LANES), F32),
+    half, ihalf = width // 2, inner // 2
+    streams = [
+        (ng_rows, half),
+        (ng_rows, half),
+        (normed_rows, ihalf),
+        (normed_rows, ihalf),
+        (normed_rows, ihalf),
+        (normed_rows, ihalf + LANES),
     ]
+    steps = pltpu.SemaphoreType.DMA((len(streams), count))
+    outs = [(shape, BF16) for shape in streams]
+    outs = outs + [((rows, cols), F32), ((8, inner + LANES), F32)]
     return pl.pallas_call(
         functools.partial(backward_kernel, dims),
         out_shape=[jax.ShapeDtypeStruct(*o) for o in outs],
-        in_specs=[spec] * len(operands),
-        out_specs=[spec] * len(outs),
-        scratch_shapes=[
+        in_specs=[spec] * 3 + [far] + [spec] * (len(operands) - 6) + [far] * 2,
+        out_specs=[far] * len(streams) + [spec] * 2,
+        scratch_shapes=[vmem((count, r // count, c), BF16) for r, c in streams]
+        + [
+            vmem((rows, inner + LANES), BF16),
+            vmem((8 * (KER + 1), inner), F32),
+            vmem((8 * (KER + 1), LANES), F32),
+            vmem((16, LANES), F32),
+            vmem((2, 2, cols, inner), BF16),
+            vmem((2, CHUNK, inner), F32),
+            vmem((parts, rows, cols), BF16),
+            vmem((parts, rows, cols), BF16),
+            vmem((rows, cols), BF16),
+            vmem((parts, chunks, 8, LANES), F32),
+            vmem((count, 8, inner + LANES), F32),
+            steps,
+            steps,
+            steps,
+            steps,
+            pltpu.SemaphoreType.DMA((len(streams),)),
+            pltpu.SemaphoreType.DMA((2,)),
+            pltpu.SemaphoreType.DMA((2,)),
+            pltpu.SemaphoreType.DMA,
+            ring,
+            ring,
+            ring,
+            ring,
+            line,
+            line,
             vmem((seqs, block + 8, inner), F32),
             vmem((block + 8, LANES), F32),
             vmem((block, LANES), F32),
@@ -889,176 +1271,6 @@
         ),
         name="mixer_backward",
     )(*operands)
-
-
-def ring_place(count):
-    place = lax.axis_index("seq")
-    row, col = place // 2, place % 2
-    return jnp.where(col == 0, row, count - 1 - row)
-
-
-def ring_device(rank, count):
-    return jnp.where(rank < count // 2, 2 * rank, 2 * (count - 1 - rank) + 1)
-
-
-def ring_kernel(count, plan, *refs):
-    n_lhs = 1 + max(p[0] for p in plan)
-    n_rhs = 1 + max(p[1] for p in plan)
-    streams = len(plan)
-    lhs, refs = refs[:n_lhs], refs[n_lhs:]
-    rhs, refs = refs[:n_rhs], refs[n_rhs:]
-    small_ref, refs = refs[0], refs[1:]
-    outs, refs = refs[:streams], refs[streams:]
-    small_out, refs = refs[0], refs[1:]
-    bufs, refs = refs[:streams], refs[streams:]
-    small_buf, rs_send, rs_recv, ag_send, ag_recv, sm_send, sm_recv = refs
-    head = lax.axis_index("head")
-    place = lax.axis_index("seq")
-    rank = ring_place(count)
-    peers = {
-        1: (ring_device(lax.rem(rank + 1, count), count), head),
-        -1: (ring_device(lax.rem(rank + count - 1, count), count), head),
-    }
-    barrier = pltpu.get_barrier_semaphore()
-
-    def greet(i, _):
-        other = lax.rem(place + i, count)
-        pl.semaphore_signal(barrier, inc=1, device_id=(other, head), device_id_type=MESH)
-        return 0
-
-    lax.fori_loop(1, count, greet, 0)
-    pl.semaphore_wait(barrier, count - 1)
-
-    small_buf[place] = small_ref[...]
-
-    def small_copy(i):
-        other = lax.rem(place + i, count)
-        return pltpu.make_async_remote_copy(
-            src_ref=small_ref,
-            dst_ref=small_buf.at[place],
-            send_sem=sm_send.at[i],
-            recv_sem=sm_recv.at[i],
-            device_id=(other, head),
-            device_id_type=MESH,
-        )
-
-    def small_start(i, _):
-        small_copy(i).start()
-        return 0
-
-    lax.fori_loop(1, count, small_start, 0)
-
-    def chunk_of(direction, step):
-        return lax.rem(rank - direction * step + 2 * count, count)
-
-    def partial(i, chunk):
-        l, r, first, cols, _ = plan[i]
-        rows = lhs[l].shape[0] // count
-        left = lhs[l][pl.ds(pl.multiple_of(chunk * rows, rows), rows), :]
-        return jnp.dot(left, rhs[r][:, first : first + cols], preferred_element_type=jnp.float32)
-
-    def rs_copy(i, step):
-        return pltpu.make_async_remote_copy(
-            src_ref=bufs[i].at[step],
-            dst_ref=bufs[i].at[step + 1],
-            send_sem=rs_send.at[i, step],
-            recv_sem=rs_recv.at[i, step],
-            device_id=peers[plan[i][4]],
-            device_id_type=MESH,
-        )
-
-    def ag_copy(i, step):
-        rows = bufs[i].shape[1]
-        chunk = chunk_of(plan[i][4], step - 1)
-        block = outs[i].at[pl.ds(pl.multiple_of(chunk * rows, rows), rows)]
-        return pltpu.make_async_remote_copy(
-            src_ref=block,
-            dst_ref=block,
-            send_sem=ag_send.at[i, step],
-            recv_sem=ag_recv.at[i, step],
-            device_id=peers[plan[i][4]],
-            device_id_type=MESH,
-        )
-
-    for i in range(streams):
-        bufs[i][0] = partial(i, chunk_of(plan[i][4], 0)).astype(jnp.bfloat16)
-        rs_copy(i, 0).start()
-
-    def rs_step(step, _):
-        for i in range(streams):
-            own = partial(i, chunk_of(plan[i][4], step))
-            rs_copy(i, step - 1).wait_recv()
-            bufs[i][step] = (own + bufs[i][step].astype(jnp.float32)).astype(jnp.bfloat16)
-            rs_copy(i, step).start()
-        return 0
-
-    lax.fori_loop(1, count - 1, rs_step, 0)
-    for i in range(streams):
-        chunk = chunk_of(plan[i][4], count - 1)
-        rows = bufs[i].shape[1]
-        own = partial(i, chunk)
-        rs_copy(i, count - 2).wait_recv()
-        done = (own + bufs[i][count - 1].astype(jnp.float32)).astype(jnp.bfloat16)
-        outs[i][pl.ds(pl.multiple_of(chunk * rows, rows), rows), :] = done
-        ag_copy(i, 0).start()
-
-    def ag_step(step, _):
-        for i in range(streams):
-            ag_copy(i, step - 1).wait_recv()
-            ag_copy(i, step).start()
-        return 0
-
-    lax.fori_loop(1, count - 1, ag_step, 0)
-    for i in range(streams):
-        ag_copy(i, count - 2).wait_recv()
-
-    def small_wait(i, _):
-        small_copy(i).wait()
-        return 0
-
-    lax.fori_loop(1, count, small_wait, 0)
-    total = small_buf[0]
-    for i in range(1, count):
-        total = total + small_buf[i]
-    small_out[...] = total
-
-    def drain(step, _):
-        for i in range(streams):
-            rs_copy(i, step).wait_send()
-            ag_copy(i, step).wait_send()
-        return 0
-
-    lax.fori_loop(0, count - 1, drain, 0)
-
-
-def ring_sum(count, plan, lhs, rhs, small):
-    rows = [lhs[p[0]].shape[0] for p in plan]
-    vmem = pl.BlockSpec(memory_space=pltpu.VMEM)
-    streams = len(plan)
-    sems = pltpu.SemaphoreType.DMA((streams, count))
-    return pl.pallas_call(
-        functools.partial(ring_kernel, count, plan),
-        out_shape=[jax.ShapeDtypeStruct((r, p[3]), jnp.bfloat16) for r, p in zip(rows, plan)]
-        + [jax.ShapeDtypeStruct(small.shape, jnp.float32)],
-        in_specs=[vmem] * (len(lhs) + len(rhs) + 1),
-        out_specs=[vmem] * (streams + 1),
-        scratch_shapes=[
-            pltpu.VMEM((count, r // count, p[3]), jnp.bfloat16) for r, p in zip(rows, plan)
-        ]
-        + [
-            pltpu.VMEM((count,) + small.shape, jnp.float32),
-            sems,
-            sems,
-            sems,
-            sems,
-            pltpu.SemaphoreType.DMA((count,)),
-            pltpu.SemaphoreType.DMA((count,)),
-        ],
-        compiler_params=pltpu.CompilerParams(
-            collective_id=1, has_side_effects=True, vmem_limit_bytes=56 * 2**20
-        ),
-        name="weight_ring",
-    )(*lhs, *rhs, small)
 
 
 def body(
@@ -1157,7 +1369,17 @@
         cot,
         output_weight,
     )
-    dx, dsmall, gx, gbc, gdt = backward(
+    def padded(array_in):
+        return jnp.pad(array_in, ((0, -array_in.shape[0] % (count * 16)), (0, 0)))
+
+    mixer = jnp.dot(ng, output_weight, preferred_element_type=F32)
+    mixed = lax.psum_scatter(
+        mixer.astype(BF16), "head", scatter_dimension=1, tiled=True
+    ).astype(F32)
+    own_inputs = lax.dynamic_slice_in_dim(input_batch, my_head * col_count, col_count, 1)
+    block_out = (own_inputs + mixed).astype(BF16)
+
+    *streams, grad_input, sums = backward(
         dims,
         dy,
         xact,
@@ -1175,82 +1397,36 @@
         vec,
         pack,
         gather,
-    )
-
-    mixer = jnp.dot(ng, output_weight, preferred_element_type=F32)
-    mixed = lax.psum_scatter(
-        mixer.astype(BF16), "head", scatter_dimension=1, tiled=True
-    ).astype(F32)
-    own_inputs = lax.dynamic_slice_in_dim(input_batch, my_head * col_count, col_count, 1)
-    block_out = (own_inputs + mixed).astype(BF16)
-
-    d_both = jnp.stack([dgate, dx], axis=1)
-    grad_normed = jnp.einsum(
-        "rkw,pkw->rp", d_both, gate_input_weight, preferred_element_type=F32
-    ) + lax.dot_general(dsmall, small_weight, (((1,), (1,)), ((), ())), preferred_element_type=F32)
-    d_own = lax.psum_scatter(
-        grad_normed.astype(BF16), "head", scatter_dimension=1, tiled=True
-    ).astype(F32)
-    own_gain = lax.dynamic_slice_in_dim(norm_gain, my_head * col_count, col_count, 0)
-    grad_norm_gain = jnp.sum(d_own * own_inputs * row_scale, axis=0)
-    d_units = d_own * own_gain
-    row_sum = lax.psum(jnp.sum(d_units * own_inputs, axis=-1, keepdims=True), "head")
-    own_cot = lax.dynamic_slice_in_dim(cot, my_head * col_count, col_count, 1).astype(F32)
-    grad_input = row_scale * d_units - own_inputs * row_scale**3 * (row_sum / width) + own_cot
-
-    def padded(array_in):
-        return jnp.pad(array_in, ((0, -array_in.shape[0] % (count * 16)), (0, 0)))
-
-    normed_t, ng_t = padded(normed.T), padded(ng.T)
-    narrow = jnp.concatenate([dx, dsmall], axis=1)
-    hw, hi = width // 2, inner // 2
-    plan = (
-        (0, 0, 0, hw, 1),
-        (0, 0, hw, hw, -1),
-        (1, 1, 0, hi, 1),
-        (1, 1, hi, hi, -1),
-        (1, 2, 0, hi, 1),
-        (1, 2, hi, hi + LANES, -1),
-    )
-    taps = gx.reshape(KER + 1, 8, inner).sum(1)
-    taps_bc = gbc.reshape(KER + 1, 8, 2, half).sum((1, 2))
-    gdt = gdt.reshape(2, 8, LANES).sum(1)[:, :heads]
-    sums = sums.reshape(2, 8, inner).sum(1)
-    skip = sums[1].reshape(heads, inner // heads).sum(1)
-    smalls = [taps.reshape(-1), taps_bc.reshape(-1), gdt.reshape(-1), skip, sums[0], grad_norm_gain]
-    sizes = [a.shape[0] for a in smalls]
-    flat = jnp.concatenate(smalls)
-    lines = -(-flat.shape[0] // 1024) * 8
-    flat = jnp.pad(flat, (0, lines * LANES - flat.shape[0])).reshape(lines, LANES)
-    *wide, flat = ring_sum(count, plan, (ng_t, normed_t), (cot, dgate, narrow), flat)
-    flat = flat.reshape(-1)
-    cuts = []
-    begin = 0
-    for size in sizes:
-        cuts.append(flat[begin : begin + size])
-        begin += size
-    taps, taps_bc = cuts[0].reshape(KER + 1, inner), cuts[1].reshape(KER + 1, 2, state_part)
-    g_dt, g_a = cuts[2].reshape(2, heads)
-    wide = [a.astype(F32) for a in wide]
-    g_w_out = jnp.concatenate(wide[:2], axis=1)[:inner]
-    g_gate = jnp.concatenate(wide[2:4], axis=1)[:width]
-    g_narrow = jnp.concatenate(wide[4:], axis=1)[:width]
-    g_small = g_narrow[:, inner:]
+        padded(normed.T),
+        padded(ng.T),
+        cot,
+        dgate,
+        small_weight,
+        sums,
+        norm_gain[None],
+        row_scale,
+        tokens.reshape(rows, width),
+        gate_input_weight.transpose(1, 0, 2),
+    )
+    g_in, g_w_out, g_small = finish_weights(width, inner, streams)
+    taps = sums[:, :inner]
+    lanes = sums[:, inner:]
+    taps_bc = (lanes[:, :half] + lanes[:, half:]).reshape(8, 2, state_part)
     return (
         block_out.reshape(seqs, block, col_count),
         grad_input.reshape(seqs, block, col_count),
-        cuts[5],
-        jnp.stack([g_gate, g_narrow[:, :inner]], axis=1),
-        g_small[:, half:].reshape(width, 2, state_part),
-        g_small[:, :heads],
+        taps[KER + 3, :col_count],
+        g_in,
+        g_small[half:].reshape(2, state_part, width).transpose(2, 0, 1),
+        g_small[:heads].T,
         taps[:KER],
         taps_bc[:KER],
         taps[KER],
         taps_bc[KER],
-        g_dt,
-        g_a,
-        cuts[3],
-        cuts[4],
+        lanes[KER + 1, :heads],
+        lanes[KER + 2, :heads],
+        taps[KER + 2].reshape(heads, inner // heads).sum(1),
+        taps[KER + 1],
         g_w_out,
     )
 

time: 468 us -> 387 us (0.83); the launches traced: 460 us -> 386 us
  local copies, waits for them, and re-layouts: 59.9 us -> 32.5 us
  waiting for transfers between devices: 16.6 us -> 0.02 us
  Pallas kernels: 309 us -> 298 us
  blocking collectives: 6.14 us -> 0 us
  matrix products: 22.1 us -> 16.1 us
  other arithmetic: 30.5 us -> 24.7 us
    pallas_call x1, Pallas kernels: 165 us -> 9.85 us  [finish_weights(): pl.pallas_call(finish_kernel, grid=(steps,), in_specs=[block(a, tall) for...]
    pallas_call x1, Pallas kernels: 69.9 us -> 214 us  [backward(): pl.pallas_call(functools.partial(backward_kernel, dims), out_shape=[jax.S...]
    unnamed x73 -> x45, local copies, waits for them, and re-layouts: 40.8 us -> 11 us
    unnamed x4 -> x1, waiting for transfers between devices: 16.6 us -> 0.02 us
    dot_general x2 -> x0, matrix products: 8.57 us -> none  [the longest x1 7.5 us: body(): jnp.einsum('rkw,pkw->rp', d_both, gate_input_weight, preferred_element_ty...]
    psum x1 -> x0, blocking collectives: 6.14 us -> none  [body(): lax.psum(jnp.sum(d_units * own_inputs, axis=-1, keepdims=True), 'head')]
    concatenate x2 -> x1, other arithmetic: 7.01 us -> 1.36 us  [body(): jnp.concatenate([step_weight, jnp.zeros((width, half - heads), BF16), coe...]
    transpose x0 -> x1, other arithmetic: none -> 5.56 us  [body(): *streams, grad_input, sums = backward(dims, dy, xact, bc, conv, convbc, d...]
  transfers between devices with their start and end apart: 2 -> 1, of which waited for: 1 -> 0; matrix products, arithmetic and copies ran while one was open for 6% -> 6% of each run, Pallas kernels for 36% -> 58%
where the time goes in v3:
time: 387 us; the launch traced here: 386 us
  Pallas kernels  298 us (77%)
  local copies, waits for them, and re-layouts  32.5 us (8%)
  other arithmetic  24.7 us (6%)
  matrix products  16.1 us (4%)
  between operations  14.3 us (4%)
    pallas_call x1, Pallas kernels, backward(): pl.pallas_call(functools.partial(backward_kernel, dims), out_shape=[jax.S...  214 us
    pallas_call x1, Pallas kernels, forward(): pl.pallas_call(functools.partial(forward_kernel, dims), out_shape=[jax.Sh...  74.4 us
    unnamed x45, local copies, waits for them, and re-layouts  11 us
    pallas_call x1, Pallas kernels, finish_weights(): pl.pallas_call(finish_kernel, grid=(steps,), in_specs=[block(a, tall) for...  9.85 us
    dot_general x1, matrix products, body(): jnp.einsum('rp,pkw->krw', normed, gate_input_weight, preferred_element_ty...  8.7 us
  transfers between devices with their start and end apart: 1, of which 0 were waited for; matrix products, arithmetic and copies ran while one was open for 6% of the time, Pallas kernels for 58%

profile of v3, /device:TPU:0, one launch (start us, length us, event | category | flops | bytes accessed | tf_op | source)
XLA Modules:
  0.0 386.0 jit_solution(15040175594039560825)
XLA Ops:
  7.2 0.5 iota_multiply_fusion
  7.7 0.6 iota_shift-right-logical_fusion.1
  8.3 0.6 fusion.40
  8.9 0.6 iota_bitcast_fusion
  9.5 0.5 compare_and_fusion
  10.0 0.8 fusion.33.expand_ref
  10.8 0.8 fusion.34.gather_ref
  11.6 2.6 multiply_reduce_fusion
  14.2 3.6 copy.51
  17.9 3.4 multiply_convert_fusion
  21.3 8.7 %fusion.3 = f32[2,1024,768]{2,1,0:T(8,128)S(1)} fusion(bf16[1536,2,768]{2,1,0:T(2,128)(2,1)} %param.17, bf16[1024,1536]{0,1:T(8,128)(2,1)S(1)} %multiply_convert_fusion), kind=kOutput, calls=%fused_computation.9 | convolution fusion | flops 4831838208 | bytes 14155776 | tf_op jit(solution)/shard_map/rp,pkw->krw/dot_general | solution.py:1308
  30.0 3.1 slice_bitcast_fusion
  33.1 0.9 copy.43
  34.0 1.0 copy.42
  35.1 1.4 pad_maximum_fusion.small_weight_ref
  36.5 1.8 fusion.42.small_ref
  38.5 0.7 negate_bitcast_fusion
  39.1 0.8 reshape.498
  39.9 0.8 reshape.497
  40.6 0.7 broadcast_bitcast_fusion
  41.4 1.1 fusion.32
  42.5 0.9 add_convert_fusion.1.unpack_ref
  43.4 0.7 maximum_maximum_fusion
  44.2 0.7 select_maximum_fusion.vec_ref
  44.8 1.3 concatenate.17.chan_ref
  46.2 74.4 %mixer_forward.1 = (bf16[1024,768]{1,0:T(8,128)(2,1)}, bf16[1024,256]{1,0:T(8,128)(2,1)}, f32[1024,768]{1,0:T(8,128)}, f32[512,128]{1,0:T(8,128)}, f32[1024,128]...) custom-call(f32[1024,768]{1,0:T(8,128)} %get-tuple-element.97.x_ref,, ...), custom_call_target="tpu_custom_call" | custom-call | tf_op jit(solution)/shard_map/mixer_forward/pallas_call | solution.py:526
  120.6 5.6 %convolution_convert_fusion = bf16[1024,1536]{0,1:T(8,128)(2,1)} fusion(bf16[1024,768]{1,0:T(8,128)(2,1)} %get-tuple-element.39, bf16[768,1536]{1,0:T(8,128)(2,1)S(1)} %copy-done.2), kind=kOutput, calls=%fused_computation.5 | convolution fusion | flops 2417491968 | bytes 7077888 | tf_op jit(solution)/shard_map/dot_general | solution.py:1375
  126.2 1.4 copy-done.4
  127.6 1.6 copy.45
  129.2 0.6 broadcast_in_dim.151.gain_ref
  129.9 5.2 %copy.62 = bf16[1536,2,768]{2,0,1:T(8,128)(2,1)} copy(bf16[1536,2,768]{2,1,0:T(2,128)(2,1)} %param.17) | data formatting | bytes 9437184 | tf_op args[2]
  135.0 1.1 copy.56
  136.6 0.9 fusion.12.pack_ref
  137.5 5.6 %fusion.47.normed_t_ref = bf16[1536,1024]{1,0:T(8,128)(2,1)} fusion(f32[1536]{0:T(1024)S(1)} %copy-done.6, f32[1024,1536]{0,1:T(8,128)} %copy.51, f32[1024]{0:T(1024)S(1)} %bitcast.69), kind=kLoop, calls=%fused_computation.99 | loop fusion | flops 4718592 | bytes 9447424 | tf_op jit(solution)/shard_map/transpose | solution.py:1400
  143.1 214.1 %mixer_backward.1 = (bf16[768,768]{1,0:T(8,128)(2,1)}, bf16[768,768]{1,0:T(8,128)(2,1)}, bf16[1536,384]{1,0:T(8,128)(2,1)}, bf16[1536,384]{1,0:T(8,128)(2,1)}, b...) custom-call(bf16[1024,768]{1,0:T(8,128)(2,1)} %get-tuple-element.40.dy_ref, ...), custom_call_target="tpu_custom_call" | custom-call | tf_op jit(solution)/shard_map/mixer_backward/pallas_call | solution.py:1216
  357.2 9.9 %finish_weights.1 = (f32[1536,2,768]{2,1,0:T(2,128)}, f32[768,1536]{1,0:T(8,128)}, f32[128,1536]{1,0:T(8,128)}) custom-call(bf16[1536,384]{1,0:T(8,128)(2,1)} %get-tuple-element.54.gr, bf16[1536,384]{1,0:T(8,128)(2,1)} %get-tuple-element.55.gl, bf16[1536,384]{1,0:T(8,128)(2,1)} %get-tuple-element.56.xr, bf16[1536,512]{1,0:T(8,128)(2,1)} %get-tuple-element.57.xl, ...), custom_call_target="tpu_custom_call" | custom-call | tf_op jit(solution)/shard_map/finish_weights/pallas_call | solution.py:688
  367.0 1.9 slice.63
  368.9 0.6 slice.65
  369.6 0.7 slice.69
  370.3 0.6 squeeze.28
  371.0 0.6 slice_reduce_fusion
  371.6 0.6 reduce_sum.19
  372.3 0.6 slice_reduce_fusion.3
  372.9 0.5 slice_bitcast_fusion.3
  373.4 1.5 slice_bitcast_fusion.2
  374.9 1.9 add_convert_fusion
  376.8 1.2 copy.53
  378.0 1.1 copy.64
  (57 shorter events, 1.1 us)
Async XLA Ops:
  7.2 7.0 %copy-start = (bf16[2,512,1536]{2,1,0:T(8,128)(2,1)S(1)}, bf16[2,512,1536]{2,1,0:T(8,128)(2,1)}, u32[]{:S(2)}) copy-start(bf16[2,512,1536]{2,1,0:T(8,128)(2,1)} %param.15) | copy-start | bytes 9437188
  7.2 367.7 %reduce-scatter.2.cloned.1.call-start = ((), (), s32[]{:S(2)}) async-start(), calls=%async_computation.1 | async-start | bytes 3932160 | tf_op jit(solution)/shard_map/reduce_scatter | solution.py:1376
  14.2 3.7 copy-start.6
  30.0 3.1 copy-start.5
  30.0 4.0 %copy-start.7 = (bf16[1536,12]{0,1:T(8,128)(2,1)S(1)}, bf16[1536,12]{0,1:T(8,128)(2,1)}, u32[]{:S(2)}) copy-start(bf16[1536,12]{0,1:T(8,128)(2,1)} %param.19) | copy-start | bytes 110596
  35.0 3.3 copy-start.13
  35.0 3.3 copy-start.14
  35.0 3.3 copy-start.18
  36.4 84.1 %copy-start.1 = (bf16[1536,128]{1,0:T(8,128)(2,1)}, bf16[1536,128]{1,0:T(8,128)(2,1)S(1)}, u32[]{:S(2)}) copy-start(bf16[1536,128]{1,0:T(8,128)(2,1)S(1)} %pad_maximum_fusion.small_weight_ref) | copy-start | bytes 1179652
  46.2 74.4 %copy-start.2 = (bf16[768,1536]{1,0:T(8,128)(2,1)S(1)}, bf16[768,1536]{1,0:T(8,128)(2,1)}, u32[]{:S(2)}) copy-start(bf16[768,1536]{1,0:T(8,128)(2,1)} %wout_ref.1) | copy-start | bytes 7077892
  126.2 1.4 copy-start.4
  129.8 6.3 %copy-start.9 = (s32[256]{0:T(256)S(1)}, s32[256]{0:T(256)}, u32[]{:S(2)}) copy-start(s32[256]{0:T(256)} %get-tuple-element.108) | copy-start | bytes 3076
  129.8 6.3 %copy-start.10 = (s32[256]{0:T(256)S(1)}, s32[256]{0:T(256)}, u32[]{:S(2)}) copy-start(s32[256]{0:T(256)} %get-tuple-element.109) | copy-start | bytes 3076
  129.8 6.3 %copy-start.11 = (s32[256]{0:T(256)S(1)}, s32[256]{0:T(256)}, u32[]{:S(2)}) copy-start(s32[256]{0:T(256)} %get-tuple-element.112) | copy-start | bytes 3076
  129.8 6.3 %copy-start.12 = (s32[256]{0:T(256)S(1)}, s32[256]{0:T(256)}, u32[]{:S(2)}) copy-start(s32[256]{0:T(256)} %get-tuple-element.113) | copy-start | bytes 3076
  129.8 6.3 %copy-start.15 = (pred[256]{0:T(512)(128)(4,1)S(1)}, pred[256]{0:T(512)(128)(4,1)}, u32[]{:S(2)}) copy-start(pred[256]{0:T(512)(128)(4,1)} %get-tuple-element.110) | copy-start | bytes 772
  129.8 6.3 %copy-start.16 = (pred[256]{0:T(512)(128)(4,1)S(1)}, pred[256]{0:T(512)(128)(4,1)}, u32[]{:S(2)}) copy-start(pred[256]{0:T(512)(128)(4,1)} %get-tuple-element.111) | copy-start | bytes 772
  129.8 6.3 %copy-start.17 = (s32[4]{0:T(128)S(1)}, s32[4]{0:T(128)}, u32[]{:S(2)}) copy-start(s32[4]{0:T(128)} %iota_multiply_fusion) | copy-start | bytes 52
  357.2 11.8 %copy-start.8 = (f32[8,896]{1,0:T(8,128)S(1)}, f32[8,896]{1,0:T(8,128)}, u32[]{:S(2)}) copy-start(f32[8,896]{1,0:T(8,128)} %get-tuple-element.53) | copy-start | bytes 86020
  367.0 11.0 %copy-start.3 = (f32[1024,384]{1,0:T(8,128)S(1)}, f32[1024,384]{1,0:T(8,128)}, u32[]{:S(2)}) copy-start(f32[1024,384]{1,0:T(8,128)} %get-tuple-element.52) | copy-start | bytes 4718596
Sparse Core Ops, SparseCore 0:
  126.3 45.1 reduce-scatter.1

commit v4 on v3

--- a/solution.py
+++ b/solution.py
@@ -2,6 +2,7 @@
 
 import jax
 import jax.numpy as jnp
+import numpy as np
 from jax import lax
 from jax.experimental import pallas as pl
 from jax.experimental.pallas import tpu as pltpu
@@ -207,28 +208,43 @@
 def forward_kernel(
     dims,
     x_ref,
-    gate_ref,
+    gate_far,
     small_ref,
     chan_ref,
     vec_ref,
     unpack_ref,
     expand_ref,
     gather_ref,
+    cot_far,
+    wout_far,
+    xact_far,
+    bc_far,
+    conv_far,
+    convbc_ref,
+    dt_far,
+    cum_far,
+    states_far,
+    ng_t_far,
+    dgate_far,
+    dy_far,
+    dyy_far,
+    decay_ref,
+    sums_ref,
+    gate_ref,
     cot_ref,
     wout_ref,
     xact_ref,
     bc_ref,
     conv_ref,
-    convbc_ref,
     dt_ref,
     cum_ref,
     states_ref,
-    ng_ref,
+    ng_t_ref,
     dgate_ref,
     dy_ref,
     dyy_ref,
-    decay_ref,
-    sums_ref,
+    fetch_sem,
+    keep_sem,
     edge_x,
     edge_s,
     ext,
@@ -262,6 +278,31 @@
     chunks = block // CHUNK
     pairs = heads // 2
     total = seqs * chunks
+    fetches = [
+        pltpu.make_async_copy(src, dst, fetch_sem.at[k])
+        for k, (src, dst) in enumerate(
+            ((cot_far, cot_ref), (wout_far, wout_ref), (gate_far, gate_ref))
+        )
+    ]
+    for copy in fetches:
+        copy.start()
+    keeps = [
+        pltpu.make_async_copy(src, dst, keep_sem.at[k])
+        for k, (src, dst) in enumerate(
+            (
+                (xact_ref, xact_far),
+                (bc_ref, bc_far),
+                (conv_ref, conv_far),
+                (dt_ref, dt_far),
+                (cum_ref, cum_far),
+                (states_ref, states_far),
+                (ng_t_ref, ng_t_far),
+                (dgate_ref, dgate_far),
+                (dy_ref, dy_far),
+                (dyy_ref, dyy_far),
+            )
+        )
+    ]
     meet(count, parts)
 
     def edge_copies(ahead):
@@ -381,6 +422,8 @@
         False,
     )
     start()
+    for copy in keeps[:5]:
+        copy.start()
 
     def within(t):
         rows = ds(t * CHUNK, CHUNK)
@@ -406,6 +449,8 @@
         decay_ref[s] = mul(decays[:, s, :], expand_ref[...], NN, EXACT)
     carry()
 
+    for copy in fetches:
+        copy.wait()
     wide = 2 * LANES
 
     def back_project(i):
@@ -450,6 +495,7 @@
 
         lax.fori_loop(0, chunks, gate, incoming[s].astype(F32))
 
+    keeps[5].start()
     rows_copy = head_copy(
         parts, lambda _: rowsum.at[head], lambda k: rowsum.at[k], row_send, row_recv
     )
@@ -475,7 +521,7 @@
             x = xact_ref[rows, lane].astype(F32)
             gain = chan_ref[5:6, lane]
             scaled = gated * scale
-            ng_ref[rows, lane] = (scaled * gain).astype(BF16)
+            ng_t_ref[lane, rows] = (scaled * gain).T.astype(BF16)
             dng = dng_ref[rows, lane]
             d_gated = scale * (dng * gain) - gated * pull
             d_ssd = d_gated * (pre * sg)
@@ -489,6 +535,10 @@
         dyy_ref[rows, :] = dyy
 
     loop(0, total, outputs)
+    for copy in keeps[6:]:
+        copy.start()
+    for copy in keeps:
+        copy.wait()
 
     @pl.when(place < count - 1)
     def _():
@@ -505,7 +555,8 @@
     rows = seqs * block
     chunks = rows // CHUNK
     cut_rows, _, cut_lanes = cut_of(count, seqs, state, inner)
-    spec = pl.BlockSpec(memory_space=pltpu.VMEM)
+    spec, far = pl.BlockSpec(memory_space=pltpu.VMEM), pl.BlockSpec(memory_space=pl.ANY)
+    fetched, kept = (1, 8, 9), (0, 1, 2, 4, 5, 6, 7, 8, 9, 10)
     line, ring = pltpu.SemaphoreType.DMA((count,)), pltpu.SemaphoreType.DMA((parts,))
     edge = pltpu.SemaphoreType.DMA((2, seqs))
     outs = [
@@ -516,7 +567,7 @@
         ((rows, LANES), F32),
         ((rows, LANES), F32),
         ((chunks, state, inner), F32),
-        ((rows, inner), BF16),
+        ((inner, rows), BF16),
         ((rows, inner), BF16),
         ((rows, inner), BF16),
         ((rows, LANES), F32),
@@ -526,9 +577,13 @@
     return pl.pallas_call(
         functools.partial(forward_kernel, dims),
         out_shape=[jax.ShapeDtypeStruct(*o) for o in outs],
-        in_specs=[spec] * len(operands),
-        out_specs=[spec] * len(outs),
-        scratch_shapes=[
+        in_specs=[far if k in fetched else spec for k in range(len(operands))],
+        out_specs=[far if k in kept else spec for k in range(len(outs))],
+        scratch_shapes=[vmem(operands[k].shape, operands[k].dtype) for k in fetched]
+        + [vmem(*outs[k]) for k in kept]
+        + [
+            pltpu.SemaphoreType.DMA((len(fetched),)),
+            pltpu.SemaphoreType.DMA((len(kept),)),
             vmem((seqs, 8, inner), F32),
             vmem((seqs, 8, LANES), F32),
             vmem((CHUNK + 8, inner), F32),
@@ -564,6 +619,54 @@
     )(*operands)
 
 
+def project_kernel(
+    tokens_ref, gain_ref, weight_ref, small_weight_ref, gate_ref, x_ref, small_ref, turned_ref, scale_ref
+):
+    tokens = tokens_ref[...].astype(F32)
+    scale = lax.rsqrt(jnp.mean(tokens * tokens, axis=1, keepdims=True) + EPSILON)
+    scale_ref[...] = scale
+    normed = tokens * scale * gain_ref[...]
+    low = normed.astype(BF16)
+    turned_ref[...] = low.T
+    x_ref[...] = mul(low, weight_ref[1], NN)
+    small_ref[...] = mul(low, small_weight_ref[...], NN)
+    gate_ref[...] = mul(low, weight_ref[0], NN)
+
+
+def project(tokens, gain, weights, small_weight):
+    rows, width = tokens.shape
+    inner = weights.shape[2]
+    tall = 2 * CHUNK
+
+    def by_rows(cols):
+        return pl.BlockSpec((tall, cols), lambda i: (i, 0))
+
+    def whole(array_in):
+        return pl.BlockSpec(array_in.shape, lambda i: (0,) * array_in.ndim)
+
+    return pl.pallas_call(
+        project_kernel,
+        grid=(rows // tall,),
+        in_specs=[by_rows(width), whole(gain), whole(weights), whole(small_weight)],
+        out_specs=[
+            by_rows(inner),
+            by_rows(inner),
+            by_rows(LANES),
+            pl.BlockSpec((width, tall), lambda i: (0, i)),
+            by_rows(1),
+        ],
+        out_shape=[
+            jax.ShapeDtypeStruct((rows, inner), F32),
+            jax.ShapeDtypeStruct((rows, inner), F32),
+            jax.ShapeDtypeStruct((rows, LANES), F32),
+            jax.ShapeDtypeStruct((width, rows), BF16),
+            jax.ShapeDtypeStruct((rows, 1), F32),
+        ],
+        compiler_params=pltpu.CompilerParams(vmem_limit_bytes=VMEM_LIMIT),
+        name="project",
+    )(tokens, gain, weights, small_weight)
+
+
 def ring_place(count):
     place = lax.axis_index("seq")
     row, col = place // 2, place % 2
@@ -574,113 +677,158 @@
     return jnp.where(rank < count // 2, 2 * rank, 2 * (count - 1 - rank) + 1)
 
 
-def ring_steps(count, plan, outs, bufs, sems):
+def ring_steps(count, plan, outs, bufs, stages, sems):
     rs_send, rs_recv, ag_send, ag_recv, keep_sem = sems
+    far = count // 2
     head = lax.axis_index("head")
     rank = ring_place(count)
-    peers = {
-        1: ring_device(lax.rem(rank + 1, count), count),
-        -1: ring_device(lax.rem(rank + count - 1, count), count),
-    }
-
-    def chunk_of(direction, step):
-        return lax.rem(rank - direction * step + 2 * count, count)
+    arms = (1, -1)
+    peers = [ring_device(lax.rem(rank + a + count, count), count) for a in arms]
+
+    def chunk_at(distance):
+        return lax.rem(rank + distance + 2 * count, count)
 
     def partial(i, chunk):
-        left, right, first, cols, _ = plan[i]
+        left, right, cols, _ = plan[i]
         rows = left.shape[0] // count
-        return mul(left[ds(chunk * rows, rows), :], right[:, first : first + cols], NN)
+        return mul(left[ds(chunk * rows, rows), :], right[:, 0:cols], NN)
+
+    def half(i, arm):
+        cols, cut = plan[i][2:]
+        return slice(0, cut) if arm == 0 else slice(cut, cols)
 
     def block_of(i, chunk):
-        return outs[i].at[ds(chunk * bufs[i].shape[1], bufs[i].shape[1])]
-
-    def rs(i, step):
+        rows = plan[i][0].shape[0] // count
+        return outs[i].at[ds(chunk * rows, rows)]
+
+    def rs(i, arm, step, first=False):
+        here = stages[i] if first else bufs[i].at[arm, step - 1]
+        there = bufs[i].at[arm, step]
+        if first:
+            here, there = here.at[:, half(i, arm)], there.at[:, half(i, arm)]
         return remote(
-            bufs[i].at[step],
-            bufs[i].at[step + 1],
-            rs_send.at[i, step],
-            rs_recv.at[i, step],
-            peers[plan[i][4]],
-            head,
+            here, there, rs_send.at[i, arm, step], rs_recv.at[i, arm, step], peers[arm], head
         )
 
-    def ag(i, step, first=False):
-        there = block_of(i, chunk_of(plan[i][4], step - 1))
-        here = bufs[i].at[count - 1] if first else there
+    def ag(i, arm, step, kind="middle"):
+        there = block_of(i, chunk_at(-arms[arm] * step))
+        here = bufs[i].at[0, far - 1] if kind == "first" else there
+        if kind == "last":
+            here, there = here.at[:, half(i, arm)], there.at[:, half(i, arm)]
         return remote(
-            here, there, ag_send.at[i, step], ag_recv.at[i, step], peers[plan[i][4]], head
+            here, there, ag_send.at[i, arm, step], ag_recv.at[i, arm, step], peers[arm], head
         )
 
     def keep(i):
-        block = block_of(i, chunk_of(plan[i][4], count - 1))
-        return pltpu.make_async_copy(bufs[i].at[count - 1], block, keep_sem.at[i])
+        return pltpu.make_async_copy(
+            bufs[i].at[0, far - 1], block_of(i, chunk_at(0)), keep_sem.at[i]
+        )
 
     def begin(i):
-        bufs[i][0] = partial(i, chunk_of(plan[i][4], 0)).astype(BF16)
-        rs(i, 0).start()
-
-    def bounds(slot, slots, steps):
-        low = lax.div(steps * slot + slots - 1, slots)
-        return 1 + low, 1 + lax.div(steps * (slot + 1) + slots - 1, slots)
+        stages[i][...] = partial(i, chunk_at(far)).astype(BF16)
+        for arm in range(2):
+            rs(i, arm, 0, True).start()
 
     def advance(streams, slot, slots):
-        def step_of(step):
+        def second(i, arm):
+            own = partial(i, chunk_at(arms[arm] * (far - 1)))
+            rs(i, arm, 0, True).wait_recv()
+            mine, other = half(i, arm), half(i, 1 - arm)
+            bufs[i][arm, 0, :, other] = own[:, other].astype(BF16)
+            bufs[i][arm, 0, :, mine] = (
+                own[:, mine] + bufs[i][arm, 0, :, mine].astype(F32)
+            ).astype(BF16)
+            rs(i, arm, 1).start()
+
+        def later(i, arm, step):
+            own = partial(i, chunk_at(arms[arm] * (far - step)))
+            rs(i, arm, step - 1).wait_recv()
+            bufs[i][arm, step - 1] = (own + bufs[i][arm, step - 1].astype(F32)).astype(BF16)
+            rs(i, arm, step).start()
+
+        def last(i):
+            own = partial(i, chunk_at(0))
+            for arm in range(2):
+                rs(i, arm, far - 1).wait_recv()
+                own = own + bufs[i][arm, far - 1].astype(F32)
+            bufs[i][0, far - 1] = own.astype(BF16)
+            for arm in range(2):
+                ag(i, arm, 0, "first").start()
+            keep(i).start()
+
+        low, high = slot * far // slots, (slot + 1) * far // slots
+        if low == 0 < high:
             for i in streams:
-                own = partial(i, chunk_of(plan[i][4], step))
-                rs(i, step - 1).wait_recv()
-                bufs[i][step] = (own + bufs[i][step].astype(F32)).astype(BF16)
-
-                @pl.when(step < count - 1)
-                def _():
-                    rs(i, step).start()
-
-                @pl.when(step == count - 1)
-                def _():
-                    ag(i, 0, True).start()
-                    keep(i).start()
-
-        loop(*bounds(slot, slots, count - 1), step_of)
+                for arm in range(2):
+                    second(i, arm)
+
+        def middle(step):
+            for i in streams:
+                for arm in range(2):
+                    later(i, arm, step)
+
+        if min(high, far - 1) > max(low, 1):
+            loop(max(low, 1) + 1, min(high, far - 1) + 1, middle)
+        if high == far:
+            for i in streams:
+                last(i)
 
     def pass_on(streams, slot, slots):
-        def step_of(step):
+        def middle(step):
             for i in streams:
-                ag(i, step - 1).wait_recv()
-                ag(i, step).start()
-
-        loop(*bounds(slot, slots, count - 2), step_of)
+                for arm in range(2):
+                    ag(i, arm, step - 1).wait_recv()
+                    ag(i, arm, step).start()
+
+        steps = far - 1
+        low, high = slot * steps // slots, (slot + 1) * steps // slots
+        if min(high, steps - 1) > low:
+            loop(low + 1, min(high, steps - 1) + 1, middle)
+        if low < high == steps:
+            for i in streams:
+                for arm in range(2):
+                    ag(i, arm, steps - 1).wait_recv()
+                    ag(i, arm, steps, "last").start()
 
     def pass_end(streams):
         for i in streams:
-            ag(i, count - 2).wait_recv()
+            for arm in range(2):
+                ag(i, arm, far - 1, "last").wait_recv()
 
     def drain(streams):
+        for i in streams:
+            for arm in range(2):
+                rs(i, arm, 0, True).wait_send()
+                ag(i, arm, 0, "first").wait_send()
+                ag(i, arm, far - 1, "last").wait_send()
+            keep(i).wait()
+
         def one(step):
             for i in streams:
-                rs(i, step).wait_send()
-                ag(i, step).wait_send()
-
-        loop(0, count - 1, one)
-        for i in streams:
-            keep(i).wait()
+                for arm in range(2):
+                    rs(i, arm, step).wait_send()
+
+                    @pl.when(step < far - 1)
+                    def _():
+                        ag(i, arm, step).wait_send()
+
+        loop(1, far, one)
 
     return begin, advance, pass_on, pass_end, drain
 
 
-def finish_kernel(gr, gl, xr, xl, wr, wl, gin_ref, wout_ref, small_ref):
-    ihalf, half = gr.shape[1], wr.shape[1]
-    gin_ref[:, 0, 0:ihalf] = gr[...].astype(F32)
-    gin_ref[:, 0, ihalf:] = gl[...].astype(F32)
-    gin_ref[:, 1, 0:ihalf] = xr[...].astype(F32)
-    gin_ref[:, 1, ihalf:] = xl[:, 0:ihalf].astype(F32)
-    small_ref[...] = xl[:, ihalf:].astype(F32).T
-    wout_ref[:, 0:half] = wr[...].astype(F32)
-    wout_ref[:, half:] = wl[...].astype(F32)
+def finish_kernel(gate, narrow, out, gin_ref, wout_ref, small_ref):
+    inner = gate.shape[1]
+    gin_ref[:, 0, :] = gate[...].astype(F32)
+    gin_ref[:, 1, :] = narrow[:, 0:inner].astype(F32)
+    small_ref[...] = narrow[:, inner:].astype(F32).T
+    wout_ref[...] = out[...].astype(F32)
 
 
 def finish_weights(width, inner, streams):
     steps = width // (2 * LANES)
     tall, low = width // steps, inner // steps
-    wr, wl, gr, gl, xr, xl = streams
+    out, gate, narrow = streams
 
     def block(array_in, rows):
         return pl.BlockSpec((rows, array_in.shape[1]), lambda i: (i, 0))
@@ -688,7 +836,7 @@
     return pl.pallas_call(
         finish_kernel,
         grid=(steps,),
-        in_specs=[block(a, tall) for a in (gr, gl, xr, xl)] + [block(a, low) for a in (wr, wl)],
+        in_specs=[block(gate, tall), block(narrow, tall), block(out, low)],
         out_specs=[
             pl.BlockSpec((tall, 2, inner), lambda i: (i, 0, 0)),
             pl.BlockSpec((low, width), lambda i: (i, 0)),
@@ -701,32 +849,35 @@
         ],
         compiler_params=pltpu.CompilerParams(vmem_limit_bytes=VMEM_LIMIT),
         name="finish_weights",
-    )(gr, gl, xr, xl, wr, wl)
+    )(gate, narrow, out)
+
+
+STEPS = 4
 
 
 def backward_kernel(
     dims,
     dy_ref,
-    xact_ref,
+    xact_far,
     bc_ref,
     conv_ref,
     convbc_ref,
     dt_ref,
     cum_ref,
-    states_ref,
+    states_far,
     dyy_ref,
     decay_ref,
-    x_ref,
+    x_far,
     small_ref,
     chan_ref,
     vec_ref,
-    pack_ref,
+    pack_far,
     gather_ref,
-    normed_t_ref,
-    ng_t_ref,
-    cot_ref,
-    dgate_ref,
-    small_weight_ref,
+    normed_t_far,
+    ng_t_far,
+    cot_far,
+    dgate_far,
+    small_weight_far,
     sums_ref,
     gain_ref,
     row_scale_ref,
@@ -735,9 +886,12 @@
     *rest,
 ):
     count, parts, seqs, block, inner, heads, state = dims
-    outs, rest = rest[:6], rest[6:]
+    outs, rest = rest[:3], rest[3:]
     grad_ref, total_ref, *rest = rest
-    bufs, rest = rest[:6], rest[6:]
+    bufs, rest = rest[:3], rest[3:]
+    stages, rest = rest[:3], rest[3:]
+    fetched, rest = rest[:7], rest[7:]
+    fetch_sem, *rest = rest
     (
         dx_ref,
         gx_ref,
@@ -745,6 +899,7 @@
         gdt_ref,
         weights,
         conv_buf,
+        state_buf,
         dn_out,
         dn_in,
         token_buf,
@@ -757,6 +912,8 @@
         keep_sem,
         weight_sem,
         conv_sem,
+        state_sem,
+        x_sem,
         token_sem,
         dn_send,
         dn_recv,
@@ -788,27 +945,46 @@
         back_send,
         back_recv,
     ) = rest
+    sources = (
+        ng_t_far,
+        cot_far,
+        normed_t_far,
+        dgate_far,
+        xact_far,
+        small_weight_far,
+        pack_far,
+    )
+    fetches = [
+        pltpu.make_async_copy(src, dst, fetch_sem.at[k])
+        for k, (src, dst) in enumerate(zip(sources, fetched))
+    ]
+    for copy in fetches:
+        copy.start()
+    (
+        ng_t_ref,
+        cot_ref,
+        normed_t_ref,
+        dgate_ref,
+        xact_ref,
+        small_weight_ref,
+        pack_ref,
+    ) = fetched
     place, head = lax.axis_index("seq"), lax.axis_index("head")
-    rank = ring_place(count)
     chunks = block // CHUNK
     pairs = heads // 2
     total = seqs * chunks
     rows_all = seqs * block
     width = cot_ref.shape[1]
     cols = width // parts
-    half, ihalf = width // 2, inner // 2
     plan = (
-        (ng_t_ref, cot_ref, 0, half, 1),
-        (ng_t_ref, cot_ref, half, half, -1),
-        (normed_t_ref, dgate_ref, 0, ihalf, 1),
-        (normed_t_ref, dgate_ref, ihalf, ihalf, -1),
-        (normed_t_ref, dx_ref, 0, ihalf, 1),
-        (normed_t_ref, dx_ref, ihalf, ihalf + LANES, -1),
+        (ng_t_ref, cot_ref, width, width // 2),
+        (normed_t_ref, dgate_ref, inner, inner // 2),
+        (normed_t_ref, dx_ref, inner + LANES, inner // 2),
     )
     begin, advance, pass_on, pass_end, drain = ring_steps(
-        count, plan, outs, bufs, (rs_send, rs_recv, ag_send, ag_recv, keep_sem)
-    )
-    out_streams, gate_streams, x_streams = (0, 1), (2, 3), (4, 5)
+        count, plan, outs, bufs, stages, (rs_send, rs_recv, ag_send, ag_recv, keep_sem)
+    )
+    out, gate, late = (0,), (1,), (2,)
     meet(count, parts)
     gdt_ref[...] = jnp.zeros_like(gdt_ref)
 
@@ -832,9 +1008,17 @@
             conv_ref.at[ds(t * CHUNK, CHUNK)], conv_buf.at[slot], conv_sem.at[slot]
         )
 
+    def state_copy(q):
+        t = q // chunks * chunks + chunks - 1 - lax.rem(q, chunks)
+        slot = lax.rem(q, 2)
+        return pltpu.make_async_copy(states_far.at[t], state_buf.at[slot], state_sem.at[slot])
+
     conv_copy(0).start()
+    state_copy(0).start()
     weight_copy(1).start()
-    for i in out_streams + gate_streams:
+    for copy in fetches[:4]:
+        copy.wait()
+    for i in out + gate:
         begin(i)
 
     for s in range(seqs):
@@ -869,13 +1053,16 @@
         (st_send, st_recv, back_send, back_recv),
         True,
     )
-    first = out_streams + gate_streams
-    slots = 2 + total
     start()
-    advance(first, 0, slots)
+    advance(out, 0, STEPS)
+    advance(gate, 0, STEPS)
+    advance(out, 1, STEPS)
     carry()
-    advance(first, 1, slots)
+    advance(gate, 1, STEPS)
+    for copy in fetches[4:]:
+        copy.wait()
     finish()
+    advance(out, 2, STEPS)
 
     side = iota((CHUNK, LANES), 1) < LANES // 2
     seen = iota((CHUNK, CHUNK), 0) <= iota((CHUNK, CHUNK), 1)
@@ -888,10 +1075,12 @@
             out_rows = ds((s * chunks + chunks - 1 - i) * CHUNK, CHUNK)
             turn = s * chunks + i
             conv_copy(turn).wait()
+            state_copy(turn).wait()
 
             @pl.when(turn + 1 < total)
             def _():
                 conv_copy(turn + 1).start()
+                state_copy(turn + 1).start()
 
             cum, dt = cum_ref[rows, :], dt_ref[rows, :]
             cum_t = cum.T
@@ -901,7 +1090,7 @@
             b_rows, c_rows = bc_ref[rows, 0:state], bc_ref[rows, state:]
             scores = mul(b_rows, c_rows, NT)
             low = held.astype(BF16)
-            begun = states_ref[t]
+            begun = state_buf[lax.rem(turn, 2)]
             begun_high, begun_low = halves_of(begun)
             pulled = mul(b_rows, low, NN)
             grad_scores = jnp.zeros((CHUNK, CHUNK), F32)
@@ -956,7 +1145,16 @@
             gdt_ref[0:8, :] += eights(d_dt)
             gdt_ref[8:16, :] += eights(d_log * (dt * vec_ref[6:7, :]))
             ddt[out_rows, :] = d_dt
-            advance(first, 2 + s * chunks + i, slots)
+
+
+            @pl.when(turn == total * 3 // 8)
+            def _():
+                advance(gate, 2, STEPS)
+
+            @pl.when(turn == total * 6 // 8)
+            def _():
+                advance(out, 3, STEPS)
+
             return fall * held + added[t]
 
         lax.fori_loop(0, chunks, chunk, incoming[s].astype(F32))
@@ -968,6 +1166,14 @@
     def pack_one(k):
         bc_out[k] = pack(k)
 
+    def x_copy(t):
+        slot = lax.rem(t, 2)
+        return pltpu.make_async_copy(
+            x_far.at[ds(t * CHUNK, CHUNK)], conv_buf.at[slot], x_sem.at[slot]
+        )
+
+    x_copy(0).start()
+    advance(gate, 3, STEPS)
     loop(0, parts, pack_one)
     share = head_copy(parts, lambda k: bc_out.at[k], lambda k: bc_in.at[k], bc_send, bc_recv)
     loop(1, parts, lambda i: share(i).start())
@@ -999,6 +1205,7 @@
         for s in range(seqs):
             edge_copy(s).start()
 
+    pass_on(out, 0, 3)
     loop(1, parts, lambda i: share(i).wait())
     bc_in[head] = bc_out[head]
     d_act = bc_in[0].astype(F32)
@@ -1027,9 +1234,15 @@
     def x_chunk(t):
         rows = ds(t * CHUNK, CHUNK)
         s, c = t // chunks, lax.rem(t, chunks)
+        x_copy(t).wait()
+
+        @pl.when(t + 1 < total)
+        def _():
+            x_copy(t + 1).start()
+
         for p in range(pairs):
             lane = slice(p * LANES, (p + 1) * LANES)
-            x = x_ref[rows, lane]
+            x = conv_buf[lax.rem(t, 2), :, lane]
             pre = jnp.zeros((CHUNK, LANES), F32)
             here = dconv[s, pl.ds(pl.multiple_of(c * CHUNK, CHUNK), CHUNK + 8), lane]
             for k in range(KER):
@@ -1040,7 +1253,10 @@
                 if k == KER - 1:
                     gx_ref[8 * KER : 8 * KER + 8, lane] += eights(d)
             dx_ref[rows, lane] = pre.astype(BF16)
-        pass_on(out_streams, t, 2 * total)
+
+        @pl.when(t == total // 2)
+        def _():
+            pass_on(gate, 0, 3)
 
     loop(0, total, x_chunk)
 
@@ -1069,7 +1285,7 @@
         step = jnp.where(at < heads, ddt[rows, :], 0.0)
         dx_ref[rows, inner:] = jnp.where(at < LANES // 2, step, mine).astype(BF16)
 
-    for i in x_streams:
+    for i in late:
         begin(i)
 
     tall = 2 * CHUNK
@@ -1077,15 +1293,13 @@
     def dn_copy(i):
         other = lax.rem(head + i, parts)
         return remote(
-            dn_out.at[other], dn_in.at[head], dn_send.at[i], dn_recv.at[i], place, other
+            dn_out.at[other], dn_in.at[i - 1], dn_send.at[i], dn_recv.at[i], place, other
         )
 
     def d_normed(i):
         other = lax.rem(head + i, parts)
-        slot = lax.rem(i + 1, 2)
-
-        @pl.when(i < parts)
-        def _():
+        slot = (i + 1) % 2
+        if i < parts:
             weight_copy(i + 1).start()
 
         weight_copy(i).wait()
@@ -1100,30 +1314,26 @@
 
         loop(0, rows_all // tall, some)
 
-        @pl.when(i < parts)
-        def _():
+        if i < parts:
             dn_copy(i).start()
 
-    def d_normed_step(i):
-        d_normed(i)
-        advance(x_streams, i - 1, parts)
-        pass_on(out_streams, total + i - 1, 2 * total)
-
-    loop(1, parts + 1, d_normed_step)
-    for i in range(parts, total):
-        pass_on(out_streams, total + i, 2 * total)
-    slots = 2 * total + 2
-    pass_on(gate_streams + x_streams, 0, slots)
+    between = ((out, 1), (gate, 1), (out, 2), (gate, 2))
+    for k in range(STEPS):
+        if k < parts:
+            d_normed(k + 1)
+        advance(late, k, STEPS)
+        pass_on(*between[k], 3)
+    for k in range(STEPS, parts):
+        d_normed(k + 1)
 
     loop(1, parts, lambda i: dn_copy(i).wait())
-    dn_in[head] = dn_out[head]
     token_copy.wait()
     my_cols = pl.ds(pl.multiple_of(head * cols, cols), cols)
 
     def own(t, grads):
         rows = ds(t * CHUNK, CHUNK)
-        d = dn_in[0, rows, :].astype(F32)
-        for k in range(1, parts):
+        d = dn_out[head, rows, :].astype(F32)
+        for k in range(parts - 1):
             d = d + dn_in[k, rows, :].astype(F32)
         token = token_buf[rows, :].astype(F32)
         grads = grads + eights(d * (token * row_scale_ref[rows, :]))
@@ -1132,7 +1342,6 @@
         line = jnp.sum(d * token, axis=1, keepdims=True)
         line = jnp.where(iota((CHUNK, LANES), 1) == 0, line, 0.0)
         rowsum[head, t] = line.T[0:8, :]
-        pass_on(gate_streams + x_streams, 1 + t, slots)
         return grads
 
     norm_grads = lax.fori_loop(0, total, own, jnp.zeros((8, cols), F32))
@@ -1156,7 +1365,7 @@
         count, lambda _: shared.at[place], lambda k: shared.at[k], sum_send, sum_recv
     )
     loop(1, count, lambda i: sums_copy(i).start())
-    pass_on(gate_streams + x_streams, 1 + total, slots)
+    pass_on(late, 0, 3)
     loop(1, parts, lambda i: rows_copy(i).wait())
 
     def finish_rows(t):
@@ -1172,16 +1381,17 @@
             - token_buf[rows, :].astype(F32) * pull
             + cot_ref[rows, my_cols].astype(F32)
         )
-        pass_on(gate_streams + x_streams, 2 + total + t, slots)
 
     loop(0, total, finish_rows)
+    pass_on(late, 1, 3)
     loop(1, count, lambda i: sums_copy(i).wait())
     everything = shared[0]
     for k in range(1, count):
         everything = everything + shared[k]
     total_ref[...] = everything
-    pass_end(out_streams + gate_streams + x_streams)
-    drain(out_streams + gate_streams + x_streams)
+    pass_on(late, 2, 3)
+    pass_end(out + gate + late)
+    drain(out + gate + late)
 
     @pl.when(place > 0)
     def _():
@@ -1197,37 +1407,35 @@
     cut_rows, _, cut_lanes = cut_of(count, seqs, state, inner)
     normed_rows, ng_rows, width = (operands[k].shape[d] for k, d in ((16, 0), (17, 0), (18, 1)))
     cols = width // parts
+    distant = (1, 3, 7, 10, 14, 16, 17, 18, 19, 20, 24, 25)
+    fetched = [operands[k] for k in (17, 18, 16, 19, 1, 20, 14)]
     spec = pl.BlockSpec(memory_space=pltpu.VMEM)
     far = pl.BlockSpec(memory_space=pl.ANY)
     line, ring = pltpu.SemaphoreType.DMA((count,)), pltpu.SemaphoreType.DMA((parts,))
     edge = pltpu.SemaphoreType.DMA((seqs + 1,))
-    half, ihalf = width // 2, inner // 2
-    streams = [
-        (ng_rows, half),
-        (ng_rows, half),
-        (normed_rows, ihalf),
-        (normed_rows, ihalf),
-        (normed_rows, ihalf),
-        (normed_rows, ihalf + LANES),
-    ]
-    steps = pltpu.SemaphoreType.DMA((len(streams), count))
+    streams = [(ng_rows, width), (normed_rows, inner), (normed_rows, inner + LANES)]
+    steps = pltpu.SemaphoreType.DMA((len(streams), 2, count // 2))
     outs = [(shape, BF16) for shape in streams]
     outs = outs + [((rows, cols), F32), ((8, inner + LANES), F32)]
     return pl.pallas_call(
         functools.partial(backward_kernel, dims),
         out_shape=[jax.ShapeDtypeStruct(*o) for o in outs],
-        in_specs=[spec] * 3 + [far] + [spec] * (len(operands) - 6) + [far] * 2,
+        in_specs=[far if k in distant else spec for k in range(len(operands))],
         out_specs=[far] * len(streams) + [spec] * 2,
-        scratch_shapes=[vmem((count, r // count, c), BF16) for r, c in streams]
+        scratch_shapes=[vmem((2, count // 2, r // count, c), BF16) for r, c in streams]
+        + [vmem((r // count, c), BF16) for r, c in streams]
+        + [vmem(a.shape, a.dtype) for a in fetched]
         + [
+            pltpu.SemaphoreType.DMA((len(fetched),)),
             vmem((rows, inner + LANES), BF16),
             vmem((8 * (KER + 1), inner), F32),
             vmem((8 * (KER + 1), LANES), F32),
             vmem((16, LANES), F32),
             vmem((2, 2, cols, inner), BF16),
             vmem((2, CHUNK, inner), F32),
+            vmem((2, state, inner), F32),
             vmem((parts, rows, cols), BF16),
-            vmem((parts, rows, cols), BF16),
+            vmem((parts - 1, rows, cols), BF16),
             vmem((rows, cols), BF16),
             vmem((parts, chunks, 8, LANES), F32),
             vmem((count, 8, inner + LANES), F32),
@@ -1236,6 +1444,8 @@
             steps,
             steps,
             pltpu.SemaphoreType.DMA((len(streams),)),
+            pltpu.SemaphoreType.DMA((2,)),
+            pltpu.SemaphoreType.DMA((2,)),
             pltpu.SemaphoreType.DMA((2,)),
             pltpu.SemaphoreType.DMA((2,)),
             pltpu.SemaphoreType.DMA,
@@ -1302,13 +1512,7 @@
     half = LANES // 2
     dims = (count, parts, seqs, block, inner, heads, state)
 
-    input_batch = tokens.astype(F32).reshape(rows, width)
-    row_scale = lax.rsqrt(jnp.mean(input_batch * input_batch, axis=-1, keepdims=True) + EPSILON)
-    normed = (input_batch * row_scale * norm_gain).astype(BF16)
-    projected = jnp.einsum(
-        "rp,pkw->krw", normed, gate_input_weight, preferred_element_type=F32
-    )
-    gate_pre, x_pre = projected[0], projected[1]
+    flat_tokens = tokens.reshape(rows, width)
     small_weight = jnp.concatenate(
         [
             step_weight,
@@ -1317,7 +1521,10 @@
         ],
         axis=1,
     )
-    small = jnp.dot(normed, small_weight, preferred_element_type=F32)
+    both_weights = gate_input_weight.transpose(1, 0, 2)
+    gate_pre, x_pre, small, normed_t, row_scale = project(
+        flat_tokens, norm_gain[None], both_weights, small_weight
+    )
 
     chan = jnp.concatenate(
         [
@@ -1338,25 +1545,25 @@
             jnp.pad(per_head, ((0, 0), (0, LANES - heads))),
         ]
     )
-    device, lane, channel = jnp.meshgrid(
-        jnp.arange(parts), jnp.arange(LANES), jnp.arange(2 * state), indexing="ij"
+    device, lane, channel = np.meshgrid(
+        np.arange(parts), np.arange(LANES), np.arange(2 * state), indexing="ij"
     )
     is_c, at = channel // state, channel % state
-    unpack = jnp.stack(
+    unpack = np.stack(
         [
             (lane == s * half + is_c * state_part + at - device * state_part)
             & (at // state_part == device)
             for s in range(seqs)
         ]
-    ).astype(BF16)
-    pack = unpack.transpose(1, 0, 3, 2)
-    unpack = unpack.reshape(seqs, parts * LANES, 2 * state)
-    expand = jnp.arange(LANES)[:, None] == jnp.arange(inner)[None, :] // (inner // heads)
-    gather = expand.T.astype(BF16)
-    expand = expand.astype(F32)
+    ).astype(np.float32)
+    pack = jnp.asarray(unpack.transpose(1, 0, 3, 2), BF16)
+    unpack = jnp.asarray(unpack.reshape(seqs, parts * LANES, 2 * state), BF16)
+    expand = np.arange(LANES)[:, None] == np.arange(inner)[None, :] // (inner // heads)
+    gather = jnp.asarray(expand.T.astype(np.float32), BF16)
+    expand = jnp.asarray(expand.astype(np.float32))
     cot = cotangent.reshape(rows, width)
 
-    xact, bc, conv, convbc, dt, cum, states, ng, dgate, dy, dyy, decay, sums = forward(
+    xact, bc, conv, convbc, dt, cum, states, ng_t, dgate, dy, dyy, decay, sums = forward(
         dims,
         x_pre,
         gate_pre,
@@ -1372,12 +1579,12 @@
     def padded(array_in):
         return jnp.pad(array_in, ((0, -array_in.shape[0] % (count * 16)), (0, 0)))
 
-    mixer = jnp.dot(ng, output_weight, preferred_element_type=F32)
+    mixer = mul(ng_t, output_weight, TN)
     mixed = lax.psum_scatter(
         mixer.astype(BF16), "head", scatter_dimension=1, tiled=True
     ).astype(F32)
-    own_inputs = lax.dynamic_slice_in_dim(input_batch, my_head * col_count, col_count, 1)
-    block_out = (own_inputs + mixed).astype(BF16)
+    own_inputs = lax.dynamic_slice_in_dim(flat_tokens, my_head * col_count, col_count, 1)
+    block_out = (own_inputs.astype(F32) + mixed).astype(BF16)
 
     *streams, grad_input, sums = backward(
         dims,
@@ -1397,16 +1604,16 @@
         vec,
         pack,
         gather,
-        padded(normed.T),
-        padded(ng.T),
+        padded(normed_t),
+        padded(ng_t),
         cot,
         dgate,
         small_weight,
         sums,
         norm_gain[None],
         row_scale,
-        tokens.reshape(rows, width),
-        gate_input_weight.transpose(1, 0, 2),
+        flat_tokens,
+        both_weights,
     )
     g_in, g_w_out, g_small = finish_weights(width, inner, streams)
     taps = sums[:, :inner]

time: 387 us -> 328 us (0.85); the launches traced: 386 us -> 322 us
  other arithmetic: 24.7 us -> 4.66 us
  Pallas kernels: 298 us -> 278 us
  local copies, waits for them, and re-layouts: 32.5 us -> 20.1 us
  matrix products: 16.1 us -> 4.8 us
    pallas_call x1, Pallas kernels: 214 us -> 188 us  [backward(): pl.pallas_call(functools.partial(backward_kernel, dims), out_shape=[jax.S...]
    dot_general x3 -> x1, matrix products: 16.1 us -> 4.8 us  [mul(): lax.dot_general(left, right, (how, ((), ())), precision=precision, prefer...]
    pallas_call x1 -> x2, Pallas kernels: 9.85 us -> 20.3 us  [the longest x1 10.8 us: project(): pl.pallas_call(project_kernel, grid=(rows // tall,), in_specs=[by_rows(wi...]
    transpose x2 -> x0, other arithmetic: 6.48 us -> none  [the longest x1 5.56 us: body(): *streams, grad_input, sums = backward(dims, dy, xact, bc, conv, convbc, d...]
    convert_element_type x5 -> x1, other arithmetic: 7.8 us -> 2.22 us  [body(): block_out = (own_inputs.astype(F32) + mixed).astype(BF16)]
    pallas_call x1, Pallas kernels: 74.4 us -> 69.5 us  [forward(): pl.pallas_call(functools.partial(forward_kernel, dims), out_shape=[jax.Sh...]
    unnamed x45 -> x31, local copies, waits for them, and re-layouts: 11 us -> 11 us
  transfers between devices with their start and end apart: 1 -> 1, of which waited for: 0 -> 0; matrix products, arithmetic and copies ran while one was open for 6% -> 2% of each run, Pallas kernels for 58% -> 61%
where the time goes in v4:
time: 328 us; the launch traced here: 322 us
  Pallas kernels  278 us (85%)
  local copies, waits for them, and re-layouts  20.1 us (6%)
  between operations  14.5 us (4%)
  matrix products  4.8 us (1%)
  other arithmetic  4.66 us (1%)
    pallas_call x1, Pallas kernels, backward(): pl.pallas_call(functools.partial(backward_kernel, dims), out_shape=[jax.S...  188 us
    pallas_call x1, Pallas kernels, forward(): pl.pallas_call(functools.partial(forward_kernel, dims), out_shape=[jax.Sh...  69.5 us
    unnamed x31, local copies, waits for them, and re-layouts  11 us
    pallas_call x1, Pallas kernels, project(): pl.pallas_call(project_kernel, grid=(rows // tall,), in_specs=[by_rows(wi...  10.8 us
    pallas_call x1, Pallas kernels, finish_weights(): pl.pallas_call(finish_kernel, grid=(steps,), in_specs=[block(gate, tall),...  9.49 us
  transfers between devices with their start and end apart: 1, of which 0 were waited for; matrix products, arithmetic and copies ran while one was open for 2% of the time, Pallas kernels for 61%

profile of v4, /device:TPU:0, one launch (start us, length us, event | category | flops | bytes accessed | tf_op | source)
XLA Modules:
  0.0 322.1 jit_solution(16536684914408663086)
XLA Ops:
  7.2 0.0 copy-start.2
  7.2 0.0 copy-start.1
  7.2 0.0 copy-start.5
  7.2 0.0 copy-start.9
  7.2 0.0 copy-start.6
  7.2 0.0 copy-start.7
  7.2 0.0 copy-start.12
  7.3 0.0 copy-start.8
  7.3 0.0 copy-start.11
  7.3 0.0 copy-start.10
  7.3 0.0 reduce-scatter.4.cloned.1.call-start
  7.3 5.2 %copy.46 = bf16[1536,2,768]{2,0,1:T(8,128)(2,1)} copy(bf16[1536,2,768]{2,1,0:T(2,128)(2,1)} %param.21) | data formatting | bytes 9437184 | tf_op args[2]
  12.5 0.2 copy.41
  12.8 0.2 copy.42
  13.0 0.6 broadcast_in_dim.19.gain_ref
  13.6 0.1 broadcast_in_dim.23
  13.7 0.1 broadcast_in_dim_reshape.3
  13.9 0.1 reshape.60
  13.9 0.0 copy-done.11
  13.9 0.1 reshape.61
  14.0 0.1 pad.14.clone
  14.1 0.1 pad.12.clone
  14.2 1.0 pad_maximum_fusion.small_weight_ref.small_weight_far
  15.2 0.1 maximum_maximum_fusion
  15.2 0.7 select_maximum_fusion.vec_ref
  15.9 10.8 %project.1 = (f32[1024,768]{1,0:T(8,128)}, f32[1024,768]{1,0:T(8,128)}, f32[1024,128]{1,0:T(8,128)}, bf16[1536,1024]{1,0:T(8,128)(2,1)}, f32[1024,1]{1,0:T(8,128)}) custom-call(bf16[1024,1536]{1,0:T(8,128)(2,1)} %bitcast.27, f32[1,1536]{1,0:T(1,128)} %broadcast_in_dim.19.gain_ref, bf16[2,1536,768]{2,1,0:T(8,128)(2,1)} %bitcast.25, ...), custom_call_target="tpu_custom_call" | custom-call | tf_op jit(solution)/shard_map/project/pallas_call | solution.py:647
  26.7 0.6 concatenate.16.chan_ref
  27.3 69.5 %mixer_forward.1 = (bf16[1024,768]{1,0:T(8,128)(2,1)}, bf16[1024,256]{1,0:T(8,128)(2,1)}, f32[1024,768]{1,0:T(8,128)}, f32[512,128]{1,0:T(8,128)}, f32[1024,128]...) custom-call(f32[1024,768]{1,0:T(8,128)} %get-tuple-element.41.x_ref., ...), custom_call_target="tpu_custom_call" | custom-call | tf_op jit(solution)/shard_map/mixer_forward/pallas_call | solution.py:577
  96.8 4.8 %convolution_convert_fusion = bf16[1024,1536]{1,0:T(8,128)(2,1)S(1)} fusion(bf16[768,1024]{1,0:T(8,128)(2,1)} %get-tuple-element.44.ng_t_far, bf16[768,1536]{1,0:T(8,128)(2,1)} %wout_far.1), kind=kOutput, calls=%fused_computation.1 | convolution fusion | flops 2417491968 | bytes 7077888 | tf_op jit(solution)/shard_map/dot_general | solution.py:26
  101.6 2.9 copy.43
  104.5 0.0 reduce-scatter.4.cloned.1.call-update
  104.5 188.2 %mixer_backward.1 = (bf16[768,1536]{1,0:T(8,128)(2,1)}, bf16[1536,768]{1,0:T(8,128)(2,1)}, bf16[1536,896]{1,0:T(8,128)(2,1)}, f32[1024,384]{1,0:T(8,128)}, f32[8,896]{1,0:T(8,128)}) custom-call(bf16[1024,768]{1,0:T(8,128)(2,1)} %get-tuple-element.45.dy_ref, bf16[1024,768]{1,0:T(8,128)(2,1)} %get-tuple-element.46.xact_far, ...), custom_call_target="tpu_custom_call" | custom-call | tf_op jit(solution)/shard_map/mixer_backward/pallas_call | solution.py:1420
  292.8 0.0 copy-start.3
  292.8 9.5 %finish_weights.1 = (f32[1536,2,768]{2,1,0:T(2,128)}, f32[768,1536]{1,0:T(8,128)}, f32[128,1536]{1,0:T(8,128)}) custom-call(bf16[1536,768]{1,0:T(8,128)(2,1)} %get-tuple-element.61.gate, bf16[1536,896]{1,0:T(8,128)(2,1)} %get-tuple-element.62.narrow, bf16[768,1536]{1,0:T(8,128)(2,1)} %get-tuple-element.63.out), custom_call_target="tpu_custom_call" | custom-call | tf_op jit(solution)/shard_map/finish_weights/pallas_call | solution.py:836
  302.3 1.9 slice.55
  304.2 0.6 slice.57
  304.8 0.6 slice_reduce_fusion
  305.4 0.1 reshape_squeeze.3
  305.4 0.6 reduce_sum.9
  306.1 0.1 slice_add_fusion
  306.2 0.7 slice.61
  306.9 0.6 squeeze.20
  307.5 0.6 slice_reduce_fusion.3
  308.1 0.5 slice_bitcast_fusion.1
  308.6 1.5 slice_bitcast_fusion
  310.2 1.5 copy.44
  311.6 2.2 add_convert_fusion
  313.9 1.1 copy.48
  (22 shorter events, 0.1 us)
Async XLA Ops:
  7.2 5.4 %copy-start.2 = (bf16[1536,12]{0,1:T(8,128)(2,1)S(1)}, bf16[1536,12]{0,1:T(8,128)(2,1)}, u32[]{:S(2)}) copy-start(bf16[1536,12]{0,1:T(8,128)(2,1)} %param.23) | copy-start | bytes 110596
  7.2 5.6 %copy-start.1 = (bf16[1536,2,32]{0,2,1:T(8,128)(2,1)S(1)}, bf16[1536,2,32]{0,2,1:T(8,128)(2,1)}, u32[]{:S(2)}) copy-start(bf16[1536,2,32]{0,2,1:T(8,128)(2,1)} %param.22) | copy-start | bytes 589828
  7.2 5.8 %copy-start.5 = (f32[1536]{0:T(1024)S(1)}, f32[1536]{0:T(1024)}, u32[]{:S(2)}) copy-start(f32[1536]{0:T(1024)} %param.20) | copy-start | bytes 18436
  7.2 6.4 %copy-start.9 = (f32[12]{0:T(128)S(1)}, f32[12]{0:T(128)}, u32[]{:S(2)}) copy-start(f32[12]{0:T(128)} %param.30) | copy-start | bytes 148
  7.2 6.6 %copy-start.6 = (f32[768]{0:T(1024)S(1)}, f32[768]{0:T(1024)}, u32[]{:S(2)}) copy-start(f32[768]{0:T(1024)} %param.26) | copy-start | bytes 9220
  7.2 6.6 %copy-start.7 = (f32[768]{0:T(1024)S(1)}, f32[768]{0:T(1024)}, u32[]{:S(2)}) copy-start(f32[768]{0:T(1024)} %param.31) | copy-start | bytes 9220
  7.2 6.6 %copy-start.12 = (f32[12]{0:T(128)S(1)}, f32[12]{0:T(128)}, u32[]{:S(2)}) copy-start(f32[12]{0:T(128)} %param.29) | copy-start | bytes 148
  7.3 6.6 %copy-start.8 = (f32[4,2,32]{2,1,0:T(2,128)S(1)}, f32[4,2,32]{2,1,0:T(2,128)}, u32[]{:S(2)}) copy-start(f32[4,2,32]{2,1,0:T(2,128)} %param.25) | copy-start | bytes 3076
  7.3 6.7 %copy-start.11 = (f32[2,32]{1,0:T(2,128)S(1)}, f32[2,32]{1,0:T(2,128)}, u32[]{:S(2)}) copy-start(f32[2,32]{1,0:T(2,128)} %param.27) | copy-start | bytes 772
  7.3 7.9 %copy-start.10 = (f32[12]{0:T(128)S(1)}, f32[12]{0:T(128)}, u32[]{:S(2)}) copy-start(f32[12]{0:T(128)} %param.28) | copy-start | bytes 148
  7.3 302.9 %reduce-scatter.4.cloned.1.call-start = ((), (), s32[]{:S(2)}) async-start(), calls=%async_computation.1 | async-start | bytes 3932160
  15.9 10.8 %copy-start.4 = (f32[4,768]{1,0:T(4,128)S(1)}, f32[4,768]{1,0:T(4,128)}, u32[]{:S(2)}) copy-start(f32[4,768]{1,0:T(4,128)} %param.24) | copy-start | bytes 36868
  292.8 11.4 %copy-start.3 = (f32[8,896]{1,0:T(8,128)S(1)}, f32[8,896]{1,0:T(8,128)}, u32[]{:S(2)}) copy-start(f32[8,896]{1,0:T(8,128)} %get-tuple-element.60) | copy-start | bytes 86020
  302.3 11.6 %copy-start = (f32[1024,384]{1,0:T(8,128)S(1)}, f32[1024,384]{1,0:T(8,128)}, u32[]{:S(2)}) copy-start(f32[1024,384]{1,0:T(8,128)} %get-tuple-element.59) | copy-start | bytes 4718596
Sparse Core Ops, SparseCore 0:
  104.7 45.2 reduce-scatter.3

commit v5 on v4

--- a/solution.py
+++ b/solution.py
@@ -16,7 +16,7 @@
 F32 = jnp.float32
 BF16 = jnp.bfloat16
 EXACT = lax.Precision.HIGHEST
-VMEM_LIMIT = 60 * 2**20
+VMEM_LIMIT = 61 * 2**20
 NN = ((1,), (0,))
 NT = ((1,), (1,))
 TN = ((0,), (0,))
@@ -689,12 +689,12 @@
         return lax.rem(rank + distance + 2 * count, count)
 
     def partial(i, chunk):
-        left, right, cols, _ = plan[i]
+        left, right, first, cols, _ = plan[i]
         rows = left.shape[0] // count
-        return mul(left[ds(chunk * rows, rows), :], right[:, 0:cols], NN)
+        return mul(left[ds(chunk * rows, rows), :], right[:, first : first + cols], NN)
 
     def half(i, arm):
-        cols, cut = plan[i][2:]
+        cols, cut = plan[i][3:]
         return slice(0, cut) if arm == 0 else slice(cut, cols)
 
     def block_of(i, chunk):
@@ -817,39 +817,114 @@
     return begin, advance, pass_on, pass_end, drain
 
 
-def finish_kernel(gate, narrow, out, gin_ref, wout_ref, small_ref):
-    inner = gate.shape[1]
+def finish_kernel(
+    gate,
+    narrow_low,
+    narrow,
+    out,
+    sums_ref,
+    gather_ref,
+    block_far,
+    input_far,
+    gin_ref,
+    wout_ref,
+    coef_ref,
+    step_ref,
+    taps_ref,
+    taps_bc_ref,
+    bias_ref,
+    bias_bc_ref,
+    dt_ref,
+    log_ref,
+    skip_ref,
+    gain_ref,
+    norm_ref,
+    block_out,
+    input_out,
+):
+    inner, half = gate.shape[1], narrow_low.shape[1]
+    heads, state_part = step_ref.shape[0], bias_bc_ref.shape[1]
+    block_out[...] = block_far[...]
+    input_out[...] = input_far[...]
+
+    @pl.when(pl.program_id(0) == 0)
+    def _():
+        lanes = sums_ref[:, inner:]
+        both = lanes + pltpu.roll(lanes, LANES // 2, 1)
+        taps_ref[...] = sums_ref[0:KER, 0:inner]
+        bias_ref[...] = sums_ref[KER : KER + 1, 0:inner]
+        gain_ref[...] = sums_ref[KER + 1 : KER + 2, 0:inner]
+        norm_ref[...] = sums_ref[KER + 3 : KER + 4, 0 : norm_ref.shape[1]]
+        for k in range(2):
+            at = slice(k * state_part, (k + 1) * state_part)
+            taps_bc_ref[:, k, :] = both[0:KER, at]
+            bias_bc_ref[k : k + 1, :] = both[KER : KER + 1, at]
+        dt_ref[...] = lanes[KER + 1 : KER + 2, 0:heads]
+        log_ref[...] = lanes[KER + 2 : KER + 3, 0:heads]
+        skip_ref[...] = head_sums(sums_ref[:, 0:inner], gather_ref[...])[KER + 2 : KER + 3, 0:heads]
+
     gin_ref[:, 0, :] = gate[...].astype(F32)
-    gin_ref[:, 1, :] = narrow[:, 0:inner].astype(F32)
-    small_ref[...] = narrow[:, inner:].astype(F32).T
+    gin_ref[:, 1, 0:half] = narrow_low[...].astype(F32)
+    gin_ref[:, 1, half:] = narrow[:, 0 : inner - half].astype(F32)
+    small = narrow[:, inner - half :].astype(F32).T
+    step_ref[...] = small[0:heads]
+    for k in range(2):
+        low = LANES // 2 + k * state_part
+        coef_ref[k] = small[low : low + state_part]
     wout_ref[...] = out[...].astype(F32)
 
 
-def finish_weights(width, inner, streams):
-    steps = width // (2 * LANES)
-    tall, low = width // steps, inner // steps
-    out, gate, narrow = streams
+def finish(width, inner, heads, state_part, streams, sums, gather, block_out, grad_input):
+    steps = 4
+    tall, low, part = width // steps, inner // steps, grad_input.shape[0] // steps
+    out, gate, narrow_low, narrow = streams
+    cols = grad_input.shape[1]
+    mine = pl.BlockSpec((part, cols), lambda i: (i, 0))
 
     def block(array_in, rows):
         return pl.BlockSpec((rows, array_in.shape[1]), lambda i: (i, 0))
 
+    def whole(shape):
+        return pl.BlockSpec(shape, lambda i: (0,) * len(shape))
+
+    little = [
+        (KER, inner),
+        (KER, 2, state_part),
+        (1, inner),
+        (2, state_part),
+        (1, heads),
+        (1, heads),
+        (1, heads),
+        (1, inner),
+        (1, cols),
+    ]
     return pl.pallas_call(
         finish_kernel,
         grid=(steps,),
-        in_specs=[block(gate, tall), block(narrow, tall), block(out, low)],
+        in_specs=[block(gate, tall), block(narrow_low, tall), block(narrow, tall), block(out, low)]
+        + [whole(sums.shape), whole(gather.shape), mine, mine],
         out_specs=[
             pl.BlockSpec((tall, 2, inner), lambda i: (i, 0, 0)),
             pl.BlockSpec((low, width), lambda i: (i, 0)),
-            pl.BlockSpec((LANES, tall), lambda i: (0, i)),
-        ],
+            pl.BlockSpec((2, state_part, tall), lambda i: (0, 0, i)),
+            pl.BlockSpec((heads, tall), lambda i: (0, i)),
+        ]
+        + [whole(s) for s in little]
+        + [mine, mine],
         out_shape=[
             jax.ShapeDtypeStruct((width, 2, inner), F32),
             jax.ShapeDtypeStruct((inner, width), F32),
-            jax.ShapeDtypeStruct((LANES, width), F32),
+            jax.ShapeDtypeStruct((2, state_part, width), F32),
+            jax.ShapeDtypeStruct((heads, width), F32),
+        ]
+        + [jax.ShapeDtypeStruct(s, F32) for s in little]
+        + [
+            jax.ShapeDtypeStruct(block_out.shape, BF16),
+            jax.ShapeDtypeStruct(grad_input.shape, F32),
         ],
         compiler_params=pltpu.CompilerParams(vmem_limit_bytes=VMEM_LIMIT),
-        name="finish_weights",
-    )(gate, narrow, out)
+        name="finish",
+    )(gate, narrow_low, narrow, out, sums, gather, block_out, grad_input)
 
 
 STEPS = 4
@@ -883,13 +958,14 @@
     row_scale_ref,
     tokens_ref,
     weight_ref,
+    wout_far,
     *rest,
 ):
     count, parts, seqs, block, inner, heads, state = dims
-    outs, rest = rest[:3], rest[3:]
-    grad_ref, total_ref, *rest = rest
-    bufs, rest = rest[:3], rest[3:]
-    stages, rest = rest[:3], rest[3:]
+    outs, rest = rest[:4], rest[4:]
+    grad_ref, total_ref, mixed_ref, *rest = rest
+    bufs, rest = rest[:4], rest[4:]
+    stages, rest = rest[:4], rest[4:]
     fetched, rest = rest[:7], rest[7:]
     fetch_sem, *rest = rest
     (
@@ -902,6 +978,8 @@
         state_buf,
         dn_out,
         dn_in,
+        wout,
+        mix_in,
         token_buf,
         rowsum,
         shared,
@@ -917,6 +995,9 @@
         token_sem,
         dn_send,
         dn_recv,
+        wout_sem,
+        mix_send,
+        mix_recv,
         row_send,
         row_recv,
         sum_send,
@@ -929,7 +1010,6 @@
         prebc,
         dbc,
         ddt,
-        added,
         local,
         arrived,
         passed,
@@ -977,14 +1057,15 @@
     width = cot_ref.shape[1]
     cols = width // parts
     plan = (
-        (ng_t_ref, cot_ref, width, width // 2),
-        (normed_t_ref, dgate_ref, inner, inner // 2),
-        (normed_t_ref, dx_ref, inner + LANES, inner // 2),
+        (ng_t_ref, cot_ref, 0, width, width // 2),
+        (normed_t_ref, dgate_ref, 0, inner, inner // 2),
+        (normed_t_ref, dx_ref, 0, inner // 2, LANES),
+        (normed_t_ref, dx_ref, inner // 2, inner // 2 + LANES, 2 * LANES),
     )
     begin, advance, pass_on, pass_end, drain = ring_steps(
         count, plan, outs, bufs, stages, (rs_send, rs_recv, ag_send, ag_recv, keep_sem)
     )
-    out, gate, late = (0,), (1,), (2,)
+    out, gate, late = (0,), (1,), (2, 3)
     meet(count, parts)
     gdt_ref[...] = jnp.zeros_like(gdt_ref)
 
@@ -1020,6 +1101,38 @@
         copy.wait()
     for i in out + gate:
         begin(i)
+
+    tall = 2 * CHUNK
+
+    def wout_copy(i):
+        other = lax.rem(head + i, parts)
+        return pltpu.make_async_copy(
+            wout_far.at[:, pl.ds(pl.multiple_of(other * cols, cols), cols)],
+            wout.at[i % 2],
+            wout_sem.at[i % 2],
+        )
+
+    def mix_copy(i):
+        other = lax.rem(head + i, parts)
+        return remote(
+            dn_out.at[other], mix_in.at[i - 1], mix_send.at[i], mix_recv.at[i], place, other
+        )
+
+    def mix(i):
+        other = lax.rem(head + i, parts)
+        if i < parts:
+            wout_copy(i + 1).start()
+        wout_copy(i).wait()
+
+        def some(r):
+            rows = ds(r * tall, tall)
+            dn_out[other, rows, :] = mul(ng_t_ref[0:inner, rows], wout[i % 2], TN).astype(BF16)
+
+        loop(0, rows_all // tall, some)
+        if i < parts:
+            mix_copy(i).start()
+
+    wout_copy(1).start()
 
     for s in range(seqs):
 
@@ -1037,7 +1150,6 @@
                 axis=1,
             )
             new = mul(bc_ref[rows, state:], weighted, TN)
-            added[t] = new
             return spread(grown[CHUNK - 1 :, :], pairs) * held + new
 
         held = lax.fori_loop(0, chunks, alone, jnp.zeros((state, inner), F32))
@@ -1055,14 +1167,19 @@
     )
     start()
     advance(out, 0, STEPS)
+    mix(1)
     advance(gate, 0, STEPS)
+    mix(2)
     advance(out, 1, STEPS)
     carry()
     advance(gate, 1, STEPS)
     for copy in fetches[4:]:
         copy.wait()
     finish()
+    mix(3)
     advance(out, 2, STEPS)
+    for i in range(4, parts + 1):
+        mix(i)
 
     side = iota((CHUNK, LANES), 1) < LANES // 2
     seen = iota((CHUNK, CHUNK), 0) <= iota((CHUNK, CHUNK), 1)
@@ -1155,7 +1272,7 @@
             def _():
                 advance(out, 3, STEPS)
 
-            return fall * held + added[t]
+            return fall * held + mul(c_rows, into_y, TN)
 
         lax.fori_loop(0, chunks, chunk, incoming[s].astype(F32))
 
@@ -1288,7 +1405,18 @@
     for i in late:
         begin(i)
 
-    tall = 2 * CHUNK
+    loop(1, parts, lambda i: mix_copy(i).wait())
+    token_copy.wait()
+
+    def add_up(t):
+        rows = ds(t * CHUNK, CHUNK)
+        d = dn_out[head, rows, :].astype(F32)
+        for k in range(parts - 1):
+            d = d + mix_in[k, rows, :].astype(F32)
+        mixed_ref[rows, :] = (token_buf[rows, :].astype(F32) + d).astype(BF16)
+
+    loop(0, total, add_up)
+
 
     def dn_copy(i):
         other = lax.rem(head + i, parts)
@@ -1327,7 +1455,6 @@
         d_normed(k + 1)
 
     loop(1, parts, lambda i: dn_copy(i).wait())
-    token_copy.wait()
     my_cols = pl.ds(pl.multiple_of(head * cols, cols), cols)
 
     def own(t, grads):
@@ -1407,21 +1534,26 @@
     cut_rows, _, cut_lanes = cut_of(count, seqs, state, inner)
     normed_rows, ng_rows, width = (operands[k].shape[d] for k, d in ((16, 0), (17, 0), (18, 1)))
     cols = width // parts
-    distant = (1, 3, 7, 10, 14, 16, 17, 18, 19, 20, 24, 25)
+    distant = (1, 3, 7, 10, 14, 16, 17, 18, 19, 20, 24, 25, 26)
     fetched = [operands[k] for k in (17, 18, 16, 19, 1, 20, 14)]
     spec = pl.BlockSpec(memory_space=pltpu.VMEM)
     far = pl.BlockSpec(memory_space=pl.ANY)
     line, ring = pltpu.SemaphoreType.DMA((count,)), pltpu.SemaphoreType.DMA((parts,))
     edge = pltpu.SemaphoreType.DMA((seqs + 1,))
-    streams = [(ng_rows, width), (normed_rows, inner), (normed_rows, inner + LANES)]
+    streams = [
+        (ng_rows, width),
+        (normed_rows, inner),
+        (normed_rows, inner // 2),
+        (normed_rows, inner // 2 + LANES),
+    ]
     steps = pltpu.SemaphoreType.DMA((len(streams), 2, count // 2))
     outs = [(shape, BF16) for shape in streams]
-    outs = outs + [((rows, cols), F32), ((8, inner + LANES), F32)]
+    outs = outs + [((rows, cols), F32), ((8, inner + LANES), F32), ((rows, cols), BF16)]
     return pl.pallas_call(
         functools.partial(backward_kernel, dims),
         out_shape=[jax.ShapeDtypeStruct(*o) for o in outs],
         in_specs=[far if k in distant else spec for k in range(len(operands))],
-        out_specs=[far] * len(streams) + [spec] * 2,
+        out_specs=[far] * len(streams) + [spec] * 3,
         scratch_shapes=[vmem((2, count // 2, r // count, c), BF16) for r, c in streams]
         + [vmem((r // count, c), BF16) for r, c in streams]
         + [vmem(a.shape, a.dtype) for a in fetched]
@@ -1435,6 +1567,8 @@
             vmem((2, CHUNK, inner), F32),
             vmem((2, state, inner), F32),
             vmem((parts, rows, cols), BF16),
+            vmem((parts - 1, rows, cols), BF16),
+            vmem((2, inner, cols), BF16),
             vmem((parts - 1, rows, cols), BF16),
             vmem((rows, cols), BF16),
             vmem((parts, chunks, 8, LANES), F32),
@@ -1451,6 +1585,9 @@
             pltpu.SemaphoreType.DMA,
             ring,
             ring,
+            pltpu.SemaphoreType.DMA((2,)),
+            ring,
+            ring,
             ring,
             ring,
             line,
@@ -1460,7 +1597,6 @@
             vmem((block, LANES), F32),
             vmem((rows, 2 * state), BF16),
             vmem((rows, LANES), F32),
-            vmem((chunks, state, inner), F32),
             vmem((seqs, state, inner), BF16),
             vmem((count, cut_rows, cut_lanes), BF16),
             vmem((count, cut_rows, cut_lanes), BF16),
@@ -1505,7 +1641,6 @@
     state_part = coefficient_weight.shape[2]
     heads = step_weight.shape[1]
     count, parts = lax.axis_size("seq"), lax.axis_size("head")
-    my_head = lax.axis_index("head")
     state = state_part * parts
     rows = seqs * block
     col_count = width // parts
@@ -1579,14 +1714,7 @@
     def padded(array_in):
         return jnp.pad(array_in, ((0, -array_in.shape[0] % (count * 16)), (0, 0)))
 
-    mixer = mul(ng_t, output_weight, TN)
-    mixed = lax.psum_scatter(
-        mixer.astype(BF16), "head", scatter_dimension=1, tiled=True
-    ).astype(F32)
-    own_inputs = lax.dynamic_slice_in_dim(flat_tokens, my_head * col_count, col_count, 1)
-    block_out = (own_inputs.astype(F32) + mixed).astype(BF16)
-
-    *streams, grad_input, sums = backward(
+    *streams, grad_input, sums, block_out = backward(
         dims,
         dy,
         xact,
@@ -1614,26 +1742,42 @@
         row_scale,
         flat_tokens,
         both_weights,
-    )
-    g_in, g_w_out, g_small = finish_weights(width, inner, streams)
-    taps = sums[:, :inner]
-    lanes = sums[:, inner:]
-    taps_bc = (lanes[:, :half] + lanes[:, half:]).reshape(8, 2, state_part)
+        output_weight,
+    )
+    (
+        g_in,
+        g_w_out,
+        g_coef,
+        g_step,
+        taps,
+        taps_bc,
+        bias,
+        bias_bc,
+        g_dt,
+        g_log,
+        g_skip,
+        g_gain,
+        g_norm,
+        block_out,
+        grad_input,
+    ) = finish(
+        width, inner, heads, state_part, streams, sums, gather, block_out, grad_input
+    )
     return (
         block_out.reshape(seqs, block, col_count),
         grad_input.reshape(seqs, block, col_count),
-        taps[KER + 3, :col_count],
+        g_norm[0],
         g_in,
-        g_small[half:].reshape(2, state_part, width).transpose(2, 0, 1),
-        g_small[:heads].T,
-        taps[:KER],
-        taps_bc[:KER],
-        taps[KER],
-        taps_bc[KER],
-        lanes[KER + 1, :heads],
-        lanes[KER + 2, :heads],
-        taps[KER + 2].reshape(heads, inner // heads).sum(1),
-        taps[KER + 1],
+        g_coef.transpose(2, 0, 1),
+        g_step.T,
+        taps,
+        taps_bc,
+        bias[0],
+        bias_bc,
+        g_dt[0],
+        g_log[0],
+        g_skip[0],
+        g_gain[0],
         g_w_out,
     )
 

time: 328 us -> 305 us (0.930); the launches traced: 322 us -> 304 us
  between operations: 14.5 us -> 0.69 us
  local copies, waits for them, and re-layouts: 20.1 us -> 13.8 us
  Pallas kernels: 278 us -> 283 us
  matrix products: 4.8 us -> 0 us
    unnamed x31 -> x2, local copies, waits for them, and re-layouts: 11 us -> 6.17 us
    dot_general x1 -> x0, matrix products: 4.8 us -> none  [mul(): lax.dot_general(left, right, (how, ((), ())), precision=precision, prefer...]
    slice x7 -> x0, local copies, waits for them, and re-layouts: 4.41 us -> none  [the longest x1 1.89 us: body(): g_small[half:].reshape(2, state_part, width).transpose(2, 0, 1)]
    pallas_call x0 -> x3, other arithmetic: none -> 3.85 us  [finish(): pl.pallas_call(finish_kernel, grid=(steps,), in_specs=[block(gate, tall),...]
  transfers between devices with their start and end apart: 1 -> 0, of which waited for: 0 -> 0; matrix products, arithmetic and copies ran while one was open for 2% -> 0% of each run, Pallas kernels for 61% -> 0%
where the time goes in v5:
time: 305 us; the launch traced here: 304 us
  Pallas kernels  283 us (93%)
  local copies, waits for them, and re-layouts  13.8 us (5%)
  other arithmetic  6.9 us (2%)
    pallas_call x1, Pallas kernels, backward(): pl.pallas_call(functools.partial(backward_kernel, dims), out_shape=[jax.S...  191 us
    pallas_call x1, Pallas kernels, forward(): pl.pallas_call(functools.partial(forward_kernel, dims), out_shape=[jax.Sh...  69.5 us
    pallas_call x1, Pallas kernels, finish(): pl.pallas_call(finish_kernel, grid=(steps,), in_specs=[block(gate, tall),...  10.9 us
    pallas_call x1, Pallas kernels, project(): pl.pallas_call(project_kernel, grid=(rows // tall,), in_specs=[by_rows(wi...  10.7 us
    unnamed x2, local copies, waits for them, and re-layouts  6.17 us

profile of v5, /device:TPU:0, one launch (start us, length us, event | category | flops | bytes accessed | tf_op | source)
XLA Modules:
  0.0 304.0 jit_solution(4783237095785933965)
XLA Ops:
  0.6 0.8 reshape.54
  1.4 0.7 negate_bitcast_fusion
  2.1 0.1 pad.14.clone
  2.1 0.1 pad.12.clone
  2.2 0.7 maximum_maximum_fusion
  3.0 0.8 reshape.53
  3.7 0.7 select_maximum_fusion.vec_ref
  4.4 0.7 broadcast_in_dim.21
  5.1 0.7 broadcast_in_dim.22
  5.8 1.3 broadcast_in_dim.19.gain_ref
  7.1 0.7 broadcast_in_dim.23
  7.8 0.1 broadcast_in_dim_reshape.3
  7.9 1.3 concatenate.16.chan_ref
  9.2 1.1 copy.39
  10.4 1.1 copy.38
  11.4 1.0 pad_maximum_fusion.small_weight_ref.small_weight_far
  12.4 5.1 %copy.41 = bf16[1536,2,768]{2,0,1:T(8,128)(2,1)} copy(bf16[1536,2,768]{2,1,0:T(2,128)(2,1)} %param.21) | data formatting | bytes 9437184 | tf_op args[2]
  17.5 10.7 %project.1 = (f32[1024,768]{1,0:T(8,128)}, f32[1024,768]{1,0:T(8,128)}, f32[1024,128]{1,0:T(8,128)}, bf16[1536,1024]{1,0:T(8,128)(2,1)}, f32[1024,1]{1,0:T(8,128)}) custom-call(bf16[1024,1536]{1,0:T(8,128)(2,1)} %bitcast.19, f32[1,1536]{1,0:T(1,128)} %broadcast_in_dim.19.gain_ref, bf16[2,1536,768]{2,1,0:T(8,128)(2,1)} %bitcast.17, ...), custom_call_target="tpu_custom_call" | custom-call | tf_op jit(solution)/shard_map/project/pallas_call | solution.py:647
  28.3 69.5 %mixer_forward.1 = (bf16[1024,768]{1,0:T(8,128)(2,1)}, bf16[1024,256]{1,0:T(8,128)(2,1)}, f32[1024,768]{1,0:T(8,128)}, f32[512,128]{1,0:T(8,128)}, f32[1024,128]...) custom-call(f32[1024,768]{1,0:T(8,128)} %get-tuple-element.55.x_ref., ...), custom_call_target="tpu_custom_call" | custom-call | tf_op jit(solution)/shard_map/mixer_forward/pallas_call | solution.py:577
  97.8 191.5 %mixer_backward.1 = (bf16[768,1536]{1,0:T(8,128)(2,1)}, bf16[1536,768]{1,0:T(8,128)(2,1)}, bf16[1536,384]{1,0:T(8,128)(2,1)}, bf16[1536,512]{1,0:T(8,128)(2,1)},...) custom-call(bf16[1024,768]{1,0:T(8,128)(2,1)} %get-tuple-element.58.dy_ref, ...), custom_call_target="tpu_custom_call" | custom-call | tf_op jit(solution)/shard_map/mixer_backward/pallas_call | solution.py:1552
  289.3 10.9 %finish.1 = (f32[1536,2,768]{2,1,0:T(2,128)}, f32[768,1536]{1,0:T(8,128)}, f32[2,32,1536]{2,1,0:T(8,128)}, f32[12,1536]{1,0:T(8,128)}, f32[4,768]{1,0:T(4,128)},...) custom-call(bf16[1536,768]{1,0:T(8,128)(2,1)} %get-tuple-element.73., ...), custom_call_target="tpu_custom_call" | custom-call | tf_op jit(solution)/shard_map/finish/pallas_call | solution.py:901
  300.2 1.3 reduce
  301.4 1.3 reduce.1
  302.7 1.3 reduce.2
  (2 shorter events, 0.0 us)

commit v6 on v5

--- a/solution.py
+++ b/solution.py
@@ -130,77 +130,86 @@
     return copy
 
 
-def cut_of(count, seqs, state, inner):
-    rows = max(16, seqs * state // count)
-    lane_cuts = count * rows // (seqs * state)
-    return rows, lane_cuts, inner // lane_cuts
-
-
-def piece_of(k, count, seqs, state, inner):
-    rows, lane_cuts, lanes = cut_of(count, seqs, state, inner)
-    each = count // seqs
-    seq, rest = k // each, lax.rem(k, each)
-    row = pl.multiple_of(rest // lane_cuts * rows, rows)
-    if lane_cuts == 1:
-        return seq, pl.ds(row, rows), slice(None)
-    lane = pl.multiple_of(lax.rem(rest, lane_cuts) * lanes, lanes)
-    return seq, pl.ds(row, rows), pl.ds(lane, lanes)
-
-
-def carry_exchange(dims, local, arrived, passed, incoming, decay_ref, sems, reverse):
+def cut_of(count, seqs, state):
+    group = count // 2
+    return group, seqs * state // group
+
+
+def carry_exchange(dims, local, arrived, passed, total, incoming, decay_ref, sems, reverse):
     count, _, seqs, _, inner, _, state = dims
     place, head = lax.axis_index("seq"), lax.axis_index("head")
-    send, recv, back_send, back_recv = sems
-    piece = functools.partial(piece_of, count=count, seqs=seqs, state=state, inner=inner)
-    rows, _, lanes = cut_of(count, seqs, state, inner)
+    send, recv, back_send, back_recv, over_send, over_recv = sems
+    group, rows = cut_of(count, seqs, state)
+    base, me = place // group * group, lax.rem(place, group)
+    leads = place >= group if reverse else place < group
+    each = group // seqs
 
     def at(ref, k):
-        seq, row, lane = piece(k)
-        return ref.at[seq, row, lane]
-
-    out = line_copy(count, lambda other: at(local, other), lambda k: arrived.at[k], send, recv)
+        return ref.at[k // each, ds(lax.rem(k, each) * rows, rows)]
+
+    def out(i):
+        other = lax.rem(me + i, group)
+        return remote(at(local, other), arrived.at[me], send.at[i], recv.at[i], base + other, head)
 
     def back(j):
-        i = lax.rem(j - place + count, count)
+        i = lax.rem(j - me + group, group)
         return remote(
-            passed.at[j], at(incoming, place), back_send.at[i], back_recv.at[i], j, head
+            passed.at[j], at(incoming, me), back_send.at[i], back_recv.at[i], base + j, head
         )
 
+    def over():
+        other = lax.rem(place + group, count)
+        return remote(total.at[0], total.at[1], over_send, over_recv, other, head)
+
     def start():
-        loop(1, count, lambda i: out(i).start())
-        seq, row, lane = piece(place)
-        arrived[place] = local[seq, row, lane]
+        loop(1, group, lambda i: out(i).start())
+        arrived[me] = local[me // each, ds(lax.rem(me, each) * rows, rows)]
 
     def carry():
-        seq, row, lane = piece(place)
-        held = jnp.zeros((rows, lanes), F32)
-        for step in range(count):
-            j = count - 1 - step if reverse else step
-            i = lax.rem(place - j + count, count)
-
-            @pl.when(j != place)
+        @pl.when(leads)
+        def _():
+            total[1] = jnp.zeros((rows, inner), total.dtype)
+
+        @pl.when(~leads)
+        def _():
+            over().wait_recv()
+
+        held = total[1].astype(F32)
+        seq = me // each
+        for step in range(group):
+            j = group - 1 - step if reverse else step
+
+            @pl.when(j != me)
             def _():
-                out(i).wait_recv()
+                out(lax.rem(me - j + group, group)).wait_recv()
 
             passed[j] = held.astype(passed.dtype)
 
-            @pl.when(j != place)
+            @pl.when(j != me)
             def _():
                 back(j).start()
 
-            @pl.when(j == place)
+            @pl.when(j == me)
             def _():
-                incoming[seq, row, lane] = passed[j]
-
-            decay = decay_ref[seq, pl.ds(j, 1), lane]
-            held = decay * held + arrived[j].astype(F32)
+                incoming[seq, ds(lax.rem(me, each) * rows, rows)] = passed[j]
+
+            held = decay_ref[seq, pl.ds(base + j, 1), :] * held + arrived[j].astype(F32)
+
+        @pl.when(leads)
+        def _():
+            total[0] = held.astype(total.dtype)
+            over().start()
 
     def finish():
         def one(i):
             out(i).wait_send()
-            back(lax.rem(place + i, count)).wait()
-
-        loop(1, count, one)
+            back(lax.rem(me + i, group)).wait()
+
+        loop(1, group, one)
+
+        @pl.when(leads)
+        def _():
+            over().wait_send()
 
     return start, carry, finish
 
@@ -258,6 +267,7 @@
     local,
     arrived,
     passed,
+    handed,
     incoming,
     rowsum,
     edge_send,
@@ -270,6 +280,8 @@
     st_recv,
     back_send,
     back_recv,
+    over_send,
+    over_recv,
     row_send,
     row_recv,
 ):
@@ -416,9 +428,10 @@
         local,
         arrived,
         passed,
+        handed,
         incoming,
         decay_ref,
-        (st_send, st_recv, back_send, back_recv),
+        (st_send, st_recv, back_send, back_recv, over_send, over_recv),
         False,
     )
     start()
@@ -554,7 +567,7 @@
     count, parts, seqs, block, inner, heads, state = dims
     rows = seqs * block
     chunks = rows // CHUNK
-    cut_rows, _, cut_lanes = cut_of(count, seqs, state, inner)
+    group, cut_rows = cut_of(count, seqs, state)
     spec, far = pl.BlockSpec(memory_space=pltpu.VMEM), pl.BlockSpec(memory_space=pl.ANY)
     fetched, kept = (1, 8, 9), (0, 1, 2, 4, 5, 6, 7, 8, 9, 10)
     line, ring = pltpu.SemaphoreType.DMA((count,)), pltpu.SemaphoreType.DMA((parts,))
@@ -595,8 +608,9 @@
             vmem((rows, inner), F32),
             vmem((count, 8, LANES), F32),
             vmem((seqs, state, inner), F32),
-            vmem((count, cut_rows, cut_lanes), F32),
-            vmem((count, cut_rows, cut_lanes), F32),
+            vmem((group, cut_rows, inner), F32),
+            vmem((group, cut_rows, inner), F32),
+            vmem((2, cut_rows, inner), F32),
             vmem((seqs, state, inner), F32),
             vmem((parts, chunks, 8, LANES), F32),
             edge,
@@ -609,6 +623,8 @@
             line,
             line,
             line,
+            pltpu.SemaphoreType.DMA,
+            pltpu.SemaphoreType.DMA,
             ring,
             ring,
         ],
@@ -620,20 +636,66 @@
 
 
 def project_kernel(
-    tokens_ref, gain_ref, weight_ref, small_weight_ref, gate_ref, x_ref, small_ref, turned_ref, scale_ref
+    tokens_ref,
+    gain_ref,
+    weight_ref,
+    step_ref,
+    coef_ref,
+    taps_ref,
+    taps_bc_ref,
+    bias_ref,
+    bias_bc_ref,
+    dt_bias_ref,
+    a_log_ref,
+    skip_ref,
+    gate_gain_ref,
+    gate_ref,
+    x_ref,
+    small_ref,
+    turned_ref,
+    scale_ref,
+    small_weight_ref,
+    chan_ref,
+    vec_ref,
+    gain_row,
 ):
+    heads, state_part = step_ref.shape[0], coef_ref.shape[1]
+
+    def flat(ref):
+        return jnp.concatenate([ref[k : k + 1, :] for k in range(ref.shape[0])], axis=1)
+
+    @pl.when(pl.program_id(0) == 0)
+    def _():
+        small_weight_ref[...] = jnp.zeros_like(small_weight_ref)
+        small_weight_ref[0:heads, :] = step_ref[...]
+        for k in range(2):
+            low = LANES // 2 + k * state_part
+            small_weight_ref[low : low + state_part, :] = coef_ref[k]
+        gain_row[...] = flat(gain_ref)
+        chan_ref[...] = jnp.zeros_like(chan_ref)
+        chan_ref[0:KER, :] = taps_ref[...]
+        chan_ref[4:5, :] = flat(bias_ref)
+        chan_ref[5:6, :] = flat(gate_gain_ref)
+        chan_ref[6:7, :] = spread(skip_ref[...], heads // 2)
+        vec_ref[...] = jnp.zeros_like(vec_ref)
+        for k in range(4):
+            at = slice(k * state_part, (k + 1) * state_part)
+            vec_ref[0:KER, at] = taps_bc_ref[:, k % 2, :]
+            vec_ref[4:5, at] = bias_bc_ref[k % 2 : k % 2 + 1, :]
+        vec_ref[5:6, 0:heads] = dt_bias_ref[...]
+        vec_ref[6:7, 0:heads] = -jnp.exp(a_log_ref[...])
+
     tokens = tokens_ref[...].astype(F32)
     scale = lax.rsqrt(jnp.mean(tokens * tokens, axis=1, keepdims=True) + EPSILON)
     scale_ref[...] = scale
-    normed = tokens * scale * gain_ref[...]
-    low = normed.astype(BF16)
+    low = (tokens * scale * gain_row[...]).astype(BF16)
     turned_ref[...] = low.T
     x_ref[...] = mul(low, weight_ref[1], NN)
-    small_ref[...] = mul(low, small_weight_ref[...], NN)
+    small_ref[...] = mul(low, small_weight_ref[...], NT)
     gate_ref[...] = mul(low, weight_ref[0], NN)
 
 
-def project(tokens, gain, weights, small_weight):
+def project(tokens, gain, weights, *params):
     rows, width = tokens.shape
     inner = weights.shape[2]
     tall = 2 * CHUNK
@@ -641,19 +703,22 @@
     def by_rows(cols):
         return pl.BlockSpec((tall, cols), lambda i: (i, 0))
 
-    def whole(array_in):
-        return pl.BlockSpec(array_in.shape, lambda i: (0,) * array_in.ndim)
+    def whole(shape):
+        return pl.BlockSpec(shape, lambda i: (0,) * len(shape))
 
     return pl.pallas_call(
         project_kernel,
         grid=(rows // tall,),
-        in_specs=[by_rows(width), whole(gain), whole(weights), whole(small_weight)],
+        in_specs=[by_rows(width)] + [whole(a.shape) for a in (gain, weights) + params],
         out_specs=[
             by_rows(inner),
             by_rows(inner),
             by_rows(LANES),
             pl.BlockSpec((width, tall), lambda i: (0, i)),
             by_rows(1),
+            whole((LANES, width)),
+            whole((8, inner)),
+            whole((8, LANES)),
         ],
         out_shape=[
             jax.ShapeDtypeStruct((rows, inner), F32),
@@ -661,10 +726,14 @@
             jax.ShapeDtypeStruct((rows, LANES), F32),
             jax.ShapeDtypeStruct((width, rows), BF16),
             jax.ShapeDtypeStruct((rows, 1), F32),
+            jax.ShapeDtypeStruct((LANES, width), BF16),
+            jax.ShapeDtypeStruct((8, inner), F32),
+            jax.ShapeDtypeStruct((8, LANES), F32),
         ],
+        scratch_shapes=[pltpu.VMEM((1, width), F32)],
         compiler_params=pltpu.CompilerParams(vmem_limit_bytes=VMEM_LIMIT),
         name="project",
-    )(tokens, gain, weights, small_weight)
+    )(tokens, gain, weights, *params)
 
 
 def ring_place(count):
@@ -852,9 +921,9 @@
         lanes = sums_ref[:, inner:]
         both = lanes + pltpu.roll(lanes, LANES // 2, 1)
         taps_ref[...] = sums_ref[0:KER, 0:inner]
-        bias_ref[...] = sums_ref[KER : KER + 1, 0:inner]
-        gain_ref[...] = sums_ref[KER + 1 : KER + 2, 0:inner]
-        norm_ref[...] = sums_ref[KER + 3 : KER + 4, 0 : norm_ref.shape[1]]
+        for ref, row in ((bias_ref, KER), (gain_ref, KER + 1), (norm_ref, KER + 3)):
+            for k in range(ref.shape[0]):
+                ref[k : k + 1, :] = sums_ref[row : row + 1, k * LANES : (k + 1) * LANES]
         for k in range(2):
             at = slice(k * state_part, (k + 1) * state_part)
             taps_bc_ref[:, k, :] = both[0:KER, at]
@@ -890,13 +959,13 @@
     little = [
         (KER, inner),
         (KER, 2, state_part),
-        (1, inner),
+        (inner // LANES, LANES),
         (2, state_part),
         (1, heads),
         (1, heads),
         (1, heads),
-        (1, inner),
-        (1, cols),
+        (inner // LANES, LANES),
+        (cols // LANES, LANES),
     ]
     return pl.pallas_call(
         finish_kernel,
@@ -1013,6 +1082,7 @@
         local,
         arrived,
         passed,
+        handed,
         incoming,
         bc_out,
         bc_in,
@@ -1024,6 +1094,8 @@
         st_recv,
         back_send,
         back_recv,
+        over_send,
+        over_recv,
     ) = rest
     sources = (
         ng_t_far,
@@ -1160,9 +1232,10 @@
         local,
         arrived,
         passed,
+        handed,
         incoming,
         decay_ref,
-        (st_send, st_recv, back_send, back_recv),
+        (st_send, st_recv, back_send, back_recv, over_send, over_recv),
         True,
     )
     start()
@@ -1431,13 +1504,13 @@
             weight_copy(i + 1).start()
 
         weight_copy(i).wait()
-        mine = small_weight_ref[pl.ds(pl.multiple_of(other * cols, cols), cols), :]
+        mine = small_weight_ref[:, pl.ds(pl.multiple_of(other * cols, cols), cols)]
 
         def some(r):
             rows = ds(r * tall, tall)
             part = mul(dgate_ref[rows, :], weights[slot, 0], NT)
             part = part + mul(dx_ref[rows, 0:inner], weights[slot, 1], NT)
-            part = part + mul(dx_ref[rows, inner:], mine, NT)
+            part = part + mul(dx_ref[rows, inner:], mine, NN)
             dn_out[other, rows, :] = part.astype(BF16)
 
         loop(0, rows_all // tall, some)
@@ -1531,7 +1604,7 @@
     count, parts, seqs, block, inner, heads, state = dims
     rows = seqs * block
     chunks = rows // CHUNK
-    cut_rows, _, cut_lanes = cut_of(count, seqs, state, inner)
+    group, cut_rows = cut_of(count, seqs, state)
     normed_rows, ng_rows, width = (operands[k].shape[d] for k, d in ((16, 0), (17, 0), (18, 1)))
     cols = width // parts
     distant = (1, 3, 7, 10, 14, 16, 17, 18, 19, 20, 24, 25, 26)
@@ -1598,8 +1671,9 @@
             vmem((rows, 2 * state), BF16),
             vmem((rows, LANES), F32),
             vmem((seqs, state, inner), BF16),
-            vmem((count, cut_rows, cut_lanes), BF16),
-            vmem((count, cut_rows, cut_lanes), BF16),
+            vmem((group, cut_rows, inner), BF16),
+            vmem((group, cut_rows, inner), BF16),
+            vmem((2, cut_rows, inner), BF16),
             vmem((seqs, state, inner), BF16),
             vmem((parts, block, LANES), BF16),
             vmem((parts, block, LANES), BF16),
@@ -1611,6 +1685,8 @@
             line,
             line,
             line,
+            pltpu.SemaphoreType.DMA,
+            pltpu.SemaphoreType.DMA,
         ],
         compiler_params=pltpu.CompilerParams(
             collective_id=3, has_side_effects=True, vmem_limit_bytes=VMEM_LIMIT
@@ -1648,37 +1724,21 @@
     dims = (count, parts, seqs, block, inner, heads, state)
 
     flat_tokens = tokens.reshape(rows, width)
-    small_weight = jnp.concatenate(
-        [
-            step_weight,
-            jnp.zeros((width, half - heads), BF16),
-            coefficient_weight.reshape(width, 2 * state_part),
-        ],
-        axis=1,
-    )
     both_weights = gate_input_weight.transpose(1, 0, 2)
-    gate_pre, x_pre, small, normed_t, row_scale = project(
-        flat_tokens, norm_gain[None], both_weights, small_weight
-    )
-
-    chan = jnp.concatenate(
-        [
-            conv_x,
-            conv_bias_x[None],
-            gate_gain[None],
-            jnp.repeat(d_skip, inner // heads)[None],
-            jnp.zeros((1, inner), F32),
-        ]
-    )
-    twice = jnp.concatenate(
-        [conv_bc.reshape(KER, 2 * state_part), conv_bias_bc.reshape(1, 2 * state_part)]
-    )
-    per_head = jnp.stack([dt_bias, -jnp.exp(a_log), jnp.zeros_like(a_log)])
-    vec = jnp.concatenate(
-        [
-            jnp.concatenate([twice, twice], axis=1),
-            jnp.pad(per_head, ((0, 0), (0, LANES - heads))),
-        ]
+    gate_pre, x_pre, small, normed_t, row_scale, small_weight, chan, vec = project(
+        flat_tokens,
+        norm_gain.reshape(-1, LANES),
+        both_weights,
+        step_weight.T,
+        coefficient_weight.transpose(1, 2, 0),
+        conv_x,
+        conv_bc,
+        conv_bias_x.reshape(-1, LANES),
+        conv_bias_bc,
+        dt_bias.reshape(1, heads),
+        a_log.reshape(1, heads),
+        d_skip.reshape(1, heads),
+        gate_gain.reshape(-1, LANES),
     )
     device, lane, channel = np.meshgrid(
         np.arange(parts), np.arange(LANES), np.arange(2 * state), indexing="ij"
@@ -1766,18 +1826,18 @@
     return (
         block_out.reshape(seqs, block, col_count),
         grad_input.reshape(seqs, block, col_count),
-        g_norm[0],
+        g_norm.reshape(-1),
         g_in,
         g_coef.transpose(2, 0, 1),
         g_step.T,
         taps,
         taps_bc,
-        bias[0],
+        bias.reshape(-1),
         bias_bc,
-        g_dt[0],
-        g_log[0],
-        g_skip[0],
-        g_gain[0],
+        g_dt.reshape(-1),
+        g_log.reshape(-1),
+        g_skip.reshape(-1),
+        g_gain.reshape(-1),
         g_w_out,
     )
 

time: 305 us -> 286 us (0.938)
  local copies, waits for them, and re-layouts: 13.8 us -> 6.42 us
  other arithmetic: 6.9 us -> 0 us
  Pallas kernels: 283 us -> 278 us
    pallas_call x1, Pallas kernels: 69.5 us -> 63.5 us  [forward(): pl.pallas_call(functools.partial(forward_kernel, dims), out_shape=[jax.Sh...]
    pallas_call x3 -> x0, other arithmetic: 3.85 us -> none  [finish(): pl.pallas_call(finish_kernel, grid=(steps,), in_specs=[block(gate, tall),...]
    unnamed x2 -> x1, local copies, waits for them, and re-layouts: 6.17 us -> 5.12 us
where the time goes in v6:
time: 286 us; the launch traced here: 285 us
  Pallas kernels  278 us (97%)
  local copies, waits for them, and re-layouts  6.42 us (2%)
    pallas_call x1, Pallas kernels, backward(): pl.pallas_call(functools.partial(backward_kernel, dims), out_shape=[jax.S...  192 us
    pallas_call x1, Pallas kernels, forward(): pl.pallas_call(functools.partial(forward_kernel, dims), out_shape=[jax.Sh...  63.5 us
    pallas_call x1, Pallas kernels, project(): pl.pallas_call(project_kernel, grid=(rows // tall,), in_specs=[by_rows(wi...  11.1 us
    pallas_call x1, Pallas kernels, finish(): pl.pallas_call(finish_kernel, grid=(steps,), in_specs=[block(gate, tall),...  10.9 us

profile of v6, /device:TPU:0, one launch (start us, length us, event | category | flops | bytes accessed | tf_op | source)
XLA Modules:
  0.0 285.3 jit_solution(17939672444166833286)
XLA Ops:
  0.6 1.3 broadcast_in_dim.3.gain_ref
  1.9 5.1 %copy.36 = bf16[1536,2,768]{2,0,1:T(8,128)(2,1)} copy(bf16[1536,2,768]{2,1,0:T(2,128)(2,1)} %param.21) | data formatting | bytes 9437184 | tf_op args[2]
  7.1 11.1 %project.1 = (f32[1024,768]{1,0:T(8,128)}, f32[1024,768]{1,0:T(8,128)}, f32[1024,128]{1,0:T(8,128)}, bf16[1536,1024]{1,0:T(8,128)(2,1)}, f32[1024,1]{1,0:T(8,128...) custom-call(bf16[1024,1536]{1,0:T(8,128)(2,1)} %bitcast.25, f32[12,128]{1,0:T(8,128)} %bitcast.31, ...), custom_call_target="tpu_custom_call" | custom-call | tf_op jit(solution)/shard_map/project/pallas_call | solution.py:709
  18.2 63.5 %mixer_forward.1 = (bf16[1024,768]{1,0:T(8,128)(2,1)}, bf16[1024,256]{1,0:T(8,128)(2,1)}, f32[1024,768]{1,0:T(8,128)}, f32[512,128]{1,0:T(8,128)}, f32[1024,128]...) custom-call(f32[1024,768]{1,0:T(8,128)} %get-tuple-element.58.x_ref., ...), custom_call_target="tpu_custom_call" | custom-call | tf_op jit(solution)/shard_map/mixer_forward/pallas_call | solution.py:590
  81.7 192.5 %mixer_backward.1 = (bf16[768,1536]{1,0:T(8,128)(2,1)}, bf16[1536,768]{1,0:T(8,128)(2,1)}, bf16[1536,384]{1,0:T(8,128)(2,1)}, bf16[1536,512]{1,0:T(8,128)(2,1)},...) custom-call(bf16[1024,768]{1,0:T(8,128)(2,1)} %get-tuple-element.63.dy_ref, ...), custom_call_target="tpu_custom_call" | custom-call | tf_op jit(solution)/shard_map/mixer_backward/pallas_call | solution.py:1625
  274.2 10.9 %finish.1 = (f32[1536,2,768]{2,1,0:T(2,128)}, f32[768,1536]{1,0:T(8,128)}, f32[2,32,1536]{2,1,0:T(8,128)}, f32[12,1536]{1,0:T(8,128)}, f32[4,768]{1,0:T(4,128)},...) custom-call(bf16[1536,768]{1,0:T(8,128)(2,1)} %get-tuple-element.79., ...), custom_call_target="tpu_custom_call" | custom-call | tf_op jit(solution)/shard_map/finish/pallas_call | solution.py:970
